TPU v7x, 32 devices: a whole 2x2x4 slice. The times are simulated.
32 devices in a mesh: gx: 8 (over z, x), gy: 4 (over y, core).
Axes of the slice: x: 2, y: 2, z: 4, core: 2. Of those that a mesh axis runs over, the one named last changes fastest.
Arguments:
- features: bfloat16 [96, 4096], P(None, ('gx', 'gy')), may hold values from -6 to 6
- kernel_map: int32 [27, 4096], P(None, ('gx', 'gy')), may hold values from 0 to 256
- send_rows: int32 [8, 512], P(None, ('gx', 'gy')), may hold values from 0 to 127
- counts: int32 [32], P(('gx', 'gy')), may hold values from 32 to 128, as said below
- weight_one: bfloat16 [27, 96, 96], replicated, may hold values from -0.15625 to 0.15625
- weight_two: bfloat16 [27, 96, 96], replicated, may hold values from -0.15625 to 0.15625
- first_norm_scale: float32 [96], replicated, may hold values from 0.5 to 1.5
- first_norm_bias: float32 [96], replicated, may hold values from -3 to 3
- second_norm_scale: float32 [96], replicated, may hold values from 0.5 to 1.5
- second_norm_bias: float32 [96], replicated, may hold values from -3 to 3
- cotangent: bfloat16 [96, 4096], P(None, ('gx', 'gy')), may hold values from -6 to 6
Outputs:
- output: bfloat16 [96, 4096], P(None, ('gx', 'gy'))
- grad_features: bfloat16 [96, 4096], P(None, ('gx', 'gy'))
- grad_weight_one: float32 [27, 96, 96], replicated
- grad_weight_two: float32 [27, 96, 96], replicated
- grad_norms: float32 [4, 96], replicated
Inputs may be any that keep to these rules, and one draw needn't show every extreme that they name: `counts`: counts rise along the device order; the first device uses 128 // 4 rows and the last device of the grid uses all 128 rows.
All inputs are finite; a program needn't handle non-finite values.
Results may differ from a plain program's by a relative error of at most 0.0075.
Values may be sent and summed in bfloat16 or wider, within the bound.
No kernel may reach another device: no remote copies, remote signals or barrier semaphores. Data moves between devices by JAX's collectives and lax.ppermute only.
A program may use at most 64 MiB of HBM per device.

v0:
```python
import jax
import jax.numpy as jnp
from jax import lax
from jax.sharding import PartitionSpec as P

EPS = 1e-05
STEP_LIST = ((1, 0), (-1, 0), (0, 1), (0, -1), (1, 1), (1, -1), (-1, 1), (-1, -1))


def from_behind(x, axis, by):
    size = lax.axis_size(axis)
    pairs = [(i, i + by) for i in range(size) if 0 <= i + by < size]
    return lax.ppermute(x, axis, pairs)


def silu_value(values):
    return values * jax.nn.sigmoid(values)


def silu_slope(values):
    sigma = jax.nn.sigmoid(values)
    return sigma * (1.0 + values * (1.0 - sigma))


def move_blocks(blocks, step_pairs):
    result = []
    for slot_id in range(8):
        piece = blocks[slot_id]
        if step_pairs[slot_id][0] != 0:
            piece = from_behind(piece, "gx", step_pairs[slot_id][0])
        if step_pairs[slot_id][1] != 0:
            piece = from_behind(piece, "gy", step_pairs[slot_id][1])
        result.append(piece)
    return result


def extend(values, send_rows):
    channels = values.shape[0]
    outgoing = [jnp.take(values, send_rows[slot_id], axis=1) for slot_id in range(8)]
    arrived = move_blocks(outgoing, STEP_LIST)
    zero_col = jnp.zeros((channels, 1), values.dtype)
    return jnp.concatenate([values] + arrived + [zero_col], axis=1)


def convolve(extended, weights, kernel_map):
    channels = extended.shape[0]
    gathered = jnp.take(extended, kernel_map.reshape(-1), axis=1).reshape(
        channels, kernel_map.shape[0], kernel_map.shape[1]
    )
    return (
        jnp.einsum("kio,ikr->or", weights, gathered, preferred_element_type=jnp.float32),
        gathered,
    )


def spread_back(grad_rows, weights, kernel_map, send_rows, table_len):
    channels, rows_here = grad_rows.shape
    width = send_rows.shape[1]
    terms = jnp.einsum("kio,or->ikr", weights, grad_rows, preferred_element_type=jnp.float32)
    table = (
        jnp.zeros((channels, table_len), jnp.float32)
        .at[:, kernel_map.reshape(-1)]
        .add(terms.reshape(channels, -1))
    )
    returned = [
        table[:, rows_here + slot_id * width : rows_here + (slot_id + 1) * width].astype(
            jnp.bfloat16
        )
        for slot_id in range(8)
    ]
    back_steps = tuple(((-pair[0], -pair[1]) for pair in STEP_LIST))
    arrived = move_blocks(returned, back_steps)
    joined = jnp.concatenate(arrived, axis=1).astype(jnp.float32)
    return table[:, :rows_here].at[:, send_rows.reshape(-1)].add(joined)


def apply_batch_norm(pre_norm, active_mask):
    masked = pre_norm * active_mask
    sums, squares, row_total = lax.psum(
        (jnp.sum(masked, axis=1), jnp.sum(masked * pre_norm, axis=1), jnp.sum(active_mask)),
        ("gx", "gy"),
    )
    mean = sums / row_total
    var = squares / row_total - mean * mean
    inverse_deviation = lax.rsqrt(var + EPS)
    return ((pre_norm - mean[:, None]) * inverse_deviation[:, None], inverse_deviation, row_total)


def norm_backward_step(
    linear_gradient, normalized_input, inverse_deviation, norm_scale, active_mask, row_total
):
    scale_gradient, bias_gradient = lax.psum(
        (
            jnp.sum(linear_gradient * normalized_input * active_mask, axis=1),
            jnp.sum(linear_gradient, axis=1),
        ),
        ("gx", "gy"),
    )
    prenorm_gradient = (
        (norm_scale * inverse_deviation)[:, None]
        * (
            linear_gradient
            - (bias_gradient[:, None] + normalized_input * scale_gradient[:, None]) / row_total
        )
        * active_mask
    )
    return (prenorm_gradient.astype(jnp.bfloat16), scale_gradient, bias_gradient)


def on_device(
    features,
    kernel_map,
    send_rows,
    counts,
    weight_one,
    weight_two,
    first_norm_scale,
    first_norm_bias,
    second_norm_scale,
    second_norm_bias,
    cotangent,
):
    rows_here = features.shape[1]
    active_mask = (jnp.arange(rows_here, dtype=jnp.int32) < counts[0]).astype(jnp.float32)
    begin_offset = (features.astype(jnp.float32) * active_mask).astype(jnp.bfloat16)
    ext_zero = extend(begin_offset, send_rows)
    table_len = ext_zero.shape[1]
    first_hidden, taken_zero = convolve(ext_zero, weight_one, kernel_map)
    first_normalized, first_inverse_deviation, row_total = apply_batch_norm(
        first_hidden, active_mask
    )
    first_linear = first_norm_scale[:, None] * first_normalized + first_norm_bias[:, None]
    act_one = (silu_value(first_linear) * active_mask).astype(jnp.bfloat16)
    ext_one = extend(act_one, send_rows)
    second_hidden, taken_one = convolve(ext_one, weight_two, kernel_map)
    second_normalized, second_inverse_deviation, recount_total = apply_batch_norm(
        second_hidden, active_mask
    )
    accumulated_sum = (
        second_norm_scale[:, None] * second_normalized
        + second_norm_bias[:, None]
        + begin_offset.astype(jnp.float32)
    )
    output = (silu_value(accumulated_sum) * active_mask).astype(jnp.bfloat16)
    gradient_total = cotangent.astype(jnp.float32) * active_mask * silu_slope(accumulated_sum)
    second_gradient, second_scale_gradient, second_bias_gradient = norm_backward_step(
        gradient_total,
        second_normalized,
        second_inverse_deviation,
        second_norm_scale,
        active_mask,
        recount_total,
    )
    grad_weight_two = jnp.einsum(
        "ikr,or->kio", taken_one, second_gradient, preferred_element_type=jnp.float32
    )
    linear_gradient = (
        spread_back(second_gradient, weight_two, kernel_map, send_rows, table_len)
        * active_mask
        * silu_slope(first_linear)
    )
    first_gradient, first_scale_gradient, first_bias_gradient = norm_backward_step(
        linear_gradient,
        first_normalized,
        first_inverse_deviation,
        first_norm_scale,
        active_mask,
        row_total,
    )
    grad_weight_one = jnp.einsum(
        "ikr,or->kio", taken_zero, first_gradient, preferred_element_type=jnp.float32
    )
    grad_weight_one, grad_weight_two = lax.psum((grad_weight_one, grad_weight_two), ("gx", "gy"))
    grad_features = (
        (spread_back(first_gradient, weight_one, kernel_map, send_rows, table_len) + gradient_total)
        * active_mask
    ).astype(jnp.bfloat16)
    grad_norms = jnp.stack(
        [first_scale_gradient, first_bias_gradient, second_scale_gradient, second_bias_gradient]
    )
    return (output, grad_features, grad_weight_one, grad_weight_two, grad_norms)


def solution(mesh):
    return jax.shard_map(
        on_device,
        mesh=mesh,
        in_specs=(
            P(None, ("gx", "gy")),
            P(None, ("gx", "gy")),
            P(None, ("gx", "gy")),
            P(("gx", "gy")),
            P(),
            P(),
            P(),
            P(),
            P(),
            P(),
            P(None, ("gx", "gy")),
        ),
        out_specs=(P(None, ("gx", "gy")), P(None, ("gx", "gy")), P(), P(), P()),
        check_vma=False,
    )
```

profile of v0, /device:TPU:0, one launch (start us, length us, event | category | flops | bytes accessed | tf_op | source)
XLA Modules:
  0.0 527.3 jit_solution(15396579108231757494)
XLA Ops:
  10.5 4.8 collective-permute-start
  20.1 4.4 collective-permute-start.4
  25.1 4.3 collective-permute-start.6
  41.7 4.3 collective-permute-start.9
  50.6 7.1 %gather_fusion.8 = bf16[3456,96]{1,0:T(8,128)(2,1)S(1)} fusion(bf16[96,257]{0,1:T(8,128)(2,1)S(1)} %copy.192, s32[4096]{0:T(1024)S(1)} %pad_clamp_fusion), kind=kCustom, calls=%fused_computation.1.clone | custom fusion | bytes 1340928 | tf_op jit(solution)/shard_map/jit(_take)/gather | solution.py:47
  60.8 43.4 %all-reduce.3 = (f32[96]{0:T(128)S(1)}, f32[]{:T(128)}, f32[96]{0:T(128)S(1)}) all-reduce(f32[96]{0:T(128)S(1)} %get-tuple-element.25, f32[]{:T(128)} %fusion.18, f32[96]{0:T(128)S(1)} %get-tuple-element.24), channel_id=1, replica_groups=mesh['gx'=8,'gy'=4] {'gx','gy'}, use_global_device_ids=true, to_apply=%region_1.4 | all-reduce | flops 193 | bytes 1544 | tf_op jit(solution)/shard_map/psum | solution.py:79
  117.5 4.5 collective-permute-start.16
  130.4 5.2 collective-permute-start.17
  136.8 4.3 collective-permute-start.21
  145.8 7.1 %gather_fusion.17 = bf16[3456,96]{1,0:T(8,128)(2,1)S(1)} fusion(bf16[96,257]{0,1:T(8,128)(2,1)S(1)} %copy.211, s32[4096]{0:T(1024)S(1)} %pad_clamp_fusion), kind=kCustom, calls=%fused_computation.17.clone | custom fusion | bytes 1340928 | tf_op jit(solution)/shard_map/jit(_take)/gather | solution.py:47
  155.3 43.0 %all-reduce.2 = (f32[96]{0:T(128)S(1)}, f32[96]{0:T(128)S(1)}) all-reduce(f32[96]{0:T(128)S(1)} %get-tuple-element.23, f32[96]{0:T(128)S(1)} %get-tuple-element.22), channel_id=1, replica_groups=mesh['gx'=8,'gy'=4] {'gx','gy'}, use_global_device_ids=true, to_apply=%region_7.10 | all-reduce | flops 192 | bytes 1536 | tf_op jit(solution)/shard_map/psum | solution.py:79
  199.8 39.9 %all-reduce.1 = (f32[96]{0:T(128)S(1)}, f32[96]{0:T(128)S(1)}) all-reduce(f32[96]{0:T(128)S(1)} %get-tuple-element.29, f32[96]{0:T(128)S(1)} %get-tuple-element.28), channel_id=1, replica_groups=mesh['gx'=8,'gy'=4] {'gx','gy'}, use_global_device_ids=true, to_apply=%region_13.16 | all-reduce | flops 192 | bytes 1536 | tf_op jit(solution)/shard_map/psum | solution.py:92
  245.1 20.0 %scatter_custom_fusion = f32[96,257]{0,1:T(8,128)S(1)} fusion(s32[3456]{0:T(1024)S(1)} %fusion.16, f32[3456,96]{1,0:T(8,128)} %copy.215, f32[]{:T(128)} %constant.24.clone.1), kind=kCustom, calls=%fused_computation.39 | custom fusion | flops 331776 | bytes 99200 | tf_op jit(solution)/shard_map/scatter-add | solution.py:63
  268.8 4.8 collective-permute-start.25
  277.5 6.1 %collective-permute-start.32 = (bf16[96,16]{0,1:T(8,128)(2,1)S(1)}, bf16[96,16]{0,1:T(8,128)(2,1)S(1)}, u32[]{:S(2)}, u32[]{:S(2)}) collective-permute-start(bf16[96,16]{0,1:T(8,128)(2,1)S(1)} %get-tuple-element.75), channel_id=1, source_target_pairs={{0,4},{4,8},{8,12},{12,16},{16,20},{20,24},{24,28},{1,5},{5,9},{9,... | collective-permute-start | bytes 9224 | tf_op jit(solution)/shard_map/ppermute | solution.py:13
  283.6 4.8 collective-permute-start.34
  297.4 4.3 collective-permute-start.35
  305.7 42.8 %all-reduce = (f32[96]{0:T(128)S(1)}, f32[96]{0:T(128)}) all-reduce(f32[96]{0:T(128)S(1)} %get-tuple-element.27, f32[96]{0:T(128)S(1)} %get-tuple-element.26), channel_id=1, replica_groups=mesh['gx'=8,'gy'=4] {'gx','gy'}, use_global_device_ids=true, to_apply=%region_19.22 | all-reduce | flops 192 | bytes 1536 | tf_op jit(solution)/shard_map/psum | solution.py:92
  356.4 20.1 %scatter_custom_fusion.2 = f32[96,257]{0,1:T(8,128)S(1)} fusion(s32[3456]{0:T(1024)} %copy-done.11, f32[3456,96]{1,0:T(8,128)S(1)} %copy.218, f32[]{:T(128)} %constant.24.clone.1), kind=kCustom, calls=%fused_computation.37 | custom fusion | flops 331776 | bytes 99200 | tf_op jit(solution)/shard_map/scatter-add | solution.py:63
  378.9 4.8 collective-permute-start.37
  387.6 6.1 %collective-permute-start.44 = (bf16[96,16]{0,1:T(8,128)(2,1)S(1)}, bf16[96,16]{0,1:T(8,128)(2,1)S(1)}, u32[]{:S(2)}, u32[]{:S(2)}) collective-permute-start(bf16[96,16]{0,1:T(8,128)(2,1)S(1)} %get-tuple-element.67), channel_id=1, source_target_pairs={{0,4},{4,8},{8,12},{12,16},{16,20},{20,24},{24,28},{1,5},{5,9},{9,... | collective-permute-start | bytes 9224 | tf_op jit(solution)/shard_map/ppermute | solution.py:13
  393.7 4.8 collective-permute-start.46
  402.0 4.3 collective-permute-start.43
  414.9 101.2 %all-reduce.7.cloned.1.call-done = (f32[27,96,96]{1,2,0:T(8,128)}, f32[27,96,96]{1,2,0:T(8,128)}) async-done(((f32[27,96,96]{1,2,0:T(8,128)}, f32[27,96,96]{1,2,0:T(8,128)}), (f32[27,96,96]{1,2,0:T(8,128)}, f32[27,96,96]{1,2,0:T(8,128)})) %all-reduce.7.cloned.1.call-update) | async-done | bytes 1990672 | tf_op jit(solution)/shard_map/psum | solution.py:173
  (252 shorter events, 114.8 us)
Async XLA Ops:
  7.2 508.8 %all-reduce.7.cloned.1.call-start = ((), (), s32[]{:S(2)}) async-start(), calls=%async_computation | async-start | bytes 5308416 | tf_op jit(solution)/shard_map/psum | solution.py:173
  10.5 21.1 %collective-permute-start = (bf16[96,16]{0,1:T(8,128)(2,1)S(1)}, bf16[96,16]{0,1:T(8,128)(2,1)S(1)}, u32[]{:S(2)}, u32[]{:S(2)}) collective-permute-start(bf16[96,16]{0,1:T(8,128)(2,1)S(1)} %select_bitcast_fusion.15), channel_id=1, source_target_pairs={{0,4},{4,8},{8,12},{12,16},{16,20},{20,24},{24,28},{1,5},{5,9},{9,... | collective-permute-start | bytes 9224 | tf_op jit(solution)/shard_map/ppermute | solution.py:13
  16.0 16.9 %collective-permute-start.1 = (bf16[96,16]{0,1:T(8,128)(2,1)S(1)}, bf16[96,16]{0,1:T(8,128)(2,1)S(1)}, u32[]{:S(2)}, u32[]{:S(2)}) collective-permute-start(bf16[96,16]{0,1:T(8,128)(2,1)S(1)} %select_bitcast_fusion.14), channel_id=1, source_target_pairs={{4,0},{8,4},{12,8},{16,12},{20,16},{24,20},{28,24},{5,1},{9,5},{13... | collective-permute-start | bytes 9224 | tf_op jit(solution)/shard_map/ppermute | solution.py:13
  18.0 16.8 %collective-permute-start.2 = (bf16[96,16]{0,1:T(8,128)(2,1)S(1)}, bf16[96,16]{0,1:T(8,128)(2,1)S(1)}, u32[]{:S(2)}, u32[]{:S(2)}) collective-permute-start(bf16[96,16]{0,1:T(8,128)(2,1)S(1)} %select_bitcast_fusion.13), channel_id=1, source_target_pairs={{0,1},{1,2},{2,3},{4,5},{5,6},{6,7},{8,9},{9,10},{10,11},{12,13},{... | collective-permute-start | bytes 9224 | tf_op jit(solution)/shard_map/ppermute | solution.py:13
  20.1 16.0 %collective-permute-start.4 = (bf16[96,16]{0,1:T(8,128)(2,1)S(1)}, bf16[96,16]{0,1:T(8,128)(2,1)S(1)}, u32[]{:S(2)}, u32[]{:S(2)}) collective-permute-start(bf16[96,16]{0,1:T(8,128)(2,1)S(1)} %select_bitcast_fusion.11), channel_id=1, source_target_pairs={{0,4},{4,8},{8,12},{12,16},{16,20},{20,24},{24,28},{1,5},{5,9},{9,... | collective-permute-start | bytes 9224 | tf_op jit(solution)/shard_map/ppermute | solution.py:13
  25.1 15.2 %collective-permute-start.6 = (bf16[96,16]{0,1:T(8,128)(2,1)S(1)}, bf16[96,16]{0,1:T(8,128)(2,1)S(1)}, u32[]{:S(2)}, u32[]{:S(2)}) collective-permute-start(bf16[96,16]{0,1:T(8,128)(2,1)S(1)} %select_bitcast_fusion.10), channel_id=1, source_target_pairs={{0,4},{4,8},{8,12},{12,16},{16,20},{20,24},{24,28},{1,5},{5,9},{9,... | collective-permute-start | bytes 9224 | tf_op jit(solution)/shard_map/ppermute | solution.py:13
  34.8 13.4 %collective-permute-start.3 = (bf16[96,16]{0,1:T(8,128)(2,1)S(1)}, bf16[96,16]{0,1:T(8,128)(2,1)S(1)}, u32[]{:S(2)}, u32[]{:S(2)}) collective-permute-start(bf16[96,16]{0,1:T(8,128)(2,1)S(1)} %select_bitcast_fusion.12), channel_id=1, source_target_pairs={{1,0},{2,1},{3,2},{5,4},{6,5},{7,6},{9,8},{10,9},{11,10},{13,12},{... | collective-permute-start | bytes 9224 | tf_op jit(solution)/shard_map/ppermute | solution.py:13
  110.5 15.8 %collective-permute-start.12 = (bf16[96,16]{0,1:T(8,128)(2,1)S(1)}, bf16[96,16]{0,1:T(8,128)(2,1)S(1)}, u32[]{:S(2)}, u32[]{:S(2)}) collective-permute-start(bf16[96,16]{0,1:T(8,128)(2,1)S(1)} %select_bitcast_fusion.7), channel_id=1, source_target_pairs={{0,4},{4,8},{8,12},{12,16},{16,20},{20,24},{24,28},{1,5},{5,9},{9,... | collective-permute-start | bytes 9224 | tf_op jit(solution)/shard_map/ppermute | solution.py:13
  122.1 13.4 %collective-permute-start.18 = (bf16[96,16]{0,1:T(8,128)(2,1)S(1)}, bf16[96,16]{0,1:T(8,128)(2,1)S(1)}, u32[]{:S(2)}, u32[]{:S(2)}) collective-permute-start(bf16[96,16]{0,1:T(8,128)(2,1)S(1)} %select_bitcast_fusion.2), channel_id=1, source_target_pairs={{0,4},{4,8},{8,12},{12,16},{16,20},{20,24},{24,28},{1,5},{5,9},{9,... | collective-permute-start | bytes 9224 | tf_op jit(solution)/shard_map/ppermute | solution.py:13
  127.7 13.5 %collective-permute-start.22 = (bf16[96,16]{0,1:T(8,128)(2,1)S(1)}, bf16[96,16]{0,1:T(8,128)(2,1)S(1)}, u32[]{:S(2)}, u32[]{:S(2)}) collective-permute-start(bf16[96,16]{0,1:T(8,128)(2,1)S(1)} %select_bitcast_fusion), channel_id=1, source_target_pairs={{4,0},{8,4},{12,8},{16,12},{20,16},{24,20},{28,24},{5,1},{9,5},{13... | collective-permute-start | bytes 9224 | tf_op jit(solution)/shard_map/ppermute | solution.py:13
  129.1 13.8 %collective-permute-start.15 = (bf16[96,16]{0,1:T(8,128)(2,1)S(1)}, bf16[96,16]{0,1:T(8,128)(2,1)S(1)}, u32[]{:S(2)}, u32[]{:S(2)}) collective-permute-start(bf16[96,16]{0,1:T(8,128)(2,1)S(1)} %select_bitcast_fusion.4), channel_id=1, source_target_pairs={{1,0},{2,1},{3,2},{5,4},{6,5},{7,6},{9,8},{10,9},{11,10},{13,12},{... | collective-permute-start | bytes 9224 | tf_op jit(solution)/shard_map/ppermute | solution.py:13
  268.8 14.8 %collective-permute-start.25 = (bf16[96,16]{0,1:T(8,128)(2,1)S(1)}, bf16[96,16]{0,1:T(8,128)(2,1)S(1)}, u32[]{:S(2)}, u32[]{:S(2)}) collective-permute-start(bf16[96,16]{0,1:T(8,128)(2,1)S(1)} %get-tuple-element.80), channel_id=1, source_target_pairs={{0,4},{4,8},{8,12},{12,16},{16,20},{20,24},{24,28},{1,5},{5,9},{9,... | collective-permute-start | bytes 9224 | tf_op jit(solution)/shard_map/ppermute | solution.py:13
  273.6 14.9 %collective-permute-start.26 = (bf16[96,16]{0,1:T(8,128)(2,1)S(1)}, bf16[96,16]{0,1:T(8,128)(2,1)S(1)}, u32[]{:S(2)}, u32[]{:S(2)}) collective-permute-start(bf16[96,16]{0,1:T(8,128)(2,1)S(1)} %get-tuple-element.79), channel_id=1, source_target_pairs={{1,0},{2,1},{3,2},{5,4},{6,5},{7,6},{9,8},{10,9},{11,10},{13,12},{... | collective-permute-start | bytes 9224 | tf_op jit(solution)/shard_map/ppermute | solution.py:13
  274.9 15.8 %collective-permute-start.28 = (bf16[96,16]{0,1:T(8,128)(2,1)S(1)}, bf16[96,16]{0,1:T(8,128)(2,1)S(1)}, u32[]{:S(2)}, u32[]{:S(2)}) collective-permute-start(bf16[96,16]{0,1:T(8,128)(2,1)S(1)} %get-tuple-element.77), channel_id=1, source_target_pairs={{4,0},{8,4},{12,8},{16,12},{20,16},{24,20},{28,24},{5,1},{9,5},{13... | collective-permute-start | bytes 9224 | tf_op jit(solution)/shard_map/ppermute | solution.py:13
  276.2 15.8 %collective-permute-start.30 = (bf16[96,16]{0,1:T(8,128)(2,1)S(1)}, bf16[96,16]{0,1:T(8,128)(2,1)S(1)}, u32[]{:S(2)}, u32[]{:S(2)}) collective-permute-start(bf16[96,16]{0,1:T(8,128)(2,1)S(1)} %get-tuple-element.76), channel_id=1, source_target_pairs={{4,0},{8,4},{12,8},{16,12},{20,16},{24,20},{28,24},{5,1},{9,5},{13... | collective-permute-start | bytes 9224 | tf_op jit(solution)/shard_map/ppermute | solution.py:13
  277.5 18.6 %collective-permute-start.32 = (bf16[96,16]{0,1:T(8,128)(2,1)S(1)}, bf16[96,16]{0,1:T(8,128)(2,1)S(1)}, u32[]{:S(2)}, u32[]{:S(2)}) collective-permute-start(bf16[96,16]{0,1:T(8,128)(2,1)S(1)} %get-tuple-element.75), channel_id=1, source_target_pairs={{0,4},{4,8},{8,12},{12,16},{16,20},{20,24},{24,28},{1,5},{5,9},{9,... | collective-permute-start | bytes 9224 | tf_op jit(solution)/shard_map/ppermute | solution.py:13
  283.6 13.8 %collective-permute-start.34 = (bf16[96,16]{0,1:T(8,128)(2,1)S(1)}, bf16[96,16]{0,1:T(8,128)(2,1)S(1)}, u32[]{:S(2)}, u32[]{:S(2)}) collective-permute-start(bf16[96,16]{0,1:T(8,128)(2,1)S(1)} %get-tuple-element.74), channel_id=1, source_target_pairs={{0,4},{4,8},{8,12},{12,16},{16,20},{20,24},{24,28},{1,5},{5,9},{9,... | collective-permute-start | bytes 9224 | tf_op jit(solution)/shard_map/ppermute | solution.py:13
  378.9 14.8 %collective-permute-start.37 = (bf16[96,16]{0,1:T(8,128)(2,1)S(1)}, bf16[96,16]{0,1:T(8,128)(2,1)S(1)}, u32[]{:S(2)}, u32[]{:S(2)}) collective-permute-start(bf16[96,16]{0,1:T(8,128)(2,1)S(1)} %get-tuple-element.72), channel_id=1, source_target_pairs={{0,4},{4,8},{8,12},{12,16},{16,20},{20,24},{24,28},{1,5},{5,9},{9,... | collective-permute-start | bytes 9224 | tf_op jit(solution)/shard_map/ppermute | solution.py:13
  383.7 14.9 %collective-permute-start.38 = (bf16[96,16]{0,1:T(8,128)(2,1)S(1)}, bf16[96,16]{0,1:T(8,128)(2,1)S(1)}, u32[]{:S(2)}, u32[]{:S(2)}) collective-permute-start(bf16[96,16]{0,1:T(8,128)(2,1)S(1)} %get-tuple-element.71), channel_id=1, source_target_pairs={{1,0},{2,1},{3,2},{5,4},{6,5},{7,6},{9,8},{10,9},{11,10},{13,12},{... | collective-permute-start | bytes 9224 | tf_op jit(solution)/shard_map/ppermute | solution.py:13
  385.0 15.8 %collective-permute-start.40 = (bf16[96,16]{0,1:T(8,128)(2,1)S(1)}, bf16[96,16]{0,1:T(8,128)(2,1)S(1)}, u32[]{:S(2)}, u32[]{:S(2)}) collective-permute-start(bf16[96,16]{0,1:T(8,128)(2,1)S(1)} %get-tuple-element.69), channel_id=1, source_target_pairs={{4,0},{8,4},{12,8},{16,12},{20,16},{24,20},{28,24},{5,1},{9,5},{13... | collective-permute-start | bytes 9224 | tf_op jit(solution)/shard_map/ppermute | solution.py:13
  386.3 15.8 %collective-permute-start.42 = (bf16[96,16]{0,1:T(8,128)(2,1)S(1)}, bf16[96,16]{0,1:T(8,128)(2,1)S(1)}, u32[]{:S(2)}, u32[]{:S(2)}) collective-permute-start(bf16[96,16]{0,1:T(8,128)(2,1)S(1)} %get-tuple-element.68), channel_id=1, source_target_pairs={{4,0},{8,4},{12,8},{16,12},{20,16},{24,20},{28,24},{5,1},{9,5},{13... | collective-permute-start | bytes 9224 | tf_op jit(solution)/shard_map/ppermute | solution.py:13
  387.6 18.8 %collective-permute-start.44 = (bf16[96,16]{0,1:T(8,128)(2,1)S(1)}, bf16[96,16]{0,1:T(8,128)(2,1)S(1)}, u32[]{:S(2)}, u32[]{:S(2)}) collective-permute-start(bf16[96,16]{0,1:T(8,128)(2,1)S(1)} %get-tuple-element.67), channel_id=1, source_target_pairs={{0,4},{4,8},{8,12},{12,16},{16,20},{20,24},{24,28},{1,5},{5,9},{9,... | collective-permute-start | bytes 9224 | tf_op jit(solution)/shard_map/ppermute | solution.py:13
  393.7 14.0 %collective-permute-start.46 = (bf16[96,16]{0,1:T(8,128)(2,1)S(1)}, bf16[96,16]{0,1:T(8,128)(2,1)S(1)}, u32[]{:S(2)}, u32[]{:S(2)}) collective-permute-start(bf16[96,16]{0,1:T(8,128)(2,1)S(1)} %get-tuple-element.66), channel_id=1, source_target_pairs={{0,4},{4,8},{8,12},{12,16},{16,20},{20,24},{24,28},{1,5},{5,9},{9,... | collective-permute-start | bytes 9224 | tf_op jit(solution)/shard_map/ppermute | solution.py:13
  398.5 13.4 %collective-permute-start.39 = (bf16[96,16]{0,1:T(8,128)(2,1)S(1)}, bf16[96,16]{0,1:T(8,128)(2,1)S(1)}, u32[]{:S(2)}, u32[]{:S(2)}) collective-permute-start(bf16[96,16]{0,1:T(8,128)(2,1)S(1)} %get-tuple-element.70), channel_id=1, source_target_pairs={{0,1},{1,2},{2,3},{4,5},{5,6},{6,7},{8,9},{9,10},{10,11},{12,13},{... | collective-permute-start | bytes 9224 | tf_op jit(solution)/shard_map/ppermute | solution.py:13
  (48 other events, 1066.7 us)
Sparse Core Ops, SparseCore 0:
  378.1 137.8 all-reduce.6
where the time goes:
time: 530 us; the launch traced here: 527 us
  blocking collectives  169 us (32%)
  starting transfers between devices  130 us (25%)
  waiting for transfers between devices  106 us (20%)
  other arithmetic  57.2 us (11%)
  local copies, waits for them, and re-layouts  38.3 us (7%)
  between operations  16.1 us (3%)
  matrix products  9.74 us (2%)
    ppermute x48, starting transfers between devices, from_behind(): return lax.ppermute(x, axis, pairs)  130 us
    psum x1, waiting for transfers between devices, on_device(): lax.psum((grad_weight_one, grad_weight_two), ('gx', 'gy'))  101 us
    psum x2, blocking collectives, apply_batch_norm(): lax.psum((jnp.sum(masked, axis=1), jnp.sum(masked * pre_norm, axis=1), jn...  86.4 us
    psum x2, blocking collectives, norm_backward_step(): lax.psum((jnp.sum(linear_gradient * normalized_input * active_mask, axis=...  82.7 us
    scatter-add x2, other arithmetic, spread_back(): table = jnp.zeros((channels, table_len), jnp.float32).at[:, kernel_map.re...  40.1 us
    gather x2, local copies, waits for them, and re-layouts, convolve(): jnp.take(extended, kernel_map.reshape(-1), axis=1)  14.3 us
  transfers between devices with their start and end apart: 49, of which 5 were waited for; matrix products, arithmetic and copies ran while one was open for 3% of the time, Pallas kernels for 0%

commit v1 on v0

v1 whole, which is shorter than its diff:
```python
import functools

import jax
import jax.numpy as jnp
from jax import lax
from jax.experimental import pallas as pl
from jax.experimental.pallas import tpu as pltpu
from jax.sharding import PartitionSpec as P

EPS = 1e-05
STEP_LIST = ((1, 0), (-1, 0), (0, 1), (0, -1), (1, 1), (1, -1), (-1, 1), (-1, -1))
AXES = ("gx", "gy")
LANES = 128
F32 = jnp.float32
BF16 = jnp.bfloat16


def nn(a, b):
    return lax.dot_general(a, b, (((1,), (0,)), ((), ())), preferred_element_type=F32)


def nt(a, b):
    return lax.dot_general(a, b, (((1,), (1,)), ((), ())), preferred_element_type=F32)


def iota(shape, dim):
    return lax.broadcasted_iota(jnp.int32, shape, dim)


def eye(size):
    return jnp.where(iota((size, size), 0) == iota((size, size), 1), 1.0, 0.0).astype(BF16)


def sigmoid(v):
    return 1.0 / (1.0 + jnp.exp(-v))


def neighbour(place, grid, step):
    i, j = place[0] + step[0], place[1] + step[1]
    inside = (i >= 0) & (i < grid[0]) & (j >= 0) & (j < grid[1])
    return jnp.where(inside, i * grid[1] + j, place[0] * grid[1] + place[1]), inside


def here():
    return lax.axis_index("gx"), lax.axis_index("gy")


def put_blocks(buf_ref, rows, grid, sign, width, base=None):
    place = here()
    for n, (a, b) in enumerate(STEP_LIST):
        dest, _ = neighbour(place, grid, (sign * a, sign * b))
        block = rows[n * width : (n + 1) * width]
        if base is not None:
            block = jnp.where(iota(block.shape, 1) < 96, block, base)
        buf_ref[dest, 0:width, :] = block.astype(BF16)


def take_blocks(buf_ref, grid, sign, width):
    place = here()
    blocks = []
    for a, b in STEP_LIST:
        src, inside = neighbour(place, grid, (sign * a, sign * b))
        block = buf_ref[src, 0:width, :].astype(F32)
        blocks.append(jnp.where(inside, block, 0.0))
    return jnp.concatenate(blocks, axis=0)


def pad_to(x, rows, lanes):
    if x.shape[1] < lanes:
        x = jnp.concatenate([x, jnp.zeros((x.shape[0], lanes - x.shape[1]), x.dtype)], axis=1)
    if x.shape[0] < rows:
        x = jnp.concatenate([x, jnp.zeros((rows - x.shape[0], lanes), x.dtype)], axis=0)
    return x


def cols_to_rows(cols):
    lane = iota((cols[0].shape[0], LANES), 1)
    total = jnp.zeros((cols[0].shape[0], LANES), F32)
    for at, col in enumerate(cols):
        total = jnp.where(lane == at, col, total)
    return pad_to(total, LANES, LANES).T


def rows_to_cols(rows):
    sub = iota((LANES, LANES), 0)
    total = jnp.zeros((LANES, LANES), F32)
    for at, row in enumerate(rows):
        total = jnp.where(sub == at, row, total)
    total = total.T
    return [total[:, at : at + 1] for at in range(len(rows))]


def split3(x):
    high = x.astype(BF16).astype(F32)
    mid = (x - high).astype(BF16).astype(F32)
    low = (x - high - mid).astype(BF16).astype(F32)
    return [high, mid, low]


def pack_rows(pieces, last):
    sub = iota((16, LANES), 0)
    lane = iota((16, LANES), 1)
    total = jnp.zeros((16, LANES), F32)
    for q, piece in enumerate(pieces):
        total = jnp.where(sub // 3 == q, piece, total)
    part = sub % 3
    moved = jnp.where(
        part == 0,
        pltpu.roll(total, 96, 1),
        jnp.where(part == 1, pltpu.roll(total, 64, 1), pltpu.roll(total, 32, 1)),
    )
    moved = jnp.where(sub == 15, last, moved)
    return jnp.where(lane >= 96, moved, 0.0)


def unpack_rows(tiles, groups):
    devices = tiles.shape[0]
    flat = tiles.reshape(devices * 16, LANES)
    sub = iota(tiles.shape, 1)
    lane = iota(tiles.shape, 2)
    part = sub % 3
    moved = [pltpu.roll(flat, 32 * (p + 1), 1).reshape(tiles.shape) for p in range(3)]
    value = jnp.where(part == 0, moved[0], jnp.where(part == 1, moved[1], moved[2]))
    value = jnp.where((lane // 32 == part) & (sub < 15), value, 0.0)
    results = []
    for low, high in groups:
        mask = (sub >= 3 * low) & (sub < 3 * high)
        results.append(jnp.sum(jnp.where(mask, value, 0.0), axis=1))
    return results


def valid_lanes(counts_ref, rows=1):
    return (iota((rows, LANES), 1) < counts_ref[0]).astype(F32)


def open_kernel(grid, counts_ref, features_ref, send_ref, buf_ref, start_ref, pick_ref, place_ref):
    width = send_ref.shape[1]
    send = send_ref[...].astype(F32).astype(BF16)
    spread = jnp.where(iota((width, LANES), 1) % width == iota((width, LANES), 0), 1.0, 0.0).astype(BF16)
    wide = nn(send, spread)
    wide = jnp.where(iota(wide.shape, 1) // width == iota(wide.shape, 0), wide, 0.0)
    row = jnp.sum(wide, axis=0, keepdims=True)
    pick = jnp.where(row == iota((LANES, LANES), 0).astype(F32), 1.0, 0.0)
    pick_ref[...] = pick.astype(BF16)
    place = pick.T.astype(BF16)
    place_ref[...] = place
    valid = valid_lanes(counts_ref)
    start = features_ref[...].astype(F32) * valid
    start_ref[...] = start.astype(BF16)
    extra = jnp.where(iota((LANES - 96, LANES), 0) == 0, valid, 0.0)
    rows = nt(place, jnp.concatenate([start, extra], axis=0).astype(BF16))
    put_blocks(buf_ref, rows, grid, 1, width)


def prepare_kernel(map_ref, one_ref, two_ref, hot_ref, one_t_ref, two_t_ref):
    table = hot_ref.shape[0]
    sub = iota((table, LANES), 0)
    for k in range(map_ref.shape[0]):
        hot_ref[:, k * LANES : (k + 1) * LANES] = jnp.where(
            sub == map_ref[k : k + 1, :], 1.0, 0.0
        ).astype(BF16)
    unit = eye(one_ref.shape[1])
    one_t_ref[...] = nt(unit, one_ref[...]).astype(BF16)
    two_t_ref[...] = nt(unit, two_ref[...]).astype(BF16)


def gather_convolve(table, hot_ref, weight_t_ref, taken_ref):
    channels = table.shape[0]
    taken = nn(table, hot_ref[...]).astype(BF16)
    offsets = hot_ref.shape[1] // LANES
    for k in range(offsets):
        taken_ref[k * channels : (k + 1) * channels, :] = taken[:, k * LANES : (k + 1) * LANES]
    return nn(weight_t_ref[...], taken_ref[...])


def first_kernel(
    grid, counts_ref, buf_ref, start_ref, hot_ref, weight_ref, place_ref,
    out_buf_ref, hidden_ref, taken_ref, flag_ref,
):
    width = buf_ref.shape[1]
    channels = start_ref.shape[0]
    halo_rows = take_blocks(buf_ref, grid, -1, width).astype(BF16)
    flag_ref[...] = jnp.broadcast_to(halo_rows[:, 96:97].astype(F32), (LANES, LANES))
    halo = nt(eye(LANES), halo_rows)[:channels].astype(BF16)
    table = jnp.concatenate([start_ref[...], halo], axis=1)
    hidden = gather_convolve(table, hot_ref, weight_ref, taken_ref)
    hidden_ref[...] = hidden
    valid = valid_lanes(counts_ref)
    count = counts_ref[0].astype(F32)
    sums = jnp.sum(hidden * valid, axis=1, keepdims=True)
    centred = (hidden - sums / count) * valid
    spread = jnp.sum(centred * centred, axis=1, keepdims=True)
    stat = cols_to_rows([sums, spread])
    base = pack_rows(split3(stat[0:1]) + split3(stat[1:2])[:2], count)
    out_buf_ref[...] = jnp.broadcast_to(base.astype(BF16)[None], out_buf_ref.shape)
    rows = pad_to(nt(place_ref[...], centred.astype(BF16)), LANES, LANES)
    put_blocks(out_buf_ref, rows, grid, 1, width, base)


def second_kernel(
    grid, counts_ref, buf_ref, hidden_ref, flag_ref, scale_ref, bias_ref, hot_ref, weight_ref,
    out_buf_ref, hidden_two_ref, taken_ref, norm_ref, slope_ref, halo_slope_ref, halo_cross_ref,
    const_ref, mean_ref,
):
    width = buf_ref.shape[1]
    channels = hidden_ref.shape[0]
    tiles = buf_ref[...].astype(F32)
    sums, spreads = unpack_rows(tiles, ((0, 3), (3, 5)))
    counts = tiles[:, 15, 96:97]
    total = jnp.sum(counts, axis=0, keepdims=True)
    means = sums / counts
    mean_ref[...] = means
    mean = jnp.sum(sums, axis=0, keepdims=True) / total
    apart = means - mean
    var = jnp.sum(spreads + counts * apart * apart, axis=0, keepdims=True) / total
    rstd = lax.rsqrt(var + EPS)
    scale = pad_to(scale_ref[...], 1, LANES)
    bias = pad_to(bias_ref[...], 1, LANES)
    total_row = jnp.broadcast_to(total, (1, LANES))
    mean_c, rstd_c, scale_c, bias_c = [c[:channels] for c in rows_to_cols([mean, rstd, scale, bias])]
    sub = iota((8, LANES), 0)
    const_ref[...] = jnp.where(sub == 0, scale * rstd, jnp.where(sub == 1, total_row, 0.0))

    valid = valid_lanes(counts_ref)
    normal = (hidden_ref[...] - mean_c) * rstd_c
    norm_ref[...] = normal
    linear = scale_c * normal + bias_c
    sig = sigmoid(linear)
    slope_ref[...] = sig * (1.0 + linear * (1.0 - sig)) * valid
    act = (linear * sig * valid).astype(BF16)

    place = here()
    lifted = []
    for n, (a, b) in enumerate(STEP_LIST):
        src, inside = neighbour(place, grid, (-a, -b))
        block = buf_ref[src, 0:width, :].astype(F32) + mean_ref[pl.ds(src, 1), :]
        lifted.append(jnp.where(inside, block, 0.0))
    lane = iota((LANES, LANES), 1)
    halo = jnp.where(lane < channels, jnp.concatenate(lifted, axis=0), 0.0)
    flag = flag_ref[...]
    halo_normal = (halo - mean) * rstd
    halo_linear = scale * halo_normal + bias
    halo_sig = sigmoid(halo_linear)
    halo_slope = halo_sig * (1.0 + halo_linear * (1.0 - halo_sig)) * flag
    halo_slope_ref[...] = halo_slope
    halo_cross_ref[...] = halo_slope * halo_normal
    halo_act = nt(eye(LANES), (halo_linear * halo_sig * flag).astype(BF16))[:channels].astype(BF16)

    hidden = gather_convolve(jnp.concatenate([act, halo_act], axis=1), hot_ref, weight_ref, taken_ref)
    hidden_two_ref[...] = hidden
    count = counts_ref[0].astype(F32)
    sums_two = jnp.sum(hidden * valid, axis=1, keepdims=True)
    centred = (hidden - sums_two / count) * valid
    spread_two = jnp.sum(centred * centred, axis=1, keepdims=True)
    stat = cols_to_rows([sums_two, spread_two])[0:2]
    stat = jnp.where(iota((2, LANES), 1) < 96, stat, count)
    out_buf_ref[...] = jnp.broadcast_to(stat[None], out_buf_ref.shape)


def third_kernel(
    counts_ref, buf_ref, hidden_ref, start_ref, cotangent_ref, scale_ref, bias_ref,
    out_buf_ref, output_ref, norm_ref, grad_ref, const_ref,
):
    channels = hidden_ref.shape[0]
    sums = buf_ref[:, 0, :]
    spreads = buf_ref[:, 1, :]
    counts = sums[:, 96:97]
    total = jnp.sum(counts, axis=0, keepdims=True)
    mean = jnp.sum(sums, axis=0, keepdims=True) / total
    apart = sums / counts - mean
    var = jnp.sum(spreads + counts * apart * apart, axis=0, keepdims=True) / total
    rstd = lax.rsqrt(var + EPS)
    scale = pad_to(scale_ref[...], 1, LANES)
    bias = pad_to(bias_ref[...], 1, LANES)
    total_row = jnp.broadcast_to(total, (1, LANES))
    mean_c, rstd_c, scale_c, bias_c = [c[:channels] for c in rows_to_cols([mean, rstd, scale, bias])]
    sub = iota((8, LANES), 0)
    const_ref[...] = jnp.where(sub == 0, scale * rstd, jnp.where(sub == 1, total_row, 0.0))
    valid = valid_lanes(counts_ref)
    normal = (hidden_ref[...] - mean_c) * rstd_c
    norm_ref[...] = normal
    summed = scale_c * normal + bias_c + start_ref[...].astype(F32)
    sig = sigmoid(summed)
    output_ref[...] = (summed * sig * valid).astype(BF16)
    grad = cotangent_ref[...].astype(F32) * valid * (sig * (1.0 + summed * (1.0 - sig)))
    grad_ref[...] = grad
    dbias = jnp.sum(grad, axis=1, keepdims=True)
    dgain = jnp.sum(grad * normal * valid, axis=1, keepdims=True)
    rows = cols_to_rows([dgain, dbias])[0:2]
    out_buf_ref[...] = jnp.broadcast_to(rows[None], out_buf_ref.shape)


def scatter(grad, weight_ref, hot_ref):
    channels = grad.shape[0]
    terms = nn(weight_ref[...], grad).astype(BF16)
    offsets = hot_ref.shape[1] // LANES
    wide = jnp.concatenate([terms[k * channels : (k + 1) * channels] for k in range(offsets)], axis=1)
    return nt(wide, hot_ref[...])


def row_gradient(grad, normal, const, dgain, dbias, valid):
    channels = grad.shape[0]
    factor, part_bias, part_gain = rows_to_cols([const[0:1], dbias / const[1:2], dgain / const[1:2]])
    return (
        factor[:channels] * (grad - (part_bias[:channels] + normal * part_gain[:channels])) * valid
    ).astype(BF16)


def fourth_kernel(
    grid, counts_ref, buf_ref, norm_ref, grad_ref, const_ref, weight_ref, hot_ref,
    norm_one_ref, slope_ref, halo_slope_ref, halo_cross_ref,
    out_buf_ref, grad_two_ref, table_ref, sums_ref,
):
    channels = norm_ref.shape[0]
    width = out_buf_ref.shape[1]
    valid = valid_lanes(counts_ref)
    both = jnp.sum(buf_ref[...], axis=0)
    sums_ref[...] = both
    grad = row_gradient(grad_ref[...], norm_ref[...], const_ref[...], both[0:1], both[1:2], valid)
    grad_two_ref[...] = grad
    table = scatter(grad, weight_ref, hot_ref)
    local = table[:, :LANES]
    table_ref[...] = local
    halo = pad_to(table[:, LANES : 2 * LANES], LANES, LANES).T
    pulled = local * slope_ref[...]
    dbias = jnp.sum(pulled, axis=1, keepdims=True)
    dgain = jnp.sum(pulled * norm_one_ref[...], axis=1, keepdims=True)
    rows = cols_to_rows([dgain, dbias])
    dgain = rows[0:1] + jnp.sum(halo * halo_cross_ref[...], axis=0, keepdims=True)
    dbias = rows[1:2] + jnp.sum(halo * halo_slope_ref[...], axis=0, keepdims=True)
    base = pack_rows(split3(dgain)[:2] + split3(dbias)[:2], 0.0)
    out_buf_ref[...] = jnp.broadcast_to(base.astype(BF16)[None], out_buf_ref.shape)
    put_blocks(out_buf_ref, halo, grid, -1, width, base)


def packed_weight_grad(taken_ref, grad, put):
    channels = grad.shape[0]
    zero = jnp.zeros((channels, LANES), BF16)

    def taken(k):
        return taken_ref[k * channels : (k + 1) * channels, :]

    for part in range(3):
        upper = jnp.concatenate([grad, zero], axis=1)
        lower = jnp.concatenate([zero[:32], grad[32 * part : 32 * part + 32]], axis=1)
        right = jnp.concatenate([upper, lower], axis=0)
        left = jnp.concatenate(
            [
                jnp.concatenate([taken(3 * e + part) for e in range(6)], axis=0),
                jnp.concatenate([taken(21 + e) for e in range(6)], axis=0),
            ],
            axis=1,
        )
        result = nt(left, right)
        for e in range(6):
            put(3 * e + part, result[e * channels : (e + 1) * channels])
    last = nt(taken_ref[18 * channels : 21 * channels, :], pad_to(grad, LANES, LANES))
    for e in range(3):
        put(18 + e, last[e * channels : (e + 1) * channels])


def weight_two_kernel(taken_ref, grad_ref, out_ref):
    channels = grad_ref.shape[0]

    def put(block, value):
        out_ref[block * channels : (block + 1) * channels, :] = value.astype(BF16)

    packed_weight_grad(taken_ref, grad_ref[...], put)
    tail = out_ref.shape[0] - 21 * channels
    if tail:
        out_ref[21 * channels :, :] = jnp.zeros((tail, LANES), BF16)


def fifth_kernel(
    grid, counts_ref, buf_ref, table_ref, place_ref, norm_ref, slope_ref, const_ref, sums_two_ref, taken_ref,
    packed_two_ref, grad_one_ref, give_ref, keep_ref, sums_ref,
):
    width = buf_ref.shape[1]
    channels = norm_ref.shape[0]
    valid = valid_lanes(counts_ref)
    dgains, dbiases = unpack_rows(buf_ref[...].astype(F32), ((0, 2), (2, 4)))
    dgain = jnp.sum(dgains, axis=0, keepdims=True)
    dbias = jnp.sum(dbiases, axis=0, keepdims=True)
    two = sums_two_ref[...]
    sums_ref[...] = jnp.concatenate([dgain, dbias, two], axis=0)[:, :channels]
    arrived = nt(eye(LANES), take_blocks(buf_ref, grid, 1, width).astype(BF16))[:channels].astype(BF16)
    back = table_ref[...] + nn(arrived, place_ref[...])
    grad = row_gradient(back * slope_ref[...], norm_ref[...], const_ref[...], dgain, dbias, valid)
    grad_one_ref[...] = grad
    core = lax.axis_index("gy") % 2
    used = 21 * channels

    @pl.when(core == 0)
    def _():
        def put(block, value):
            keep_ref[block * channels : (block + 1) * channels, :] = value.astype(BF16)

        packed_weight_grad(taken_ref, grad, put)
        give_ref[...] = packed_two_ref[...]
        if keep_ref.shape[0] > used:
            keep_ref[used:, :] = jnp.zeros((keep_ref.shape[0] - used, LANES), BF16)

    @pl.when(core != 0)
    def _():
        def put(block, value):
            give_ref[block * channels : (block + 1) * channels, :] = value.astype(BF16)

        packed_weight_grad(taken_ref, grad, put)
        keep_ref[...] = packed_two_ref[...]
        if keep_ref.shape[0] > used:
            give_ref[used:, :] = jnp.zeros((keep_ref.shape[0] - used, LANES), BF16)


def back_kernel(grad_ref, weight_ref, hot_ref, table_ref, halo_ref):
    table = scatter(grad_ref[...], weight_ref, hot_ref)
    table_ref[...] = table[:, :LANES]
    halo_ref[...] = pad_to(table[:, LANES : 2 * LANES], LANES, LANES).T.astype(BF16)


def sixth_kernel(grid, width, halo_ref, keep_ref, got_ref, out_buf_ref):
    devices, rows = out_buf_ref.shape[0], out_buf_ref.shape[1] - width
    put_blocks(out_buf_ref, halo_ref[...], grid, -1, width)
    total = (keep_ref[...].astype(F32) + got_ref[...].astype(F32)).astype(BF16)
    out_buf_ref[:, width:, :] = total.reshape(devices, rows, LANES)


def seventh_kernel(grid, width, counts_ref, buf_ref, table_ref, place_ref, grad_ref, out_buf_ref, out_ref):
    channels = table_ref.shape[0]
    devices, rows = buf_ref.shape[0], buf_ref.shape[1] - width
    valid = valid_lanes(counts_ref)
    arrived = nt(eye(LANES), take_blocks(buf_ref, grid, 1, width).astype(BF16))[:channels].astype(BF16)
    back = table_ref[...] + nn(arrived, place_ref[...])
    out_ref[...] = ((back + grad_ref[...]) * valid).astype(BF16)
    pieces = []
    for core in range(2):
        total = jnp.zeros((rows, LANES), F32)
        for d in range(core, devices, 2):
            total = total + buf_ref[d, width:, :].astype(F32)
        pieces.append(total.astype(BF16))
    for d in range(devices):
        out_buf_ref[d] = pieces[d % 2]


def last_kernel(own_ref, other_ref, one_ref, two_ref):
    core = lax.axis_index("gy") % 2
    channels = one_ref.shape[1]

    def unpack(src_ref, dst_ref):
        lane = iota((channels, LANES), 1)
        for e in range(7):
            extra = jnp.zeros((channels, LANES), F32)
            for part in range(3):
                block = 3 * e + part
                value = src_ref[block * channels : (block + 1) * channels, :].astype(F32)
                dst_ref[block] = value[:, :channels]
                if e < 6:
                    moved = pltpu.roll(value, 32 * (part + 1), 1)
                    extra = jnp.where(lane // 32 == part, moved, extra)
            if e < 6:
                dst_ref[21 + e] = extra[:, :channels]

    @pl.when(core == 0)
    def _():
        unpack(own_ref, one_ref)
        unpack(other_ref, two_ref)

    @pl.when(core != 0)
    def _():
        unpack(other_ref, one_ref)
        unpack(own_ref, two_ref)


def call(kernel, outs, *args, smem=0, scratch=()):
    specs = [
        pl.BlockSpec(memory_space=pltpu.SMEM if at < smem else pltpu.VMEM) for at in range(len(args))
    ]
    shapes = tuple(jax.ShapeDtypeStruct(shape, dtype) for shape, dtype in outs)
    result = pl.pallas_call(
        kernel,
        out_shape=shapes,
        in_specs=specs,
        out_specs=tuple(pl.BlockSpec(memory_space=pltpu.VMEM) for _ in shapes),
        scratch_shapes=list(scratch),
        compiler_params=pltpu.CompilerParams(vmem_limit_bytes=40 * 1024 * 1024),
    )(*args)
    return result


def to_all(x):
    return lax.all_to_all(x, AXES, 0, 0)


def swap_core(x):
    size = lax.axis_size("gy")
    return lax.ppermute(x, "gy", [(i, i ^ 1) for i in range(size)])


def on_device(
    features, kernel_map, send_rows, counts, weight_one, weight_two,
    first_norm_scale, first_norm_bias, second_norm_scale, second_norm_bias, cotangent,
):
    channels, rows = features.shape
    offsets = kernel_map.shape[0]
    width = send_rows.shape[1]
    grid = (lax.axis_size("gx"), lax.axis_size("gy"))
    devices = grid[0] * grid[1]
    flat = offsets * channels
    table = rows + 8 * width
    piece = -(-21 * channels // (devices * 16)) * 16
    packed = piece * devices
    full = (channels, rows)
    square = (LANES, LANES)
    one_flat = weight_one.reshape(flat, channels)
    two_flat = weight_two.reshape(flat, channels)
    scale_one, bias_one, scale_two, bias_two = [
        v.reshape(1, channels)
        for v in (first_norm_scale, first_norm_bias, second_norm_scale, second_norm_bias)
    ]

    buf, start, pick, place = call(
        functools.partial(open_kernel, grid),
        [((devices, width, LANES), BF16), (full, BF16), (square, BF16), (square, BF16)],
        counts, features, send_rows, smem=1,
    )
    buf = to_all(buf)
    hot, one_t, two_t = call(
        prepare_kernel,
        [((table, offsets * LANES), BF16), ((channels, flat), BF16), ((channels, flat), BF16)],
        kernel_map, one_flat, two_flat,
    )
    buf, hidden_one, taken_zero, flag = call(
        functools.partial(first_kernel, grid),
        [((devices, width, LANES), BF16), (full, F32), ((flat, LANES), BF16), (square, F32)],
        counts, buf, start, hot, one_t, place, smem=1,
    )
    buf = to_all(buf)
    buf, hidden_two, taken_one, norm_one, slope_one, halo_slope, halo_cross, const_one = call(
        functools.partial(second_kernel, grid),
        [
            ((devices, 2, LANES), F32), (full, F32), ((flat, LANES), BF16), (full, F32), (full, F32),
            (square, F32), (square, F32), ((8, LANES), F32),
        ],
        counts, buf, hidden_one, flag, scale_one, bias_one, hot, two_t,
        smem=1, scratch=[pltpu.VMEM((devices, LANES), F32)],
    )
    buf = to_all(buf)
    buf, output, norm_two, grad_sum, const_two = call(
        third_kernel,
        [((devices, 2, LANES), F32), (full, BF16), (full, F32), (full, F32), ((8, LANES), F32)],
        counts, buf, hidden_two, start, cotangent, scale_two, bias_two, smem=1,
    )
    buf = to_all(buf)
    buf, grad_two, table_two, sums_two = call(
        functools.partial(fourth_kernel, grid),
        [((devices, width, LANES), BF16), (full, BF16), (full, F32), ((2, LANES), F32)],
        counts, buf, norm_two, grad_sum, const_two, two_flat, hot, norm_one, slope_one, halo_slope, halo_cross,
        smem=1,
    )
    buf = to_all(buf)
    (packed_two,) = call(weight_two_kernel, [((packed, LANES), BF16)], taken_one, grad_two)
    grad_one, give, keep, grad_norms = call(
        functools.partial(fifth_kernel, grid),
        [(full, BF16), ((packed, LANES), BF16), ((packed, LANES), BF16), ((4, channels), F32)],
        counts, buf, table_two, place, norm_one, slope_one, const_one, sums_two, taken_zero, packed_two,
        smem=1,
    )
    got = swap_core(give)
    table_one, halo_one = call(
        back_kernel, [(full, F32), (square, BF16)], grad_one, one_flat, hot
    )
    (buf,) = call(
        functools.partial(sixth_kernel, grid, width),
        [((devices, width + piece, LANES), BF16)],
        halo_one, keep, got,
    )
    buf = to_all(buf)
    buf, grad_features = call(
        functools.partial(seventh_kernel, grid, width),
        [((devices, piece, LANES), BF16), (full, BF16)],
        counts, buf, table_one, place, grad_sum, smem=1,
    )
    own = to_all(buf).reshape(packed, LANES)
    other = swap_core(own)
    grad_weight_one, grad_weight_two = call(
        last_kernel,
        [(weight_one.shape, F32), (weight_two.shape, F32)],
        own, other,
    )
    return (output, grad_features, grad_weight_one, grad_weight_two, grad_norms)


def solution(mesh):
    return jax.shard_map(
        on_device,
        mesh=mesh,
        in_specs=(
            P(None, ("gx", "gy")),
            P(None, ("gx", "gy")),
            P(None, ("gx", "gy")),
            P(("gx", "gy")),
            P(),
            P(),
            P(),
            P(),
            P(),
            P(),
            P(None, ("gx", "gy")),
        ),
        out_specs=(P(None, ("gx", "gy")), P(None, ("gx", "gy")), P(), P(), P()),
        check_vma=False,
    )
```

time: 530 us -> 113 us (0.21)
  starting transfers between devices: 130 us -> 10.1 us
  blocking collectives: 169 us -> 66.4 us
  waiting for transfers between devices: 106 us -> 13.7 us
  other arithmetic: 57.2 us -> 0 us
  local copies, waits for them, and re-layouts: 38.3 us -> 8.18 us
  between operations: 16.1 us -> 1.41 us
  Pallas kernels: 0 us -> 13.1 us
  matrix products: 9.74 us -> 0 us
    psum x4 -> x0, blocking collectives: 169 us -> none  [the longest x2 86.4 us: apply_batch_norm(): lax.psum((jnp.sum(masked, axis=1), jnp.sum(masked * pre_norm, axis=1), jn...]
    ppermute x48 -> x2, starting transfers between devices: 130 us -> 0.23 us  [swap_core(): return lax.ppermute(x, 'gy', [(i, i ^ 1) for i in range(size)])]
    psum x1 -> x0, waiting for transfers between devices: 101 us -> none  [on_device(): lax.psum((grad_weight_one, grad_weight_two), ('gx', 'gy'))]
    all_to_all x0 -> x5, blocking collectives: none -> 66.4 us  [to_all(): return lax.all_to_all(x, AXES, 0, 0)]
    scatter-add x4 -> x0, other arithmetic: 42.9 us -> none  [the longest x2 40.1 us: spread_back(): table = jnp.zeros((channels, table_len), jnp.float32).at[:, kernel_map.re...]
    gather x18 -> x0, local copies, waits for them, and re-layouts: 23.5 us -> none  [the longest x2 14.3 us: convolve(): jnp.take(extended, kernel_map.reshape(-1), axis=1)]
    pallas_call x0 -> x12, Pallas kernels: none -> 13.1 us  [call(): pl.pallas_call(kernel, out_shape=shapes, in_specs=specs, out_specs=tuple(...]
    all_to_all x0 -> x2, waiting for transfers between devices: none -> 11.2 us  [to_all(): return lax.all_to_all(x, AXES, 0, 0)]
  transfers between devices with their start and end apart: 49 -> 4, of which waited for: 5 -> 4; matrix products, arithmetic and copies ran while one was open for 3% -> 0% of each run, Pallas kernels for 0% -> 2%
where the time goes in v1:
time: 113 us
  blocking collectives  66.4 us (59%)
  waiting for transfers between devices  13.7 us (12%)
  Pallas kernels  13.1 us (12%)
  starting transfers between devices  10.1 us (9%)
  local copies, waits for them, and re-layouts  8.18 us (7%)
  between operations  1.41 us (1%)
    all_to_all x5, blocking collectives, to_all(): return lax.all_to_all(x, AXES, 0, 0)  66.4 us
    pallas_call x12, Pallas kernels, call(): pl.pallas_call(kernel, out_shape=shapes, in_specs=specs, out_specs=tuple(...  13.1 us
    all_to_all x2, waiting for transfers between devices, to_all(): return lax.all_to_all(x, AXES, 0, 0)  11.2 us
    all_to_all x2, starting transfers between devices, to_all(): return lax.all_to_all(x, AXES, 0, 0)  9.87 us
    unnamed x32, local copies, waits for them, and re-layouts  8.18 us
    ppermute x2, waiting for transfers between devices, swap_core(): return lax.ppermute(x, 'gy', [(i, i ^ 1) for i in range(size)])  2.57 us
  transfers between devices with their start and end apart: 4, of which 4 were waited for; matrix products, arithmetic and copies ran while one was open for 0% of the time, Pallas kernels for 2%

profile of v1, /device:TPU:0, one launch (start us, length us, event | category | flops | bytes accessed | tf_op | source)
XLA Modules:
  0.0 112.9 jit_solution(14954368600920232864)
XLA Ops:
  2.7 1.0 shard_map.146
  3.7 7.3 %all-to-all-start = ((bf16[32,16,128]{2,1,0:T(8,128)(2,1)}), bf16[32,16,128]{2,1,0:T(8,128)(2,1)S(1)}, u32[]{:S(2)}, u32[]{:S(2)}) async-start(bf16[32,16,128]{2,1,0:T(8,128)(2,1)} %get-tuple-element.42), calls=%async_computation | async-start | bytes 262144 | tf_op jit(solution)/shard_map/all_to_all | solution.py:490
  11.0 1.1 copy-done
  12.1 1.1 copy-done.2
  13.9 0.9 shard_map.147
  14.8 4.4 %all-to-all-done.buf_ref = bf16[32,16,128]{2,1,0:T(8,128)(2,1)S(1)} async-done(((bf16[32,16,128]{2,1,0:T(8,128)(2,1)}), bf16[32,16,128]{2,1,0:T(8,128)(2,1)S(1)}, u32[]{:S(2)}, u32[]{:S(2)}) %all-to-all-start) | async-done | bytes 131104 | tf_op jit(solution)/shard_map/all_to_all | solution.py:490
  19.2 1.1 shard_map.148
  21.2 10.0 %all_to_all.35.buf_ref = bf16[32,16,128]{2,1,0:T(8,128)(2,1)S(1)} all-to-all(bf16[32,16,128]{2,1,0:T(8,128)(2,1)S(1)} %get-tuple-element.47), channel_id=1, replica_groups=mesh['gx'=8,'gy'=4] {'gx','gy'}, dimensions={0} | all-to-all | bytes 262144 | tf_op jit(solution)/shard_map/all_to_all | solution.py:490
  31.2 1.3 %shard_map.149 = (f32[32,2,128]{2,1,0:T(2,128)S(1)}, f32[96,128]{1,0:T(8,128)S(1)}, bf16[2592,128]{1,0:T(8,128)(2,1)S(1)}, f32[96,128]{1,0:T(8,128)S(1)}, f32[96...) custom-call(s32[1]{0:T(128)S(6)} %copy.16.counts_ref, ...), custom_call_target="tpu_custom_call" | custom-call | tf_op jit(solution)/shard_map/pallas_call | solution.py:478
  33.4 9.0 %all_to_all.36.buf_ref = f32[32,2,128]{2,1,0:T(2,128)S(1)} all-to-all(f32[32,2,128]{2,1,0:T(2,128)S(1)} %get-tuple-element.51), channel_id=1, replica_groups=mesh['gx'=8,'gy'=4] {'gx','gy'}, dimensions={0} | all-to-all | bytes 65536 | tf_op jit(solution)/shard_map/all_to_all | solution.py:490
  42.4 1.0 shard_map.150
  43.4 8.9 %all_to_all.37.buf_ref = f32[32,2,128]{2,1,0:T(2,128)S(1)} all-to-all(f32[32,2,128]{2,1,0:T(2,128)S(1)} %get-tuple-element.54), channel_id=1, replica_groups=mesh['gx'=8,'gy'=4] {'gx','gy'}, dimensions={0} | all-to-all | bytes 65536 | tf_op jit(solution)/shard_map/all_to_all | solution.py:490
  52.3 2.1 %shard_map.151 = (bf16[32,16,128]{2,1,0:T(8,128)(2,1)}, bf16[96,128]{1,0:T(8,128)(2,1)S(1)}, f32[96,128]{1,0:T(8,128)S(1)}, f32[2,128]{1,0:T(2,128)S(1)}) custom-call(s32[1]{0:T(128)S(6)} %copy.16.counts_ref, f32[32,2,128]{2,1,0:T(2,128)S(1)} %all_to_all.37.buf_ref, f32[96,128]{1,0:T(8,128)S(1)} %get-tuple-element.55.norm_ref, ...), custom_call_target="tpu_custom_call" | custom-call | tf_op jit(solution)/shard_map/pallas_call | solution.py:478
  54.4 2.6 %all-to-all-start.4 = ((bf16[32,16,128]{2,1,0:T(8,128)(2,1)}), bf16[32,16,128]{2,1,0:T(8,128)(2,1)S(1)}, u32[]{:S(2)}, u32[]{:S(2)}) async-start(bf16[32,16,128]{2,1,0:T(8,128)(2,1)} %get-tuple-element.62), calls=%async_computation.4 | async-start | bytes 262144 | tf_op jit(solution)/shard_map/all_to_all | solution.py:490
  57.0 1.1 copy-done.7
  58.5 6.7 %all-to-all-done.4.buf_ref = bf16[32,16,128]{2,1,0:T(8,128)(2,1)S(1)} async-done(((bf16[32,16,128]{2,1,0:T(8,128)(2,1)}), bf16[32,16,128]{2,1,0:T(8,128)(2,1)S(1)}, u32[]{:S(2)}, u32[]{:S(2)}) %all-to-all-start.4) | async-done | bytes 131104 | tf_op jit(solution)/shard_map/all_to_all | solution.py:490
  65.2 1.1 copy-done.5
  66.3 1.5 %shard_map.153 = (bf16[96,128]{1,0:T(8,128)(2,1)S(1)}, bf16[2048,128]{1,0:T(8,128)(2,1)S(1)}, bf16[2048,128]{1,0:T(8,128)(2,1)S(1)}, f32[4,96]{1,0:T(4,128)}) custom-call(s32[1]{0:T(128)S(6)} %copy.16.counts_ref, bf16[32,16,128]{2,1,0:T(8,128)(2,1)S(1)} %all-to-all-done.4.buf_ref, f32[96,128]{1,0:T(8,128)S(1)} %get-tuple-element.63.table_ref, ...), custom_call_target="tpu_custom_call" | custom-call | tf_op jit(solution)/shard_map/pallas_call | solution.py:478
  68.0 1.0 shard_map.154
  69.8 19.6 %all_to_all.38.buf_ref = bf16[32,80,128]{2,1,0:T(8,128)(2,1)S(1)} all-to-all(bf16[32,80,128]{2,1,0:T(8,128)(2,1)S(1)} %shard_map.155), channel_id=1, replica_groups=mesh['gx'=8,'gy'=4] {'gx','gy'}, dimensions={0} | all-to-all | bytes 1310720 | tf_op jit(solution)/shard_map/all_to_all | solution.py:490
  89.4 0.9 shard_map.156
  90.3 18.8 %all_to_all.39 = bf16[32,64,128]{2,1,0:T(8,128)(2,1)S(1)} all-to-all(bf16[32,64,128]{2,1,0:T(8,128)(2,1)S(1)} %get-tuple-element.75), channel_id=1, replica_groups=mesh['gx'=8,'gy'=4] {'gx','gy'}, dimensions={0} | all-to-all | bytes 1048576 | tf_op jit(solution)/shard_map/all_to_all | solution.py:490
  109.1 1.9 %collective-permute-done.1.other_ref = bf16[2048,128]{1,0:T(8,128)(2,1)S(1)} collective-permute-done((bf16[2048,128]{1,0:T(8,128)(2,1)S(1)}, bf16[2048,128]{1,0:T(8,128)(2,1)S(1)}, u32[]{:S(2)}, u32[]{:S(2)}) %collective-permute-start.1) | collective-permute-done | bytes 524320 | tf_op jit(solution)/shard_map/ppermute | solution.py:495
  111.0 1.8 %shard_map.157 = (f32[27,96,96]{2,1,0:T(8,128)}, f32[27,96,96]{2,1,0:T(8,128)}) custom-call(bf16[2048,128]{1,0:T(8,128)(2,1)S(1)} %bitcast.12, bf16[2048,128]{1,0:T(8,128)(2,1)S(1)} %collective-permute-done.1.other_ref), custom_call_target="tpu_custom_call" | custom-call | tf_op jit(solution)/shard_map/pallas_call | solution.py:478
  (33 shorter events, 5.3 us)
Async XLA Ops:
  1.3 0.7 copy-start.9
  2.0 0.7 copy-start.11
  3.7 15.5 %all-to-all-start = ((bf16[32,16,128]{2,1,0:T(8,128)(2,1)}), bf16[32,16,128]{2,1,0:T(8,128)(2,1)S(1)}, u32[]{:S(2)}, u32[]{:S(2)}) async-start(bf16[32,16,128]{2,1,0:T(8,128)(2,1)} %get-tuple-element.42), calls=%async_computation | async-start | bytes 262144 | tf_op jit(solution)/shard_map/all_to_all | solution.py:490
  11.0 1.1 copy-start
  12.1 1.1 copy-start.2
  13.2 0.7 copy-start.10
  19.2 12.0 %copy-start.12 = (f32[96]{0:T(128)S(1)}, f32[96]{0:T(128)}, u32[]{:S(2)}) copy-start(f32[96]{0:T(128)} %param.17) | copy-start | bytes 1156
  19.2 12.0 %copy-start.13 = (f32[96]{0:T(128)S(1)}, f32[96]{0:T(128)}, u32[]{:S(2)}) copy-start(f32[96]{0:T(128)} %param.18) | copy-start | bytes 1156
  20.4 0.8 copy-start.4
  31.2 11.2 %copy-start.8 = (bf16[96,128]{1,0:T(8,128)(2,1)S(1)}, bf16[96,128]{1,0:T(8,128)(2,1)}, u32[]{:S(2)}) copy-start(bf16[96,128]{1,0:T(8,128)(2,1)} %cotangent_ref.1) | copy-start | bytes 73732
  31.2 11.2 %copy-start.14 = (f32[96]{0:T(128)S(1)}, f32[96]{0:T(128)}, u32[]{:S(2)}) copy-start(f32[96]{0:T(128)} %param.19) | copy-start | bytes 1156
  31.2 11.2 %copy-start.15 = (f32[96]{0:T(128)S(1)}, f32[96]{0:T(128)}, u32[]{:S(2)}) copy-start(f32[96]{0:T(128)} %param.20) | copy-start | bytes 1156
  31.2 21.1 %copy-start.1 = (bf16[27,96,96]{2,1,0:T(8,128)(2,1)S(1)}, bf16[27,96,96]{2,1,0:T(8,128)(2,1)}, u32[]{:S(2)}) copy-start(bf16[27,96,96]{2,1,0:T(8,128)(2,1)} %param.16) | copy-start | bytes 1492996
  32.5 0.8 copy-start.6
  54.4 10.8 %all-to-all-start.4 = ((bf16[32,16,128]{2,1,0:T(8,128)(2,1)}), bf16[32,16,128]{2,1,0:T(8,128)(2,1)S(1)}, u32[]{:S(2)}, u32[]{:S(2)}) async-start(bf16[32,16,128]{2,1,0:T(8,128)(2,1)} %get-tuple-element.62), calls=%async_computation.4 | async-start | bytes 262144 | tf_op jit(solution)/shard_map/all_to_all | solution.py:490
  56.9 1.1 copy-start.7
  58.0 9.9 %copy-start.3 = (bf16[27,96,96]{2,1,0:T(8,128)(2,1)S(1)}, bf16[27,96,96]{2,1,0:T(8,128)(2,1)}, u32[]{:S(2)}) copy-start(bf16[27,96,96]{2,1,0:T(8,128)(2,1)} %param.15) | copy-start | bytes 1492996
  65.2 1.1 copy-start.5
  67.7 1.9 %collective-permute-start = (bf16[2048,128]{1,0:T(8,128)(2,1)S(1)}, bf16[2048,128]{1,0:T(8,128)(2,1)S(1)}, u32[]{:S(2)}, u32[]{:S(2)}) collective-permute-start(bf16[2048,128]{1,0:T(8,128)(2,1)S(1)} %get-tuple-element.72), channel_id=1, source_target_pairs={{0,1},{1,0},{2,3},{3,2},{4,5},{5,4},{6,7},{7,6},{8,9},{9,8},{10,11... | collective-permute-start | bytes 1572872 | tf_op jit(solution)/shard_map/ppermute | solution.py:495
  109.1 1.9 %collective-permute-start.1 = (bf16[2048,128]{1,0:T(8,128)(2,1)S(1)}, bf16[2048,128]{1,0:T(8,128)(2,1)S(1)}, u32[]{:S(2)}, u32[]{:S(2)}) collective-permute-start(bf16[2048,128]{1,0:T(8,128)(2,1)S(1)} %bitcast.11), channel_id=1, source_target_pairs={{0,1},{1,0},{2,3},{3,2},{4,5},{5,4},{6,7},{7,6},{8,9},{9,8},{10,11... | collective-permute-start | bytes 1572872 | tf_op jit(solution)/shard_map/ppermute | solution.py:495

commit v2 on v1

--- a/solution.py
+++ b/solution.py
@@ -133,16 +133,24 @@
     return (iota((rows, LANES), 1) < counts_ref[0]).astype(F32)
 
 
-def open_kernel(grid, counts_ref, features_ref, send_ref, buf_ref, start_ref, pick_ref, place_ref):
+def open_kernel(
+    grid, counts_ref, features_hbm, send_hbm, buf_ref, start_ref, place_ref, features_ref, send_ref, sems
+):
+    copies = [
+        pltpu.make_async_copy(features_hbm, features_ref, sems.at[0]),
+        pltpu.make_async_copy(send_hbm, send_ref, sems.at[1]),
+    ]
+    for copy in copies:
+        copy.start()
+    for copy in copies:
+        copy.wait()
     width = send_ref.shape[1]
     send = send_ref[...].astype(F32).astype(BF16)
     spread = jnp.where(iota((width, LANES), 1) % width == iota((width, LANES), 0), 1.0, 0.0).astype(BF16)
     wide = nn(send, spread)
     wide = jnp.where(iota(wide.shape, 1) // width == iota(wide.shape, 0), wide, 0.0)
     row = jnp.sum(wide, axis=0, keepdims=True)
-    pick = jnp.where(row == iota((LANES, LANES), 0).astype(F32), 1.0, 0.0)
-    pick_ref[...] = pick.astype(BF16)
-    place = pick.T.astype(BF16)
+    place = jnp.where(row == iota((LANES, LANES), 0).astype(F32), 1.0, 0.0).T.astype(BF16)
     place_ref[...] = place
     valid = valid_lanes(counts_ref)
     start = features_ref[...].astype(F32) * valid
@@ -164,18 +172,24 @@
     two_t_ref[...] = nt(unit, two_ref[...]).astype(BF16)
 
 
+def gather(tables, hot_ref, taken_refs):
+    channels = tables[0].shape[0]
+    taken = nn(jnp.concatenate(tables, axis=0), hot_ref[...]).astype(BF16)
+    for at, ref in enumerate(taken_refs):
+        for k in range(hot_ref.shape[1] // LANES):
+            ref[k * channels : (k + 1) * channels, :] = taken[
+                at * channels : (at + 1) * channels, k * LANES : (k + 1) * LANES
+            ]
+
+
 def gather_convolve(table, hot_ref, weight_t_ref, taken_ref):
-    channels = table.shape[0]
-    taken = nn(table, hot_ref[...]).astype(BF16)
-    offsets = hot_ref.shape[1] // LANES
-    for k in range(offsets):
-        taken_ref[k * channels : (k + 1) * channels, :] = taken[:, k * LANES : (k + 1) * LANES]
+    gather([table], hot_ref, [taken_ref])
     return nn(weight_t_ref[...], taken_ref[...])
 
 
 def first_kernel(
     grid, counts_ref, buf_ref, start_ref, hot_ref, weight_ref, place_ref,
-    out_buf_ref, hidden_ref, taken_ref, flag_ref,
+    out_buf_ref, hidden_ref, table_ref, flag_ref, taken_ref,
 ):
     width = buf_ref.shape[1]
     channels = start_ref.shape[0]
@@ -183,6 +197,7 @@
     flag_ref[...] = jnp.broadcast_to(halo_rows[:, 96:97].astype(F32), (LANES, LANES))
     halo = nt(eye(LANES), halo_rows)[:channels].astype(BF16)
     table = jnp.concatenate([start_ref[...], halo], axis=1)
+    table_ref[...] = table
     hidden = gather_convolve(table, hot_ref, weight_ref, taken_ref)
     hidden_ref[...] = hidden
     valid = valid_lanes(counts_ref)
@@ -199,8 +214,8 @@
 
 def second_kernel(
     grid, counts_ref, buf_ref, hidden_ref, flag_ref, scale_ref, bias_ref, hot_ref, weight_ref,
-    out_buf_ref, hidden_two_ref, taken_ref, norm_ref, slope_ref, halo_slope_ref, halo_cross_ref,
-    const_ref, mean_ref,
+    out_buf_ref, hidden_two_ref, table_ref, norm_ref, slope_ref, halo_slope_ref, halo_cross_ref,
+    const_ref, mean_ref, taken_ref,
 ):
     width = buf_ref.shape[1]
     channels = hidden_ref.shape[0]
@@ -246,7 +261,9 @@
     halo_cross_ref[...] = halo_slope * halo_normal
     halo_act = nt(eye(LANES), (halo_linear * halo_sig * flag).astype(BF16))[:channels].astype(BF16)
 
-    hidden = gather_convolve(jnp.concatenate([act, halo_act], axis=1), hot_ref, weight_ref, taken_ref)
+    table = jnp.concatenate([act, halo_act], axis=1)
+    table_ref[...] = table
+    hidden = gather_convolve(table, hot_ref, weight_ref, taken_ref)
     hidden_two_ref[...] = hidden
     count = counts_ref[0].astype(F32)
     sums_two = jnp.sum(hidden * valid, axis=1, keepdims=True)
@@ -359,21 +376,10 @@
         put(18 + e, last[e * channels : (e + 1) * channels])
 
 
-def weight_two_kernel(taken_ref, grad_ref, out_ref):
-    channels = grad_ref.shape[0]
-
-    def put(block, value):
-        out_ref[block * channels : (block + 1) * channels, :] = value.astype(BF16)
-
-    packed_weight_grad(taken_ref, grad_ref[...], put)
-    tail = out_ref.shape[0] - 21 * channels
-    if tail:
-        out_ref[21 * channels :, :] = jnp.zeros((tail, LANES), BF16)
-
-
 def fifth_kernel(
-    grid, counts_ref, buf_ref, table_ref, place_ref, norm_ref, slope_ref, const_ref, sums_two_ref, taken_ref,
-    packed_two_ref, grad_one_ref, give_ref, keep_ref, sums_ref,
+    grid, counts_ref, buf_ref, table_ref, place_ref, norm_ref, slope_ref, const_ref, sums_two_ref,
+    table_zero_ref, table_act_ref, hot_ref, grad_two_ref,
+    grad_one_ref, give_ref, keep_ref, sums_ref, taken_zero_ref, taken_act_ref,
 ):
     width = buf_ref.shape[1]
     channels = norm_ref.shape[0]
@@ -387,28 +393,27 @@
     back = table_ref[...] + nn(arrived, place_ref[...])
     grad = row_gradient(back * slope_ref[...], norm_ref[...], const_ref[...], dgain, dbias, valid)
     grad_one_ref[...] = grad
+    gather([table_zero_ref[...], table_act_ref[...]], hot_ref, [taken_zero_ref, taken_act_ref])
     core = lax.axis_index("gy") % 2
     used = 21 * channels
 
+    def store(taken_ref, row_grad, ref):
+        def put(block, value):
+            ref[block * channels : (block + 1) * channels, :] = value.astype(ref.dtype)
+
+        packed_weight_grad(taken_ref, row_grad, put)
+        if ref.shape[0] > used:
+            ref[used:, :] = jnp.zeros((ref.shape[0] - used, LANES), ref.dtype)
+
     @pl.when(core == 0)
     def _():
-        def put(block, value):
-            keep_ref[block * channels : (block + 1) * channels, :] = value.astype(BF16)
-
-        packed_weight_grad(taken_ref, grad, put)
-        give_ref[...] = packed_two_ref[...]
-        if keep_ref.shape[0] > used:
-            keep_ref[used:, :] = jnp.zeros((keep_ref.shape[0] - used, LANES), BF16)
+        store(taken_zero_ref, grad, keep_ref)
+        store(taken_act_ref, grad_two_ref[...], give_ref)
 
     @pl.when(core != 0)
     def _():
-        def put(block, value):
-            give_ref[block * channels : (block + 1) * channels, :] = value.astype(BF16)
-
-        packed_weight_grad(taken_ref, grad, put)
-        keep_ref[...] = packed_two_ref[...]
-        if keep_ref.shape[0] > used:
-            give_ref[used:, :] = jnp.zeros((keep_ref.shape[0] - used, LANES), BF16)
+        store(taken_zero_ref, grad, give_ref)
+        store(taken_act_ref, grad_two_ref[...], keep_ref)
 
 
 def back_kernel(grad_ref, weight_ref, hot_ref, table_ref, halo_ref):
@@ -420,7 +425,7 @@
 def sixth_kernel(grid, width, halo_ref, keep_ref, got_ref, out_buf_ref):
     devices, rows = out_buf_ref.shape[0], out_buf_ref.shape[1] - width
     put_blocks(out_buf_ref, halo_ref[...], grid, -1, width)
-    total = (keep_ref[...].astype(F32) + got_ref[...].astype(F32)).astype(BF16)
+    total = (keep_ref[...] + got_ref[...].astype(F32)).astype(BF16)
     out_buf_ref[:, width:, :] = total.reshape(devices, rows, LANES)
 
 
@@ -441,49 +446,78 @@
         out_buf_ref[d] = pieces[d % 2]
 
 
-def last_kernel(own_ref, other_ref, one_ref, two_ref):
+def unpack(src_ref, out_hbm, block_ref, sems):
+    channels = block_ref.shape[1]
+    lane = iota((channels, LANES), 1)
+    copies = []
+
+    def send(first, count):
+        part = pl.ds(first, count)
+        copies.append(pltpu.make_async_copy(block_ref.at[part], out_hbm.at[part], sems.at[len(copies)]))
+        copies[-1].start()
+
+    for e in range(7):
+        extra = jnp.zeros((channels, LANES), F32)
+        for part in range(3):
+            block = 3 * e + part
+            value = src_ref[block * channels : (block + 1) * channels, :].astype(F32)
+            block_ref[block] = value[:, :channels]
+            if e < 6:
+                moved = pltpu.roll(value, 32 * (part + 1), 1)
+                extra = jnp.where(lane // 32 == part, moved, extra)
+        send(3 * e, 3)
+        if e < 6:
+            block_ref[21 + e] = extra[:, :channels]
+            send(21 + e, 1)
+    for copy in copies:
+        copy.wait()
+
+
+def own_kernel(own_ref, small_in, more_in, sums_in, one_hbm, two_hbm, small_out, more_out, sums_out, block_ref, sems):
     core = lax.axis_index("gy") % 2
-    channels = one_ref.shape[1]
-
-    def unpack(src_ref, dst_ref):
-        lane = iota((channels, LANES), 1)
-        for e in range(7):
-            extra = jnp.zeros((channels, LANES), F32)
-            for part in range(3):
-                block = 3 * e + part
-                value = src_ref[block * channels : (block + 1) * channels, :].astype(F32)
-                dst_ref[block] = value[:, :channels]
-                if e < 6:
-                    moved = pltpu.roll(value, 32 * (part + 1), 1)
-                    extra = jnp.where(lane // 32 == part, moved, extra)
-            if e < 6:
-                dst_ref[21 + e] = extra[:, :channels]
+    small_out[...] = small_in[...]
+    more_out[...] = more_in[...]
+    sums_out[...] = sums_in[...]
 
     @pl.when(core == 0)
     def _():
-        unpack(own_ref, one_ref)
-        unpack(other_ref, two_ref)
+        unpack(own_ref, one_hbm, block_ref, sems)
 
     @pl.when(core != 0)
     def _():
-        unpack(other_ref, one_ref)
-        unpack(own_ref, two_ref)
-
-
-def call(kernel, outs, *args, smem=0, scratch=()):
-    specs = [
-        pl.BlockSpec(memory_space=pltpu.SMEM if at < smem else pltpu.VMEM) for at in range(len(args))
-    ]
+        unpack(own_ref, two_hbm, block_ref, sems)
+
+
+def other_kernel(other_ref, one_in, two_in, one_hbm, two_hbm, block_ref, sems):
+    core = lax.axis_index("gy") % 2
+
+    @pl.when(core == 0)
+    def _():
+        unpack(other_ref, two_hbm, block_ref, sems)
+
+    @pl.when(core != 0)
+    def _():
+        unpack(other_ref, one_hbm, block_ref, sems)
+
+
+def call(kernel, outs, *args, smem=0, scratch=(), hbm=(), hbm_outs=(), aliases=None):
+    def space(at):
+        if at in hbm:
+            return pltpu.HBM
+        return pltpu.SMEM if at < smem else pltpu.VMEM
+
     shapes = tuple(jax.ShapeDtypeStruct(shape, dtype) for shape, dtype in outs)
-    result = pl.pallas_call(
+    return pl.pallas_call(
         kernel,
         out_shape=shapes,
-        in_specs=specs,
-        out_specs=tuple(pl.BlockSpec(memory_space=pltpu.VMEM) for _ in shapes),
+        in_specs=[pl.BlockSpec(memory_space=space(at)) for at in range(len(args))],
+        out_specs=tuple(
+            pl.BlockSpec(memory_space=pltpu.HBM if at in hbm_outs else pltpu.VMEM) for at in range(len(shapes))
+        ),
         scratch_shapes=list(scratch),
+        input_output_aliases=aliases or {},
         compiler_params=pltpu.CompilerParams(vmem_limit_bytes=40 * 1024 * 1024),
     )(*args)
-    return result
 
 
 def to_all(x):
@@ -517,10 +551,15 @@
         for v in (first_norm_scale, first_norm_bias, second_norm_scale, second_norm_bias)
     ]
 
-    buf, start, pick, place = call(
+    taken = pltpu.VMEM((flat, LANES), BF16)
+    wide = ((channels, table), BF16)
+    buf, start, place = call(
         functools.partial(open_kernel, grid),
-        [((devices, width, LANES), BF16), (full, BF16), (square, BF16), (square, BF16)],
-        counts, features, send_rows, smem=1,
+        [((devices, width, LANES), BF16), (full, BF16), (square, BF16)],
+        counts, features, send_rows, smem=1, hbm=(1, 2),
+        scratch=[
+            pltpu.VMEM(full, BF16), pltpu.VMEM(send_rows.shape, jnp.int32), pltpu.SemaphoreType.DMA((2,)),
+        ],
     )
     buf = to_all(buf)
     hot, one_t, two_t = call(
@@ -528,20 +567,20 @@
         [((table, offsets * LANES), BF16), ((channels, flat), BF16), ((channels, flat), BF16)],
         kernel_map, one_flat, two_flat,
     )
-    buf, hidden_one, taken_zero, flag = call(
+    buf, hidden_one, table_zero, flag = call(
         functools.partial(first_kernel, grid),
-        [((devices, width, LANES), BF16), (full, F32), ((flat, LANES), BF16), (square, F32)],
-        counts, buf, start, hot, one_t, place, smem=1,
+        [((devices, width, LANES), BF16), (full, F32), wide, (square, F32)],
+        counts, buf, start, hot, one_t, place, smem=1, scratch=[taken],
     )
     buf = to_all(buf)
-    buf, hidden_two, taken_one, norm_one, slope_one, halo_slope, halo_cross, const_one = call(
+    buf, hidden_two, table_act, norm_one, slope_one, halo_slope, halo_cross, const_one = call(
         functools.partial(second_kernel, grid),
         [
-            ((devices, 2, LANES), F32), (full, F32), ((flat, LANES), BF16), (full, F32), (full, F32),
+            ((devices, 2, LANES), F32), (full, F32), wide, (full, F32), (full, F32),
             (square, F32), (square, F32), ((8, LANES), F32),
         ],
         counts, buf, hidden_one, flag, scale_one, bias_one, hot, two_t,
-        smem=1, scratch=[pltpu.VMEM((devices, LANES), F32)],
+        smem=1, scratch=[pltpu.VMEM((devices, LANES), F32), taken],
     )
     buf = to_all(buf)
     buf, output, norm_two, grad_sum, const_two = call(
@@ -557,12 +596,11 @@
         smem=1,
     )
     buf = to_all(buf)
-    (packed_two,) = call(weight_two_kernel, [((packed, LANES), BF16)], taken_one, grad_two)
     grad_one, give, keep, grad_norms = call(
         functools.partial(fifth_kernel, grid),
-        [(full, BF16), ((packed, LANES), BF16), ((packed, LANES), BF16), ((4, channels), F32)],
-        counts, buf, table_two, place, norm_one, slope_one, const_one, sums_two, taken_zero, packed_two,
-        smem=1,
+        [(full, BF16), ((packed, LANES), BF16), ((packed, LANES), F32), ((4, channels), F32)],
+        counts, buf, table_two, place, norm_one, slope_one, const_one, sums_two,
+        table_zero, table_act, hot, grad_two, smem=1, scratch=[taken, taken],
     )
     got = swap_core(give)
     table_one, halo_one = call(
@@ -581,10 +619,16 @@
     )
     own = to_all(buf).reshape(packed, LANES)
     other = swap_core(own)
+    weights = [(weight_one.shape, F32), (weight_two.shape, F32)]
+    blocks = [pltpu.VMEM(weight_one.shape, F32), pltpu.SemaphoreType.DMA((13,))]
+    grad_weight_one, grad_weight_two, output, grad_features, grad_norms = call(
+        own_kernel,
+        weights + [(full, BF16), (full, BF16), ((4, channels), F32)],
+        own, output, grad_features, grad_norms, hbm_outs=(0, 1), scratch=blocks,
+    )
     grad_weight_one, grad_weight_two = call(
-        last_kernel,
-        [(weight_one.shape, F32), (weight_two.shape, F32)],
-        own, other,
+        other_kernel, weights, other, grad_weight_one, grad_weight_two,
+        hbm=(1, 2), hbm_outs=(0, 1), scratch=blocks, aliases={1: 0, 2: 1},
     )
     return (output, grad_features, grad_weight_one, grad_weight_two, grad_norms)
 

time: 113 us -> 108 us (0.956)
  blocking collectives: 66.4 us -> 76.5 us
  waiting for transfers between devices: 13.7 us -> 5.14 us
  local copies, waits for them, and re-layouts: 8.18 us -> 4.34 us
  starting transfers between devices: 10.1 us -> 7.62 us
    all_to_all x5 -> x6, blocking collectives: 66.4 us -> 76.5 us  [to_all(): return lax.all_to_all(x, AXES, 0, 0)]
    all_to_all x2 -> x1, waiting for transfers between devices: 11.2 us -> 4.43 us  [to_all(): return lax.all_to_all(x, AXES, 0, 0)]
    unnamed x32 -> x24, local copies, waits for them, and re-layouts: 8.18 us -> 4.34 us
    all_to_all x2 -> x1, starting transfers between devices: 9.87 us -> 7.3 us  [to_all(): return lax.all_to_all(x, AXES, 0, 0)]
    ppermute x2, waiting for transfers between devices: 2.57 us -> 0.71 us  [swap_core(): return lax.ppermute(x, 'gy', [(i, i ^ 1) for i in range(size)])]
  transfers between devices with their start and end apart: 4 -> 3, of which waited for: 4 -> 3; matrix products, arithmetic and copies ran while one was open for 0% -> 0% of each run, Pallas kernels for 2% -> 3%
where the time goes in v2:
time: 108 us; the launch traced here: 107 us
  blocking collectives  76.5 us (71%)
  Pallas kernels  12.2 us (11%)
  starting transfers between devices  7.62 us (7%)
  waiting for transfers between devices  5.14 us (5%)
  local copies, waits for them, and re-layouts  4.34 us (4%)
  between operations  1.42 us (1%)
    all_to_all x6, blocking collectives, to_all(): return lax.all_to_all(x, AXES, 0, 0)  76.5 us
    pallas_call x12, Pallas kernels, call(): pl.pallas_call(kernel, out_shape=shapes, in_specs=[pl.BlockSpec(memory_sp...  12.2 us
    all_to_all x1, starting transfers between devices, to_all(): return lax.all_to_all(x, AXES, 0, 0)  7.3 us
    all_to_all x1, waiting for transfers between devices, to_all(): return lax.all_to_all(x, AXES, 0, 0)  4.43 us
    unnamed x24, local copies, waits for them, and re-layouts  4.34 us
  transfers between devices with their start and end apart: 3, of which 3 were waited for; matrix products, arithmetic and copies ran while one was open for 0% of the time, Pallas kernels for 3%

profile of v2, /device:TPU:0, one launch (start us, length us, event | category | flops | bytes accessed | tf_op | source)
XLA Modules:
  0.0 107.2 jit_solution(15477304399660230040)
XLA Ops:
  1.3 0.7 copy-done.5
  2.0 0.7 copy-done.7
  2.7 1.0 shard_map.146
  3.7 7.3 %all-to-all-start = ((bf16[32,16,128]{2,1,0:T(8,128)(2,1)}), bf16[32,16,128]{2,1,0:T(8,128)(2,1)S(1)}, u32[]{:S(2)}, u32[]{:S(2)}) async-start(bf16[32,16,128]{2,1,0:T(8,128)(2,1)} %get-tuple-element.47), calls=%async_computation | async-start | bytes 262144 | tf_op jit(solution)/shard_map/all_to_all | solution.py:524
  11.1 1.1 %copy-done = bf16[27,96,96]{2,1,0:T(8,128)(2,1)S(1)} copy-done((bf16[27,96,96]{2,1,0:T(8,128)(2,1)S(1)}, bf16[27,96,96]{2,1,0:T(8,128)(2,1)}, u32[]{:S(2)}) %copy-start) | copy-done | bytes 497688
  12.1 1.1 %copy-done.2 = bf16[27,96,96]{2,1,0:T(8,128)(2,1)S(1)} copy-done((bf16[27,96,96]{2,1,0:T(8,128)(2,1)S(1)}, bf16[27,96,96]{2,1,0:T(8,128)(2,1)}, u32[]{:S(2)}) %copy-start.2) | copy-done | bytes 497688
  13.2 0.7 copy-done.6
  14.0 0.9 shard_map.147
  14.8 4.4 %all-to-all-done.buf_ref = bf16[32,16,128]{2,1,0:T(8,128)(2,1)S(1)} async-done(((bf16[32,16,128]{2,1,0:T(8,128)(2,1)}), bf16[32,16,128]{2,1,0:T(8,128)(2,1)S(1)}, u32[]{:S(2)}, u32[]{:S(2)}) %all-to-all-start) | async-done | bytes 131104 | tf_op jit(solution)/shard_map/all_to_all | solution.py:524
  19.3 1.1 %shard_map.148 = (bf16[32,16,128]{2,1,0:T(8,128)(2,1)S(1)}, f32[96,128]{1,0:T(8,128)S(1)}, bf16[96,256]{1,0:T(8,128)(2,1)S(1)}, f32[128,128]{1,0:T(8,128)S(1)}) custom-call(s32[1]{0:T(128)S(6)} %copy.20.counts_ref, bf16[32,16,128]{2,1,0:T(8,128)(2,1)S(1)} %all-to-all-done.buf_ref, bf16[96,128]{1,0:T(8,128)(2,1)S(1)} %get-tuple-element.48.start_ref, ...), custom_call_target="tpu_custom_call" | custom-call | tf_op jit(solution)/shard_map/pallas_call | solution.py:510
  20.4 10.0 %all_to_all.35.buf_ref = bf16[32,16,128]{2,1,0:T(8,128)(2,1)S(1)} all-to-all(bf16[32,16,128]{2,1,0:T(8,128)(2,1)S(1)} %get-tuple-element.52), channel_id=1, replica_groups=mesh['gx'=8,'gy'=4] {'gx','gy'}, dimensions={0} | all-to-all | bytes 262144 | tf_op jit(solution)/shard_map/all_to_all | solution.py:524
  30.4 1.3 %shard_map.149 = (f32[32,2,128]{2,1,0:T(2,128)S(1)}, f32[96,128]{1,0:T(8,128)S(1)}, bf16[96,256]{1,0:T(8,128)(2,1)S(1)}, f32[96,128]{1,0:T(8,128)S(1)}, f32[96,1...) custom-call(s32[1]{0:T(128)S(6)} %copy.20.counts_ref, ...), custom_call_target="tpu_custom_call" | custom-call | tf_op jit(solution)/shard_map/pallas_call | solution.py:510
  31.7 9.0 %all_to_all.36.buf_ref = f32[32,2,128]{2,1,0:T(2,128)S(1)} all-to-all(f32[32,2,128]{2,1,0:T(2,128)S(1)} %get-tuple-element.56), channel_id=1, replica_groups=mesh['gx'=8,'gy'=4] {'gx','gy'}, dimensions={0} | all-to-all | bytes 65536 | tf_op jit(solution)/shard_map/all_to_all | solution.py:524
  40.7 0.5 shard_map.150
  41.2 8.9 %all_to_all.37.buf_ref = f32[32,2,128]{2,1,0:T(2,128)S(1)} all-to-all(f32[32,2,128]{2,1,0:T(2,128)S(1)} %get-tuple-element.58), channel_id=1, replica_groups=mesh['gx'=8,'gy'=4] {'gx','gy'}, dimensions={0} | all-to-all | bytes 65536 | tf_op jit(solution)/shard_map/all_to_all | solution.py:524
  50.2 1.4 %shard_map.151 = (bf16[32,16,128]{2,1,0:T(8,128)(2,1)S(1)}, bf16[96,128]{1,0:T(8,128)(2,1)S(1)}, f32[96,128]{1,0:T(8,128)S(1)}, f32[2,128]{1,0:T(2,128)S(1)}) custom-call(s32[1]{0:T(128)S(6)} %copy.20.counts_ref, f32[32,2,128]{2,1,0:T(2,128)S(1)} %all_to_all.37.buf_ref, f32[96,128]{1,0:T(8,128)S(1)} %get-tuple-element.59.norm_ref, ...), custom_call_target="tpu_custom_call" | custom-call | tf_op jit(solution)/shard_map/pallas_call | solution.py:510
  51.6 10.1 %all_to_all.38.buf_ref = bf16[32,16,128]{2,1,0:T(8,128)(2,1)S(1)} all-to-all(bf16[32,16,128]{2,1,0:T(8,128)(2,1)S(1)} %get-tuple-element.66), channel_id=1, replica_groups=mesh['gx'=8,'gy'=4] {'gx','gy'}, dimensions={0} | all-to-all | bytes 262144 | tf_op jit(solution)/shard_map/all_to_all | solution.py:524
  61.7 1.4 %shard_map.152 = (bf16[96,128]{1,0:T(8,128)(2,1)S(1)}, bf16[2048,128]{1,0:T(8,128)(2,1)S(1)}, f32[2048,128]{1,0:T(8,128)S(1)}, f32[4,96]{1,0:T(4,128)S(1)}) custom-call(s32[1]{0:T(128)S(6)} %copy.20.counts_ref, bf16[32,16,128]{2,1,0:T(8,128)(2,1)S(1)} %all_to_all.38.buf_ref, f32[96,128]{1,0:T(8,128)S(1)} %get-tuple-element.67.table_ref, ...), custom_call_target="tpu_custom_call" | custom-call | tf_op jit(solution)/shard_map/pallas_call | solution.py:510
  63.5 1.0 shard_map.153
  64.5 0.6 collective-permute-done.got_ref
  65.2 19.6 %all_to_all.39.buf_ref = bf16[32,80,128]{2,1,0:T(8,128)(2,1)S(1)} all-to-all(bf16[32,80,128]{2,1,0:T(8,128)(2,1)S(1)} %shard_map.154), channel_id=1, replica_groups=mesh['gx'=8,'gy'=4] {'gx','gy'}, dimensions={0} | all-to-all | bytes 1310720 | tf_op jit(solution)/shard_map/all_to_all | solution.py:524
  85.2 18.8 %all_to_all.40 = bf16[32,64,128]{2,1,0:T(8,128)(2,1)S(1)} all-to-all(bf16[32,64,128]{2,1,0:T(8,128)(2,1)S(1)} %get-tuple-element.78), channel_id=1, replica_groups=mesh['gx'=8,'gy'=4] {'gx','gy'}, dimensions={0} | all-to-all | bytes 1048576 | tf_op jit(solution)/shard_map/all_to_all | solution.py:524
  104.1 1.8 %shard_map.156 = (f32[27,96,96]{2,1,0:T(8,128)}, f32[27,96,96]{2,1,0:T(8,128)}, bf16[96,128]{1,0:T(8,128)(2,1)}, bf16[96,128]{1,0:T(8,128)(2,1)}, f32[4,96]{1,0:T(4,128)}) custom-call(bf16[2048,128]{1,0:T(8,128)(2,1)S(1)} %bitcast.12, bf16[96,128]{1,0:T(8,128)(2,1)S(1)} %get-tuple-element.79.small_in, bf16[96,128]{1,0:T(8,128)(2,1)S(1)} %get-tuple-element.80.more_in, ...), custom_call_target="tpu_custom_call" | custom-call | tf_op jit(solution)/shard_map/pallas_call | solution.py:510
  106.0 1.2 %shard_map.157 = (f32[27,96,96]{2,1,0:T(8,128)}, f32[27,96,96]{2,1,0:T(8,128)}) custom-call(bf16[2048,128]{1,0:T(8,128)(2,1)S(1)} %collective-permute-done.1.other_ref, f32[27,96,96]{2,1,0:T(8,128)} %get-tuple-element.84.one_in, f32[27,96,96]{2,1,0:T(8,128)} %get-tuple-element.85.two_in), custom_call_target="tpu_custom_call", output_to_operand_aliasing={{0}: (1, {}), {1}: (2, {})} | custom-call | tf_op jit(solution)/shard_map/pallas_call | solution.py:510
  (24 shorter events, 0.9 us)
Async XLA Ops:
  1.3 0.7 copy-start.5
  2.0 0.7 copy-start.7
  3.7 15.5 %all-to-all-start = ((bf16[32,16,128]{2,1,0:T(8,128)(2,1)}), bf16[32,16,128]{2,1,0:T(8,128)(2,1)S(1)}, u32[]{:S(2)}, u32[]{:S(2)}) async-start(bf16[32,16,128]{2,1,0:T(8,128)(2,1)} %get-tuple-element.47), calls=%async_computation | async-start | bytes 262144 | tf_op jit(solution)/shard_map/all_to_all | solution.py:524
  11.1 1.1 %copy-start = (bf16[27,96,96]{2,1,0:T(8,128)(2,1)S(1)}, bf16[27,96,96]{2,1,0:T(8,128)(2,1)}, u32[]{:S(2)}) copy-start(bf16[27,96,96]{2,1,0:T(8,128)(2,1)} %param.16) | copy-start | bytes 1492996
  12.1 1.1 %copy-start.2 = (bf16[27,96,96]{2,1,0:T(8,128)(2,1)S(1)}, bf16[27,96,96]{2,1,0:T(8,128)(2,1)}, u32[]{:S(2)}) copy-start(bf16[27,96,96]{2,1,0:T(8,128)(2,1)} %param.15) | copy-start | bytes 1492996
  13.2 0.7 copy-start.6
  19.3 11.1 %copy-start.8 = (f32[96]{0:T(128)S(1)}, f32[96]{0:T(128)}, u32[]{:S(2)}) copy-start(f32[96]{0:T(128)} %param.17) | copy-start | bytes 1156
  19.3 11.1 %copy-start.9 = (f32[96]{0:T(128)S(1)}, f32[96]{0:T(128)}, u32[]{:S(2)}) copy-start(f32[96]{0:T(128)} %param.18) | copy-start | bytes 1156
  30.4 10.3 %copy-start.4 = (bf16[96,128]{1,0:T(8,128)(2,1)S(1)}, bf16[96,128]{1,0:T(8,128)(2,1)}, u32[]{:S(2)}) copy-start(bf16[96,128]{1,0:T(8,128)(2,1)} %cotangent_ref.1) | copy-start | bytes 73732
  30.4 10.3 %copy-start.10 = (f32[96]{0:T(128)S(1)}, f32[96]{0:T(128)}, u32[]{:S(2)}) copy-start(f32[96]{0:T(128)} %param.19) | copy-start | bytes 1156
  30.4 10.3 %copy-start.11 = (f32[96]{0:T(128)S(1)}, f32[96]{0:T(128)}, u32[]{:S(2)}) copy-start(f32[96]{0:T(128)} %param.20) | copy-start | bytes 1156
  30.4 19.8 %copy-start.1 = (bf16[27,96,96]{2,1,0:T(8,128)(2,1)S(1)}, bf16[27,96,96]{2,1,0:T(8,128)(2,1)}, u32[]{:S(2)}) copy-start(bf16[27,96,96]{2,1,0:T(8,128)(2,1)} %param.16) | copy-start | bytes 1492996
  51.6 11.8 %copy-start.3 = (bf16[27,96,96]{2,1,0:T(8,128)(2,1)S(1)}, bf16[27,96,96]{2,1,0:T(8,128)(2,1)}, u32[]{:S(2)}) copy-start(bf16[27,96,96]{2,1,0:T(8,128)(2,1)} %param.15) | copy-start | bytes 1492996
  63.1 2.0 %collective-permute-start = (bf16[2048,128]{1,0:T(8,128)(2,1)S(1)}, bf16[2048,128]{1,0:T(8,128)(2,1)S(1)}, u32[]{:S(2)}, u32[]{:S(2)}) collective-permute-start(bf16[2048,128]{1,0:T(8,128)(2,1)S(1)} %get-tuple-element.76), channel_id=1, source_target_pairs={{0,1},{1,0},{2,3},{3,2},{4,5},{5,4},{6,7},{7,6},{8,9},{9,8},{10,11... | collective-permute-start | bytes 1572872 | tf_op jit(solution)/shard_map/ppermute | solution.py:529
  104.1 1.9 %collective-permute-start.1 = (bf16[2048,128]{1,0:T(8,128)(2,1)S(1)}, bf16[2048,128]{1,0:T(8,128)(2,1)S(1)}, u32[]{:S(2)}, u32[]{:S(2)}) collective-permute-start(bf16[2048,128]{1,0:T(8,128)(2,1)S(1)} %bitcast.11), channel_id=1, source_target_pairs={{0,1},{1,0},{2,3},{3,2},{4,5},{5,4},{6,7},{7,6},{8,9},{9,8},{10,11... | collective-permute-start | bytes 1572872 | tf_op jit(solution)/shard_map/ppermute | solution.py:529

commit v3 on v2

--- a/solution.py
+++ b/solution.py
@@ -160,15 +160,23 @@
     put_blocks(buf_ref, rows, grid, 1, width)
 
 
-def prepare_kernel(map_ref, one_ref, two_ref, hot_ref, one_t_ref, two_t_ref):
+def prepare_kernel(
+    map_hbm, one_hbm, two_hbm, hot_ref, one_t_ref, two_t_ref, map_ref, one_ref, two_ref, sems
+):
+    pairs = ((map_hbm, map_ref), (one_hbm, one_ref), (two_hbm, two_ref))
+    copies = [pltpu.make_async_copy(src, dst, sems.at[at]) for at, (src, dst) in enumerate(pairs)]
+    for copy in copies:
+        copy.start()
+    copies[0].wait()
     table = hot_ref.shape[0]
     sub = iota((table, LANES), 0)
     for k in range(map_ref.shape[0]):
-        hot_ref[:, k * LANES : (k + 1) * LANES] = jnp.where(
-            sub == map_ref[k : k + 1, :], 1.0, 0.0
-        ).astype(BF16)
+        part = slice(k * LANES, (k + 1) * LANES)
+        hot_ref[:, part] = jnp.where(sub == map_ref[k : k + 1, :], 1.0, 0.0).astype(BF16)
     unit = eye(one_ref.shape[1])
+    copies[1].wait()
     one_t_ref[...] = nt(unit, one_ref[...]).astype(BF16)
+    copies[2].wait()
     two_t_ref[...] = nt(unit, two_ref[...]).astype(BF16)
 
 
@@ -312,7 +320,8 @@
     terms = nn(weight_ref[...], grad).astype(BF16)
     offsets = hot_ref.shape[1] // LANES
     wide = jnp.concatenate([terms[k * channels : (k + 1) * channels] for k in range(offsets)], axis=1)
-    return nt(wide, hot_ref[...])
+    table = pad_to(nt(hot_ref[...], wide), hot_ref.shape[0], LANES)
+    return table[:LANES].T[:channels], table[LANES : 2 * LANES]
 
 
 def row_gradient(grad, normal, const, dgain, dbias, valid):
@@ -335,10 +344,8 @@
     sums_ref[...] = both
     grad = row_gradient(grad_ref[...], norm_ref[...], const_ref[...], both[0:1], both[1:2], valid)
     grad_two_ref[...] = grad
-    table = scatter(grad, weight_ref, hot_ref)
-    local = table[:, :LANES]
+    local, halo = scatter(grad, weight_ref, hot_ref)
     table_ref[...] = local
-    halo = pad_to(table[:, LANES : 2 * LANES], LANES, LANES).T
     pulled = local * slope_ref[...]
     dbias = jnp.sum(pulled, axis=1, keepdims=True)
     dgain = jnp.sum(pulled * norm_one_ref[...], axis=1, keepdims=True)
@@ -384,9 +391,9 @@
     width = buf_ref.shape[1]
     channels = norm_ref.shape[0]
     valid = valid_lanes(counts_ref)
-    dgains, dbiases = unpack_rows(buf_ref[...].astype(F32), ((0, 2), (2, 4)))
-    dgain = jnp.sum(dgains, axis=0, keepdims=True)
-    dbias = jnp.sum(dbiases, axis=0, keepdims=True)
+    dgain, dbias = unpack_rows(
+        jnp.sum(buf_ref[...].astype(F32), axis=0, keepdims=True), ((0, 2), (2, 4))
+    )
     two = sums_two_ref[...]
     sums_ref[...] = jnp.concatenate([dgain, dbias, two], axis=0)[:, :channels]
     arrived = nt(eye(LANES), take_blocks(buf_ref, grid, 1, width).astype(BF16))[:channels].astype(BF16)
@@ -417,9 +424,9 @@
 
 
 def back_kernel(grad_ref, weight_ref, hot_ref, table_ref, halo_ref):
-    table = scatter(grad_ref[...], weight_ref, hot_ref)
-    table_ref[...] = table[:, :LANES]
-    halo_ref[...] = pad_to(table[:, LANES : 2 * LANES], LANES, LANES).T.astype(BF16)
+    local, halo = scatter(grad_ref[...], weight_ref, hot_ref)
+    table_ref[...] = local
+    halo_ref[...] = halo.astype(BF16)
 
 
 def sixth_kernel(grid, width, halo_ref, keep_ref, got_ref, out_buf_ref):
@@ -506,6 +513,7 @@
             return pltpu.HBM
         return pltpu.SMEM if at < smem else pltpu.VMEM
 
+    args = [pltpu.with_memory_space_constraint(x, pltpu.HBM) if at in hbm else x for at, x in enumerate(args)]
     shapes = tuple(jax.ShapeDtypeStruct(shape, dtype) for shape, dtype in outs)
     return pl.pallas_call(
         kernel,
@@ -564,8 +572,15 @@
     buf = to_all(buf)
     hot, one_t, two_t = call(
         prepare_kernel,
-        [((table, offsets * LANES), BF16), ((channels, flat), BF16), ((channels, flat), BF16)],
-        kernel_map, one_flat, two_flat,
+        [
+            ((table, offsets * LANES), BF16),
+            ((channels, flat), BF16), ((channels, flat), BF16),
+        ],
+        kernel_map, one_flat, two_flat, hbm=(0, 1, 2),
+        scratch=[
+            pltpu.VMEM(kernel_map.shape, jnp.int32), pltpu.VMEM((flat, channels), BF16),
+            pltpu.VMEM((flat, channels), BF16), pltpu.SemaphoreType.DMA((3,)),
+        ],
     )
     buf, hidden_one, table_zero, flag = call(
         functools.partial(first_kernel, grid),

time: 108 us -> 107 us (level)
  local copies, waits for them, and re-layouts: 4.34 us -> 0.03 us
  waiting for transfers between devices: 5.14 us -> 7.1 us
  Pallas kernels: 12.2 us -> 13.8 us
    unnamed x24 -> x14, local copies, waits for them, and re-layouts: 4.34 us -> 0.03 us
    all_to_all x1, waiting for transfers between devices: 4.43 us -> 6.36 us  [to_all(): return lax.all_to_all(x, AXES, 0, 0)]
    pallas_call x12, Pallas kernels: 12.2 us -> 13.8 us  [call(): pl.pallas_call(kernel, out_shape=shapes, in_specs=[pl.BlockSpec(memory_sp...]
  transfers between devices with their start and end apart: 3 -> 3, of which waited for: 3 -> 3; matrix products, arithmetic and copies ran while one was open for 0% -> 0% of each run, Pallas kernels for 3% -> 4%
where the time goes in v3:
time: 107 us; the launch traced here: 106 us
  blocking collectives  76.5 us (71%)
  Pallas kernels  13.8 us (13%)
  starting transfers between devices  7.62 us (7%)
  waiting for transfers between devices  7.1 us (7%)
  between operations  1.4 us (1%)
    all_to_all x6, blocking collectives, to_all(): return lax.all_to_all(x, AXES, 0, 0)  76.5 us
    pallas_call x12, Pallas kernels, call(): pl.pallas_call(kernel, out_shape=shapes, in_specs=[pl.BlockSpec(memory_sp...  13.8 us
    all_to_all x1, starting transfers between devices, to_all(): return lax.all_to_all(x, AXES, 0, 0)  7.3 us
    all_to_all x1, waiting for transfers between devices, to_all(): return lax.all_to_all(x, AXES, 0, 0)  6.36 us
  transfers between devices with their start and end apart: 3, of which 3 were waited for; matrix products, arithmetic and copies ran while one was open for 0% of the time, Pallas kernels for 4%

profile of v3, /device:TPU:0, one launch (start us, length us, event | category | flops | bytes accessed | tf_op | source)
XLA Modules:
  0.0 106.4 jit_solution(10825470313267588148)
XLA Ops:
  1.3 1.8 %shard_map.146 = (bf16[32,16,128]{2,1,0:T(8,128)(2,1)}, bf16[96,128]{1,0:T(8,128)(2,1)S(1)}, bf16[128,128]{1,0:T(8,128)(2,1)S(1)}) custom-call(s32[1]{0:T(128)S(6)} %copy.20.counts_ref, bf16[96,128]{1,0:T(8,128)(2,1)} %features_hbm.1, s32[8,16]{1,0:T(8,128)} %send_hbm.1), custom_call_target="tpu_custom_call" | custom-call | tf_op jit(solution)/shard_map/pallas_call | solution.py:518
  3.0 7.3 %all-to-all-start = ((bf16[32,16,128]{2,1,0:T(8,128)(2,1)}), bf16[32,16,128]{2,1,0:T(8,128)(2,1)S(1)}, u32[]{:S(2)}, u32[]{:S(2)}) async-start(bf16[32,16,128]{2,1,0:T(8,128)(2,1)} %get-tuple-element.47), calls=%async_computation | async-start | bytes 262144 | tf_op jit(solution)/shard_map/all_to_all | solution.py:532
  10.4 1.9 %shard_map.147 = (bf16[256,3456]{1,0:T(8,128)(2,1)S(1)}, bf16[96,2592]{1,0:T(8,128)(2,1)S(1)}, bf16[96,2592]{1,0:T(8,128)(2,1)S(1)}) custom-call(s32[27,128]{1,0:T(8,128)} %map_hbm.1, bf16[2592,96]{1,0:T(8,128)(2,1)} %bitcast.9, bf16[2592,96]{1,0:T(8,128)(2,1)} %bitcast.7), custom_call_target="tpu_custom_call" | custom-call | tf_op jit(solution)/shard_map/pallas_call | solution.py:518
  12.2 6.4 %all-to-all-done.buf_ref = bf16[32,16,128]{2,1,0:T(8,128)(2,1)S(1)} async-done(((bf16[32,16,128]{2,1,0:T(8,128)(2,1)}), bf16[32,16,128]{2,1,0:T(8,128)(2,1)S(1)}, u32[]{:S(2)}, u32[]{:S(2)}) %all-to-all-start) | async-done | bytes 131104 | tf_op jit(solution)/shard_map/all_to_all | solution.py:532
  18.6 1.1 %shard_map.148 = (bf16[32,16,128]{2,1,0:T(8,128)(2,1)S(1)}, f32[96,128]{1,0:T(8,128)S(1)}, bf16[96,256]{1,0:T(8,128)(2,1)S(1)}, f32[128,128]{1,0:T(8,128)S(1)}) custom-call(s32[1]{0:T(128)S(6)} %copy.20.counts_ref, bf16[32,16,128]{2,1,0:T(8,128)(2,1)S(1)} %all-to-all-done.buf_ref, bf16[96,128]{1,0:T(8,128)(2,1)S(1)} %get-tuple-element.48.start_ref, ...), custom_call_target="tpu_custom_call" | custom-call | tf_op jit(solution)/shard_map/pallas_call | solution.py:518
  19.7 10.0 %all_to_all.35.buf_ref = bf16[32,16,128]{2,1,0:T(8,128)(2,1)S(1)} all-to-all(bf16[32,16,128]{2,1,0:T(8,128)(2,1)S(1)} %get-tuple-element.52), channel_id=1, replica_groups=mesh['gx'=8,'gy'=4] {'gx','gy'}, dimensions={0} | all-to-all | bytes 262144 | tf_op jit(solution)/shard_map/all_to_all | solution.py:532
  29.7 0.0 copy-start
  29.7 1.3 %shard_map.149 = (f32[32,2,128]{2,1,0:T(2,128)S(1)}, f32[96,128]{1,0:T(8,128)S(1)}, bf16[96,256]{1,0:T(8,128)(2,1)S(1)}, f32[96,128]{1,0:T(8,128)S(1)}, f32[96,1...) custom-call(s32[1]{0:T(128)S(6)} %copy.20.counts_ref, ...), custom_call_target="tpu_custom_call" | custom-call | tf_op jit(solution)/shard_map/pallas_call | solution.py:518
  31.0 9.0 %all_to_all.36.buf_ref = f32[32,2,128]{2,1,0:T(2,128)S(1)} all-to-all(f32[32,2,128]{2,1,0:T(2,128)S(1)} %get-tuple-element.56), channel_id=1, replica_groups=mesh['gx'=8,'gy'=4] {'gx','gy'}, dimensions={0} | all-to-all | bytes 65536 | tf_op jit(solution)/shard_map/all_to_all | solution.py:532
  40.0 0.5 shard_map.150
  40.5 8.9 %all_to_all.37.buf_ref = f32[32,2,128]{2,1,0:T(2,128)S(1)} all-to-all(f32[32,2,128]{2,1,0:T(2,128)S(1)} %get-tuple-element.58), channel_id=1, replica_groups=mesh['gx'=8,'gy'=4] {'gx','gy'}, dimensions={0} | all-to-all | bytes 65536 | tf_op jit(solution)/shard_map/all_to_all | solution.py:532
  49.5 1.5 %shard_map.151 = (bf16[32,16,128]{2,1,0:T(8,128)(2,1)S(1)}, bf16[96,128]{1,0:T(8,128)(2,1)S(1)}, f32[96,128]{1,0:T(8,128)S(1)}, f32[2,128]{1,0:T(2,128)S(1)}) custom-call(s32[1]{0:T(128)S(6)} %copy.20.counts_ref, f32[32,2,128]{2,1,0:T(2,128)S(1)} %all_to_all.37.buf_ref, f32[96,128]{1,0:T(8,128)S(1)} %get-tuple-element.59.norm_ref, ...), custom_call_target="tpu_custom_call" | custom-call | tf_op jit(solution)/shard_map/pallas_call | solution.py:518
  51.0 10.1 %all_to_all.38.buf_ref = bf16[32,16,128]{2,1,0:T(8,128)(2,1)S(1)} all-to-all(bf16[32,16,128]{2,1,0:T(8,128)(2,1)S(1)} %get-tuple-element.66), channel_id=1, replica_groups=mesh['gx'=8,'gy'=4] {'gx','gy'}, dimensions={0} | all-to-all | bytes 262144 | tf_op jit(solution)/shard_map/all_to_all | solution.py:532
  61.1 1.3 %shard_map.152 = (bf16[96,128]{1,0:T(8,128)(2,1)S(1)}, bf16[2048,128]{1,0:T(8,128)(2,1)S(1)}, f32[2048,128]{1,0:T(8,128)S(1)}, f32[4,96]{1,0:T(4,128)S(1)}) custom-call(s32[1]{0:T(128)S(6)} %copy.20.counts_ref, bf16[32,16,128]{2,1,0:T(8,128)(2,1)S(1)} %all_to_all.38.buf_ref, f32[96,128]{1,0:T(8,128)S(1)} %get-tuple-element.67.table_ref, ...), custom_call_target="tpu_custom_call" | custom-call | tf_op jit(solution)/shard_map/pallas_call | solution.py:518
  62.4 0.3 collective-permute-start
  62.7 1.0 shard_map.153
  63.7 0.7 collective-permute-done.got_ref
  64.4 0.1 shard_map.154
  64.5 19.6 %all_to_all.39.buf_ref = bf16[32,80,128]{2,1,0:T(8,128)(2,1)S(1)} all-to-all(bf16[32,80,128]{2,1,0:T(8,128)(2,1)S(1)} %shard_map.154), channel_id=1, replica_groups=mesh['gx'=8,'gy'=4] {'gx','gy'}, dimensions={0} | all-to-all | bytes 1310720 | tf_op jit(solution)/shard_map/all_to_all | solution.py:532
  84.1 0.4 shard_map.155
  84.5 18.8 %all_to_all.40 = bf16[32,64,128]{2,1,0:T(8,128)(2,1)S(1)} all-to-all(bf16[32,64,128]{2,1,0:T(8,128)(2,1)S(1)} %get-tuple-element.78), channel_id=1, replica_groups=mesh['gx'=8,'gy'=4] {'gx','gy'}, dimensions={0} | all-to-all | bytes 1048576 | tf_op jit(solution)/shard_map/all_to_all | solution.py:532
  103.3 1.8 %shard_map.156 = (f32[27,96,96]{2,1,0:T(8,128)}, f32[27,96,96]{2,1,0:T(8,128)}, bf16[96,128]{1,0:T(8,128)(2,1)}, bf16[96,128]{1,0:T(8,128)(2,1)}, f32[4,96]{1,0:T(4,128)}) custom-call(bf16[2048,128]{1,0:T(8,128)(2,1)S(1)} %bitcast.12, bf16[96,128]{1,0:T(8,128)(2,1)S(1)} %get-tuple-element.79.small_in, bf16[96,128]{1,0:T(8,128)(2,1)S(1)} %get-tuple-element.80.more_in, ...), custom_call_target="tpu_custom_call" | custom-call | tf_op jit(solution)/shard_map/pallas_call | solution.py:518
  105.2 0.1 collective-permute-done.1.other_ref
  105.2 1.2 %shard_map.157 = (f32[27,96,96]{2,1,0:T(8,128)}, f32[27,96,96]{2,1,0:T(8,128)}) custom-call(bf16[2048,128]{1,0:T(8,128)(2,1)S(1)} %collective-permute-done.1.other_ref, f32[27,96,96]{2,1,0:T(8,128)} %get-tuple-element.84.one_in, f32[27,96,96]{2,1,0:T(8,128)} %get-tuple-element.85.two_in), custom_call_target="tpu_custom_call", output_to_operand_aliasing={{0}: (1, {}), {1}: (2, {})} | custom-call | tf_op jit(solution)/shard_map/pallas_call | solution.py:518
  (14 shorter events, 0.0 us)
Async XLA Ops:
  3.0 15.5 %all-to-all-start = ((bf16[32,16,128]{2,1,0:T(8,128)(2,1)}), bf16[32,16,128]{2,1,0:T(8,128)(2,1)S(1)}, u32[]{:S(2)}, u32[]{:S(2)}) async-start(bf16[32,16,128]{2,1,0:T(8,128)(2,1)} %get-tuple-element.47), calls=%async_computation | async-start | bytes 262144 | tf_op jit(solution)/shard_map/all_to_all | solution.py:532
  18.6 11.1 %copy-start.3 = (f32[96]{0:T(128)S(1)}, f32[96]{0:T(128)}, u32[]{:S(2)}) copy-start(f32[96]{0:T(128)} %param.17) | copy-start | bytes 1156
  18.6 11.1 %copy-start.4 = (f32[96]{0:T(128)S(1)}, f32[96]{0:T(128)}, u32[]{:S(2)}) copy-start(f32[96]{0:T(128)} %param.18) | copy-start | bytes 1156
  29.7 10.3 %copy-start.2 = (bf16[96,128]{1,0:T(8,128)(2,1)S(1)}, bf16[96,128]{1,0:T(8,128)(2,1)}, u32[]{:S(2)}) copy-start(bf16[96,128]{1,0:T(8,128)(2,1)} %cotangent_ref.1) | copy-start | bytes 73732
  29.7 10.3 %copy-start.5 = (f32[96]{0:T(128)S(1)}, f32[96]{0:T(128)}, u32[]{:S(2)}) copy-start(f32[96]{0:T(128)} %param.19) | copy-start | bytes 1156
  29.7 10.3 %copy-start.6 = (f32[96]{0:T(128)S(1)}, f32[96]{0:T(128)}, u32[]{:S(2)}) copy-start(f32[96]{0:T(128)} %param.20) | copy-start | bytes 1156
  29.7 19.8 %copy-start = (bf16[27,96,96]{2,1,0:T(8,128)(2,1)S(1)}, bf16[27,96,96]{2,1,0:T(8,128)(2,1)}, u32[]{:S(2)}) copy-start(bf16[27,96,96]{2,1,0:T(8,128)(2,1)} %param.16) | copy-start | bytes 1492996
  51.0 11.7 %copy-start.1 = (bf16[27,96,96]{2,1,0:T(8,128)(2,1)S(1)}, bf16[27,96,96]{2,1,0:T(8,128)(2,1)}, u32[]{:S(2)}) copy-start(bf16[27,96,96]{2,1,0:T(8,128)(2,1)} %param.15) | copy-start | bytes 1492996
  62.4 2.0 %collective-permute-start = (bf16[2048,128]{1,0:T(8,128)(2,1)S(1)}, bf16[2048,128]{1,0:T(8,128)(2,1)S(1)}, u32[]{:S(2)}, u32[]{:S(2)}) collective-permute-start(bf16[2048,128]{1,0:T(8,128)(2,1)S(1)} %get-tuple-element.76), channel_id=1, source_target_pairs={{0,1},{1,0},{2,3},{3,2},{4,5},{5,4},{6,7},{7,6},{8,9},{9,8},{10,11... | collective-permute-start | bytes 1572872 | tf_op jit(solution)/shard_map/ppermute | solution.py:537
  103.3 1.9 %collective-permute-start.1 = (bf16[2048,128]{1,0:T(8,128)(2,1)S(1)}, bf16[2048,128]{1,0:T(8,128)(2,1)S(1)}, u32[]{:S(2)}, u32[]{:S(2)}) collective-permute-start(bf16[2048,128]{1,0:T(8,128)(2,1)S(1)} %bitcast.11), channel_id=1, source_target_pairs={{0,1},{1,0},{2,3},{3,2},{4,5},{5,4},{6,7},{7,6},{8,9},{9,8},{10,11... | collective-permute-start | bytes 1572872 | tf_op jit(solution)/shard_map/ppermute | solution.py:537

commit v4 on v3

--- a/solution.py
+++ b/solution.py
@@ -197,7 +197,7 @@
 
 def first_kernel(
     grid, counts_ref, buf_ref, start_ref, hot_ref, weight_ref, place_ref,
-    out_buf_ref, hidden_ref, table_ref, flag_ref, taken_ref,
+    out_buf_ref, hidden_ref, taken_ref, flag_ref,
 ):
     width = buf_ref.shape[1]
     channels = start_ref.shape[0]
@@ -205,7 +205,6 @@
     flag_ref[...] = jnp.broadcast_to(halo_rows[:, 96:97].astype(F32), (LANES, LANES))
     halo = nt(eye(LANES), halo_rows)[:channels].astype(BF16)
     table = jnp.concatenate([start_ref[...], halo], axis=1)
-    table_ref[...] = table
     hidden = gather_convolve(table, hot_ref, weight_ref, taken_ref)
     hidden_ref[...] = hidden
     valid = valid_lanes(counts_ref)
@@ -222,8 +221,8 @@
 
 def second_kernel(
     grid, counts_ref, buf_ref, hidden_ref, flag_ref, scale_ref, bias_ref, hot_ref, weight_ref,
-    out_buf_ref, hidden_two_ref, table_ref, norm_ref, slope_ref, halo_slope_ref, halo_cross_ref,
-    const_ref, mean_ref, taken_ref,
+    out_buf_ref, hidden_two_ref, taken_ref, norm_ref, slope_ref, halo_slope_ref, halo_cross_ref,
+    const_ref, mean_ref,
 ):
     width = buf_ref.shape[1]
     channels = hidden_ref.shape[0]
@@ -270,7 +269,6 @@
     halo_act = nt(eye(LANES), (halo_linear * halo_sig * flag).astype(BF16))[:channels].astype(BF16)
 
     table = jnp.concatenate([act, halo_act], axis=1)
-    table_ref[...] = table
     hidden = gather_convolve(table, hot_ref, weight_ref, taken_ref)
     hidden_two_ref[...] = hidden
     count = counts_ref[0].astype(F32)
@@ -383,10 +381,22 @@
         put(18 + e, last[e * channels : (e + 1) * channels])
 
 
+def store_packed(taken_ref, grad, ref):
+    channels = grad.shape[0]
+    used = 21 * channels
+
+    def put(block, value):
+        ref[block * channels : (block + 1) * channels, :] = value.astype(ref.dtype)
+
+    packed_weight_grad(taken_ref, grad, put)
+    if ref.shape[0] > used:
+        ref[used:, :] = jnp.zeros((ref.shape[0] - used, LANES), ref.dtype)
+
+
 def fifth_kernel(
     grid, counts_ref, buf_ref, table_ref, place_ref, norm_ref, slope_ref, const_ref, sums_two_ref,
-    table_zero_ref, table_act_ref, hot_ref, grad_two_ref,
-    grad_one_ref, give_ref, keep_ref, sums_ref, taken_zero_ref, taken_act_ref,
+    taken_zero_ref, taken_act_ref, grad_two_ref,
+    grad_one_ref, give_ref, sums_ref,
 ):
     width = buf_ref.shape[1]
     channels = norm_ref.shape[0]
@@ -400,30 +410,30 @@
     back = table_ref[...] + nn(arrived, place_ref[...])
     grad = row_gradient(back * slope_ref[...], norm_ref[...], const_ref[...], dgain, dbias, valid)
     grad_one_ref[...] = grad
-    gather([table_zero_ref[...], table_act_ref[...]], hot_ref, [taken_zero_ref, taken_act_ref])
     core = lax.axis_index("gy") % 2
-    used = 21 * channels
-
-    def store(taken_ref, row_grad, ref):
-        def put(block, value):
-            ref[block * channels : (block + 1) * channels, :] = value.astype(ref.dtype)
-
-        packed_weight_grad(taken_ref, row_grad, put)
-        if ref.shape[0] > used:
-            ref[used:, :] = jnp.zeros((ref.shape[0] - used, LANES), ref.dtype)
 
     @pl.when(core == 0)
     def _():
-        store(taken_zero_ref, grad, keep_ref)
-        store(taken_act_ref, grad_two_ref[...], give_ref)
+        store_packed(taken_act_ref, grad_two_ref[...], give_ref)
 
     @pl.when(core != 0)
     def _():
-        store(taken_zero_ref, grad, give_ref)
-        store(taken_act_ref, grad_two_ref[...], keep_ref)
-
-
-def back_kernel(grad_ref, weight_ref, hot_ref, table_ref, halo_ref):
+        store_packed(taken_zero_ref, grad, give_ref)
+
+
+def back_kernel(
+    grad_ref, weight_ref, hot_ref, taken_zero_ref, taken_act_ref, grad_two_ref, table_ref, halo_ref, keep_ref
+):
+    core = lax.axis_index("gy") % 2
+
+    @pl.when(core == 0)
+    def _():
+        store_packed(taken_zero_ref, grad_ref[...], keep_ref)
+
+    @pl.when(core != 0)
+    def _():
+        store_packed(taken_act_ref, grad_two_ref[...], keep_ref)
+
     local, halo = scatter(grad_ref[...], weight_ref, hot_ref)
     table_ref[...] = local
     halo_ref[...] = halo.astype(BF16)
@@ -507,25 +517,38 @@
         unpack(other_ref, one_hbm, block_ref, sems)
 
 
-def call(kernel, outs, *args, smem=0, scratch=(), hbm=(), hbm_outs=(), aliases=None):
+def call(kernel, outs, *args, smem=0, scratch=(), hbm=(), hbm_outs=(), aliases=None, carry=()):
+    n_in, n_out = len(args), len(outs)
+    aliases = dict(aliases or {})
+    aliases.update({n_in + at: n_out + at for at in range(len(carry))})
+
     def space(at):
+        if at >= n_in:
+            return pl.ANY
         if at in hbm:
             return pltpu.HBM
         return pltpu.SMEM if at < smem else pltpu.VMEM
 
+    def out_space(at):
+        if at >= n_out:
+            return pl.ANY
+        return pltpu.HBM if at in hbm_outs else pltpu.VMEM
+
+    def body(*refs):
+        first_out = n_in + len(carry)
+        kernel(*refs[:n_in], *refs[first_out : first_out + n_out], *refs[first_out + n_out + len(carry) :])
+
     args = [pltpu.with_memory_space_constraint(x, pltpu.HBM) if at in hbm else x for at, x in enumerate(args)]
-    shapes = tuple(jax.ShapeDtypeStruct(shape, dtype) for shape, dtype in outs)
+    outs = list(outs) + [(x.shape, x.dtype) for x in carry]
     return pl.pallas_call(
-        kernel,
-        out_shape=shapes,
-        in_specs=[pl.BlockSpec(memory_space=space(at)) for at in range(len(args))],
-        out_specs=tuple(
-            pl.BlockSpec(memory_space=pltpu.HBM if at in hbm_outs else pltpu.VMEM) for at in range(len(shapes))
-        ),
+        body,
+        out_shape=tuple(jax.ShapeDtypeStruct(shape, dtype) for shape, dtype in outs),
+        in_specs=[pl.BlockSpec(memory_space=space(at)) for at in range(n_in + len(carry))],
+        out_specs=tuple(pl.BlockSpec(memory_space=out_space(at)) for at in range(len(outs))),
         scratch_shapes=list(scratch),
-        input_output_aliases=aliases or {},
+        input_output_aliases=aliases,
         compiler_params=pltpu.CompilerParams(vmem_limit_bytes=40 * 1024 * 1024),
-    )(*args)
+    )(*args, *carry)
 
 
 def to_all(x):
@@ -559,8 +582,7 @@
         for v in (first_norm_scale, first_norm_bias, second_norm_scale, second_norm_bias)
     ]
 
-    taken = pltpu.VMEM((flat, LANES), BF16)
-    wide = ((channels, table), BF16)
+    taken = ((flat, LANES), BF16)
     buf, start, place = call(
         functools.partial(open_kernel, grid),
         [((devices, width, LANES), BF16), (full, BF16), (square, BF16)],
@@ -582,44 +604,46 @@
             pltpu.VMEM((flat, channels), BF16), pltpu.SemaphoreType.DMA((3,)),
         ],
     )
-    buf, hidden_one, table_zero, flag = call(
+    buf, hidden_one, taken_zero, flag = call(
         functools.partial(first_kernel, grid),
-        [((devices, width, LANES), BF16), (full, F32), wide, (square, F32)],
-        counts, buf, start, hot, one_t, place, smem=1, scratch=[taken],
+        [((devices, width, LANES), BF16), (full, F32), taken, (square, F32)],
+        counts, buf, start, hot, one_t, place, smem=1,
     )
     buf = to_all(buf)
-    buf, hidden_two, table_act, norm_one, slope_one, halo_slope, halo_cross, const_one = call(
+    buf, hidden_two, taken_act, norm_one, slope_one, halo_slope, halo_cross, const_one, taken_zero = call(
         functools.partial(second_kernel, grid),
         [
-            ((devices, 2, LANES), F32), (full, F32), wide, (full, F32), (full, F32),
+            ((devices, 2, LANES), F32), (full, F32), taken, (full, F32), (full, F32),
             (square, F32), (square, F32), ((8, LANES), F32),
         ],
         counts, buf, hidden_one, flag, scale_one, bias_one, hot, two_t,
-        smem=1, scratch=[pltpu.VMEM((devices, LANES), F32), taken],
+        smem=1, scratch=[pltpu.VMEM((devices, LANES), F32)], carry=[taken_zero],
     )
     buf = to_all(buf)
-    buf, output, norm_two, grad_sum, const_two = call(
+    buf, output, norm_two, grad_sum, const_two, taken_zero, taken_act = call(
         third_kernel,
         [((devices, 2, LANES), F32), (full, BF16), (full, F32), (full, F32), ((8, LANES), F32)],
-        counts, buf, hidden_two, start, cotangent, scale_two, bias_two, smem=1,
+        counts, buf, hidden_two, start, cotangent, scale_two, bias_two, smem=1, carry=[taken_zero, taken_act],
     )
     buf = to_all(buf)
-    buf, grad_two, table_two, sums_two = call(
+    buf, grad_two, table_two, sums_two, taken_zero, taken_act = call(
         functools.partial(fourth_kernel, grid),
         [((devices, width, LANES), BF16), (full, BF16), (full, F32), ((2, LANES), F32)],
         counts, buf, norm_two, grad_sum, const_two, two_flat, hot, norm_one, slope_one, halo_slope, halo_cross,
-        smem=1,
+        smem=1, carry=[taken_zero, taken_act],
     )
     buf = to_all(buf)
-    grad_one, give, keep, grad_norms = call(
+    grad_one, give, grad_norms = call(
         functools.partial(fifth_kernel, grid),
-        [(full, BF16), ((packed, LANES), BF16), ((packed, LANES), F32), ((4, channels), F32)],
+        [(full, BF16), ((packed, LANES), BF16), ((4, channels), F32)],
         counts, buf, table_two, place, norm_one, slope_one, const_one, sums_two,
-        table_zero, table_act, hot, grad_two, smem=1, scratch=[taken, taken],
+        taken_zero, taken_act, grad_two, smem=1,
     )
     got = swap_core(give)
-    table_one, halo_one = call(
-        back_kernel, [(full, F32), (square, BF16)], grad_one, one_flat, hot
+    table_one, halo_one, keep = call(
+        back_kernel,
+        [(full, F32), (square, BF16), ((packed, LANES), F32)],
+        grad_one, one_flat, hot, taken_zero, taken_act, grad_two,
     )
     (buf,) = call(
         functools.partial(sixth_kernel, grid, width),

time: 107 us -> 106 us (level)
  transfers between devices with their start and end apart: 3 -> 3, of which waited for: 3 -> 3; matrix products, arithmetic and copies ran while one was open for 0% -> 0% of each run, Pallas kernels for 4% -> 5%
where the time goes in v4:
time: 106 us
  blocking collectives  76.5 us (72%)
  Pallas kernels  13.6 us (13%)
  starting transfers between devices  7.61 us (7%)
  waiting for transfers between devices  6.7 us (6%)
  between operations  1.4 us (1%)
    all_to_all x6, blocking collectives, to_all(): return lax.all_to_all(x, AXES, 0, 0)  76.5 us
    pallas_call x12, Pallas kernels, call(): pl.pallas_call(body, out_shape=tuple((jax.ShapeDtypeStruct(shape, dtype)...  13.6 us
    all_to_all x1, starting transfers between devices, to_all(): return lax.all_to_all(x, AXES, 0, 0)  7.3 us
    all_to_all x1, waiting for transfers between devices, to_all(): return lax.all_to_all(x, AXES, 0, 0)  6.36 us
  transfers between devices with their start and end apart: 3, of which 3 were waited for; matrix products, arithmetic and copies ran while one was open for 0% of the time, Pallas kernels for 5%

profile of v4, /device:TPU:0, one launch (start us, length us, event | category | flops | bytes accessed | tf_op | source)
XLA Modules:
  0.0 105.9 jit_solution(11518764339321693464)
XLA Ops:
  1.3 1.8 %shard_map.146 = (bf16[32,16,128]{2,1,0:T(8,128)(2,1)}, bf16[96,128]{1,0:T(8,128)(2,1)S(1)}, bf16[128,128]{1,0:T(8,128)(2,1)S(1)}) custom-call(s32[1]{0:T(128)S(6)} %copy.30.refs_0_, bf16[96,128]{1,0:T(8,128)(2,1)} %refs_1_.1, s32[8,16]{1,0:T(8,128)} %refs_2_.1), custom_call_target="tpu_custom_call" | custom-call | tf_op jit(solution)/shard_map/pallas_call | solution.py:543
  3.0 7.3 %all-to-all-start = ((bf16[32,16,128]{2,1,0:T(8,128)(2,1)}), bf16[32,16,128]{2,1,0:T(8,128)(2,1)S(1)}, u32[]{:S(2)}, u32[]{:S(2)}) async-start(bf16[32,16,128]{2,1,0:T(8,128)(2,1)} %get-tuple-element.52), calls=%async_computation | async-start | bytes 262144 | tf_op jit(solution)/shard_map/all_to_all | solution.py:555
  10.4 1.9 %shard_map.147 = (bf16[256,3456]{1,0:T(8,128)(2,1)S(1)}, bf16[96,2592]{1,0:T(8,128)(2,1)S(1)}, bf16[96,2592]{1,0:T(8,128)(2,1)S(1)}) custom-call(s32[27,128]{1,0:T(8,128)} %refs_0_.8, bf16[2592,96]{1,0:T(8,128)(2,1)} %bitcast.9, bf16[2592,96]{1,0:T(8,128)(2,1)} %bitcast.7), custom_call_target="tpu_custom_call" | custom-call | tf_op jit(solution)/shard_map/pallas_call | solution.py:543
  12.2 6.4 %all-to-all-done.refs_1_ = bf16[32,16,128]{2,1,0:T(8,128)(2,1)S(1)} async-done(((bf16[32,16,128]{2,1,0:T(8,128)(2,1)}), bf16[32,16,128]{2,1,0:T(8,128)(2,1)S(1)}, u32[]{:S(2)}, u32[]{:S(2)}) %all-to-all-start) | async-done | bytes 131104 | tf_op jit(solution)/shard_map/all_to_all | solution.py:555
  18.6 1.1 %shard_map.148 = (bf16[32,16,128]{2,1,0:T(8,128)(2,1)S(1)}, f32[96,128]{1,0:T(8,128)S(1)}, bf16[2592,128]{1,0:T(8,128)(2,1)S(1)}, f32[128,128]{1,0:T(8,128)S(1)}) custom-call(s32[1]{0:T(128)S(6)} %copy.30.refs_0_, bf16[32,16,128]{2,1,0:T(8,128)(2,1)S(1)} %all-to-all-done.refs_1_, bf16[96,128]{1,0:T(8,128)(2,1)S(1)} %get-tuple-element.53.refs_2_.refs_3_, ...), custom_call_target="tpu_custom_call" | custom-call | tf_op jit(solution)/shard_map/pallas_call | solution.py:543
  19.7 10.0 %all_to_all.35.refs_1_ = bf16[32,16,128]{2,1,0:T(8,128)(2,1)S(1)} all-to-all(bf16[32,16,128]{2,1,0:T(8,128)(2,1)S(1)} %get-tuple-element.57), channel_id=1, replica_groups=mesh['gx'=8,'gy'=4] {'gx','gy'}, dimensions={0} | all-to-all | bytes 262144 | tf_op jit(solution)/shard_map/all_to_all | solution.py:555
  29.7 0.0 copy-start.6
  29.7 1.3 %shard_map.149 = (f32[32,2,128]{2,1,0:T(2,128)S(1)}, f32[96,128]{1,0:T(8,128)S(1)}, bf16[2592,128]{1,0:T(8,128)(2,1)S(1)}, f32[96,128]{1,0:T(8,128)S(1)}, f32[96...) custom-call(s32[1]{0:T(128)S(6)} %copy.30.refs_0_, ...), custom_call_target="tpu_custom_call", output_to_operand_aliasing={{8}: (8, {})} | custom-call | tf_op jit(solution)/shard_map/pallas_call | solution.py:543
  31.0 9.1 %all_to_all.36.refs_1_ = f32[32,2,128]{2,1,0:T(2,128)S(1)} all-to-all(f32[32,2,128]{2,1,0:T(2,128)S(1)} %get-tuple-element.62), channel_id=1, replica_groups=mesh['gx'=8,'gy'=4] {'gx','gy'}, dimensions={0} | all-to-all | bytes 65536 | tf_op jit(solution)/shard_map/all_to_all | solution.py:555
  40.1 0.5 shard_map.150
  40.6 8.9 %all_to_all.37.refs_1_ = f32[32,2,128]{2,1,0:T(2,128)S(1)} all-to-all(f32[32,2,128]{2,1,0:T(2,128)S(1)} %get-tuple-element.66), channel_id=1, replica_groups=mesh['gx'=8,'gy'=4] {'gx','gy'}, dimensions={0} | all-to-all | bytes 65536 | tf_op jit(solution)/shard_map/all_to_all | solution.py:555
  49.6 1.5 %shard_map.151 = (bf16[32,16,128]{2,1,0:T(8,128)(2,1)S(1)}, bf16[96,128]{1,0:T(8,128)(2,1)S(1)}, f32[96,128]{1,0:T(8,128)S(1)}, f32[2,128]{1,0:T(2,128)S(1)}, bf...) custom-call(s32[1]{0:T(128)S(6)} %copy.30.refs_0_, ...), custom_call_target="tpu_custom_call", output_to_operand_aliasing={{4}: (11, {}), {5}: (12, {})} | custom-call | tf_op jit(solution)/shard_map/pallas_call | solution.py:543
  51.1 10.1 %all_to_all.38.refs_1_ = bf16[32,16,128]{2,1,0:T(8,128)(2,1)S(1)} all-to-all(bf16[32,16,128]{2,1,0:T(8,128)(2,1)S(1)} %get-tuple-element.76), channel_id=1, replica_groups=mesh['gx'=8,'gy'=4] {'gx','gy'}, dimensions={0} | all-to-all | bytes 262144 | tf_op jit(solution)/shard_map/all_to_all | solution.py:555
  61.1 0.7 shard_map.152
  61.9 0.3 collective-permute-start
  62.2 1.4 %shard_map.153 = (f32[96,128]{1,0:T(8,128)S(1)}, bf16[128,128]{1,0:T(8,128)(2,1)S(1)}, f32[2048,128]{1,0:T(8,128)S(1)}) custom-call(bf16[96,128]{1,0:T(8,128)(2,1)S(1)} %get-tuple-element.83.refs_0_, bf16[2592,96]{1,0:T(8,128)(2,1)S(1)} %bitcast.10, bf16[256,3456]{1,0:T(8,128)(2,1)S(1)} %get-tuple-element.54.refs_3_.refs_6_.refs_2_, ...), custom_call_target="tpu_custom_call" | custom-call | tf_op jit(solution)/shard_map/pallas_call | solution.py:543
  63.6 0.3 collective-permute-done.refs_2_
  63.8 0.1 shard_map.154
  64.0 19.6 %all_to_all.39.refs_1_ = bf16[32,80,128]{2,1,0:T(8,128)(2,1)S(1)} all-to-all(bf16[32,80,128]{2,1,0:T(8,128)(2,1)S(1)} %shard_map.154), channel_id=1, replica_groups=mesh['gx'=8,'gy'=4] {'gx','gy'}, dimensions={0} | all-to-all | bytes 1310720 | tf_op jit(solution)/shard_map/all_to_all | solution.py:555
  83.6 0.4 shard_map.155
  84.0 18.8 %all_to_all.40 = bf16[32,64,128]{2,1,0:T(8,128)(2,1)S(1)} all-to-all(bf16[32,64,128]{2,1,0:T(8,128)(2,1)S(1)} %get-tuple-element.88), channel_id=1, replica_groups=mesh['gx'=8,'gy'=4] {'gx','gy'}, dimensions={0} | all-to-all | bytes 1048576 | tf_op jit(solution)/shard_map/all_to_all | solution.py:555
  102.8 1.8 %shard_map.156 = (f32[27,96,96]{2,1,0:T(8,128)}, f32[27,96,96]{2,1,0:T(8,128)}, bf16[96,128]{1,0:T(8,128)(2,1)}, bf16[96,128]{1,0:T(8,128)(2,1)}, f32[4,96]{1,0:T(4,128)}) custom-call(bf16[2048,128]{1,0:T(8,128)(2,1)S(1)} %bitcast.12, bf16[96,128]{1,0:T(8,128)(2,1)S(1)} %get-tuple-element.89.refs_1_, bf16[96,128]{1,0:T(8,128)(2,1)S(1)} %get-tuple-element.90.refs_2_, ...), custom_call_target="tpu_custom_call" | custom-call | tf_op jit(solution)/shard_map/pallas_call | solution.py:543
  104.6 0.1 collective-permute-done.1.refs_0_
  104.7 1.2 %shard_map.157 = (f32[27,96,96]{2,1,0:T(8,128)}, f32[27,96,96]{2,1,0:T(8,128)}) custom-call(bf16[2048,128]{1,0:T(8,128)(2,1)S(1)} %collective-permute-done.1.refs_0_, f32[27,96,96]{2,1,0:T(8,128)} %get-tuple-element.94.refs_1_, f32[27,96,96]{2,1,0:T(8,128)} %get-tuple-element.95.refs_2_), custom_call_target="tpu_custom_call", output_to_operand_aliasing={{0}: (1, {}), {1}: (2, {})} | custom-call | tf_op jit(solution)/shard_map/pallas_call | solution.py:543
  (14 shorter events, 0.0 us)
Async XLA Ops:
  3.0 15.5 %all-to-all-start = ((bf16[32,16,128]{2,1,0:T(8,128)(2,1)}), bf16[32,16,128]{2,1,0:T(8,128)(2,1)S(1)}, u32[]{:S(2)}, u32[]{:S(2)}) async-start(bf16[32,16,128]{2,1,0:T(8,128)(2,1)} %get-tuple-element.52), calls=%async_computation | async-start | bytes 262144 | tf_op jit(solution)/shard_map/all_to_all | solution.py:555
  18.6 11.1 %copy-start.3 = (f32[96]{0:T(128)S(1)}, f32[96]{0:T(128)}, u32[]{:S(2)}) copy-start(f32[96]{0:T(128)} %param.17) | copy-start | bytes 1156
  18.6 11.1 %copy-start.4 = (f32[96]{0:T(128)S(1)}, f32[96]{0:T(128)}, u32[]{:S(2)}) copy-start(f32[96]{0:T(128)} %param.18) | copy-start | bytes 1156
  29.7 10.4 %copy-start.2 = (bf16[96,128]{1,0:T(8,128)(2,1)S(1)}, bf16[96,128]{1,0:T(8,128)(2,1)}, u32[]{:S(2)}) copy-start(bf16[96,128]{1,0:T(8,128)(2,1)} %refs_4_.1) | copy-start | bytes 73732
  29.7 10.4 %copy-start.5 = (f32[96]{0:T(128)S(1)}, f32[96]{0:T(128)}, u32[]{:S(2)}) copy-start(f32[96]{0:T(128)} %param.19) | copy-start | bytes 1156
  29.7 10.4 %copy-start.6 = (f32[96]{0:T(128)S(1)}, f32[96]{0:T(128)}, u32[]{:S(2)}) copy-start(f32[96]{0:T(128)} %param.20) | copy-start | bytes 1156
  31.0 18.5 %copy-start = (bf16[27,96,96]{2,1,0:T(8,128)(2,1)S(1)}, bf16[27,96,96]{2,1,0:T(8,128)(2,1)}, u32[]{:S(2)}) copy-start(bf16[27,96,96]{2,1,0:T(8,128)(2,1)} %param.16) | copy-start | bytes 1492996
  51.0 11.1 %copy-start.1 = (bf16[27,96,96]{2,1,0:T(8,128)(2,1)S(1)}, bf16[27,96,96]{2,1,0:T(8,128)(2,1)}, u32[]{:S(2)}) copy-start(bf16[27,96,96]{2,1,0:T(8,128)(2,1)} %param.15) | copy-start | bytes 1492996
  61.9 2.0 %collective-permute-start = (bf16[2048,128]{1,0:T(8,128)(2,1)S(1)}, bf16[2048,128]{1,0:T(8,128)(2,1)S(1)}, u32[]{:S(2)}, u32[]{:S(2)}) collective-permute-start(bf16[2048,128]{1,0:T(8,128)(2,1)S(1)} %get-tuple-element.86), channel_id=1, source_target_pairs={{0,1},{1,0},{2,3},{3,2},{4,5},{5,4},{6,7},{7,6},{8,9},{9,8},{10,11... | collective-permute-start | bytes 1572872 | tf_op jit(solution)/shard_map/ppermute | solution.py:560
  102.8 1.9 %collective-permute-start.1 = (bf16[2048,128]{1,0:T(8,128)(2,1)S(1)}, bf16[2048,128]{1,0:T(8,128)(2,1)S(1)}, u32[]{:S(2)}, u32[]{:S(2)}) collective-permute-start(bf16[2048,128]{1,0:T(8,128)(2,1)S(1)} %bitcast.11), channel_id=1, source_target_pairs={{0,1},{1,0},{2,3},{3,2},{4,5},{5,4},{6,7},{7,6},{8,9},{9,8},{10,11... | collective-permute-start | bytes 1572872 | tf_op jit(solution)/shard_map/ppermute | solution.py:560

commit v5 on v4

--- a/solution.py
+++ b/solution.py
@@ -134,15 +134,14 @@
 
 
 def open_kernel(
-    grid, counts_ref, features_hbm, send_hbm, buf_ref, start_ref, place_ref, features_ref, send_ref, sems
-):
-    copies = [
-        pltpu.make_async_copy(features_hbm, features_ref, sems.at[0]),
-        pltpu.make_async_copy(send_hbm, send_ref, sems.at[1]),
-    ]
+    grid, counts_ref, features_hbm, send_hbm, map_hbm, one_hbm,
+    buf_ref, start_ref, place_ref, hot_ref, one_ref, features_ref, send_ref, map_ref, sems,
+):
+    pairs = ((features_hbm, features_ref), (send_hbm, send_ref), (map_hbm, map_ref), (one_hbm, one_ref))
+    copies = [pltpu.make_async_copy(src, dst, sems.at[at]) for at, (src, dst) in enumerate(pairs)]
     for copy in copies:
         copy.start()
-    for copy in copies:
+    for copy in copies[:2]:
         copy.wait()
     width = send_ref.shape[1]
     send = send_ref[...].astype(F32).astype(BF16)
@@ -158,26 +157,13 @@
     extra = jnp.where(iota((LANES - 96, LANES), 0) == 0, valid, 0.0)
     rows = nt(place, jnp.concatenate([start, extra], axis=0).astype(BF16))
     put_blocks(buf_ref, rows, grid, 1, width)
-
-
-def prepare_kernel(
-    map_hbm, one_hbm, two_hbm, hot_ref, one_t_ref, two_t_ref, map_ref, one_ref, two_ref, sems
-):
-    pairs = ((map_hbm, map_ref), (one_hbm, one_ref), (two_hbm, two_ref))
-    copies = [pltpu.make_async_copy(src, dst, sems.at[at]) for at, (src, dst) in enumerate(pairs)]
-    for copy in copies:
-        copy.start()
-    copies[0].wait()
-    table = hot_ref.shape[0]
-    sub = iota((table, LANES), 0)
+    copies[2].wait()
+    sub = iota((hot_ref.shape[0], LANES), 0)
     for k in range(map_ref.shape[0]):
-        part = slice(k * LANES, (k + 1) * LANES)
-        hot_ref[:, part] = jnp.where(sub == map_ref[k : k + 1, :], 1.0, 0.0).astype(BF16)
-    unit = eye(one_ref.shape[1])
-    copies[1].wait()
-    one_t_ref[...] = nt(unit, one_ref[...]).astype(BF16)
-    copies[2].wait()
-    two_t_ref[...] = nt(unit, two_ref[...]).astype(BF16)
+        hot_ref[:, k * LANES : (k + 1) * LANES] = jnp.where(
+            sub == map_ref[k : k + 1, :], 1.0, 0.0
+        ).astype(BF16)
+    copies[3].wait()
 
 
 def gather(tables, hot_ref, taken_refs):
@@ -190,9 +176,11 @@
             ]
 
 
-def gather_convolve(table, hot_ref, weight_t_ref, taken_ref):
+def gather_convolve(table, hot_ref, weight_ref, taken_ref):
     gather([table], hot_ref, [taken_ref])
-    return nn(weight_t_ref[...], taken_ref[...])
+    return lax.dot_general(
+        weight_ref[...], taken_ref[...], (((0,), (0,)), ((), ())), preferred_element_type=F32
+    )
 
 
 def first_kernel(
@@ -583,31 +571,23 @@
     ]
 
     taken = ((flat, LANES), BF16)
-    buf, start, place = call(
+    buf, start, place, hot, one_near = call(
         functools.partial(open_kernel, grid),
-        [((devices, width, LANES), BF16), (full, BF16), (square, BF16)],
-        counts, features, send_rows, smem=1, hbm=(1, 2),
+        [
+            ((devices, width, LANES), BF16), (full, BF16), (square, BF16),
+            ((table, offsets * LANES), BF16), (one_flat.shape, BF16),
+        ],
+        counts, features, send_rows, kernel_map, one_flat, smem=1, hbm=(1, 2, 3, 4),
         scratch=[
-            pltpu.VMEM(full, BF16), pltpu.VMEM(send_rows.shape, jnp.int32), pltpu.SemaphoreType.DMA((2,)),
+            pltpu.VMEM(full, BF16), pltpu.VMEM(send_rows.shape, jnp.int32),
+            pltpu.VMEM(kernel_map.shape, jnp.int32), pltpu.SemaphoreType.DMA((4,)),
         ],
     )
     buf = to_all(buf)
-    hot, one_t, two_t = call(
-        prepare_kernel,
-        [
-            ((table, offsets * LANES), BF16),
-            ((channels, flat), BF16), ((channels, flat), BF16),
-        ],
-        kernel_map, one_flat, two_flat, hbm=(0, 1, 2),
-        scratch=[
-            pltpu.VMEM(kernel_map.shape, jnp.int32), pltpu.VMEM((flat, channels), BF16),
-            pltpu.VMEM((flat, channels), BF16), pltpu.SemaphoreType.DMA((3,)),
-        ],
-    )
     buf, hidden_one, taken_zero, flag = call(
         functools.partial(first_kernel, grid),
         [((devices, width, LANES), BF16), (full, F32), taken, (square, F32)],
-        counts, buf, start, hot, one_t, place, smem=1,
+        counts, buf, start, hot, one_near, place, smem=1,
     )
     buf = to_all(buf)
     buf, hidden_two, taken_act, norm_one, slope_one, halo_slope, halo_cross, const_one, taken_zero = call(
@@ -616,7 +596,7 @@
             ((devices, 2, LANES), F32), (full, F32), taken, (full, F32), (full, F32),
             (square, F32), (square, F32), ((8, LANES), F32),
         ],
-        counts, buf, hidden_one, flag, scale_one, bias_one, hot, two_t,
+        counts, buf, hidden_one, flag, scale_one, bias_one, hot, two_flat,
         smem=1, scratch=[pltpu.VMEM((devices, LANES), F32)], carry=[taken_zero],
     )
     buf = to_all(buf)

time: 106 us -> 106 us (level)
  blocking collectives: 76.5 us -> 91.8 us
  starting transfers between devices: 7.61 us -> 0.31 us
  waiting for transfers between devices: 6.7 us -> 0.33 us
  Pallas kernels: 13.6 us -> 11.5 us
    all_to_all x6 -> x7, blocking collectives: 76.5 us -> 91.8 us  [to_all(): return lax.all_to_all(x, AXES, 0, 0)]
    all_to_all x1 -> x0, starting transfers between devices: 7.3 us -> none  [to_all(): return lax.all_to_all(x, AXES, 0, 0)]
    all_to_all x1 -> x0, waiting for transfers between devices: 6.36 us -> none  [to_all(): return lax.all_to_all(x, AXES, 0, 0)]
    pallas_call x12 -> x11, Pallas kernels: 13.6 us -> 11.5 us  [call(): pl.pallas_call(body, out_shape=tuple((jax.ShapeDtypeStruct(shape, dtype)...]
  transfers between devices with their start and end apart: 3 -> 2, of which waited for: 3 -> 2; matrix products, arithmetic and copies ran while one was open for 0% -> 0% of each run, Pallas kernels for 5% -> 3%
where the time goes in v5:
time: 106 us; the launch traced here: 105 us
  blocking collectives  91.8 us (87%)
  Pallas kernels  11.5 us (11%)
  between operations  1.39 us (1%)
    all_to_all x7, blocking collectives, to_all(): return lax.all_to_all(x, AXES, 0, 0)  91.8 us
    pallas_call x11, Pallas kernels, call(): pl.pallas_call(body, out_shape=tuple((jax.ShapeDtypeStruct(shape, dtype)...  11.5 us
  transfers between devices with their start and end apart: 2, of which 2 were waited for; matrix products, arithmetic and copies ran while one was open for 0% of the time, Pallas kernels for 3%

profile of v5, /device:TPU:0, one launch (start us, length us, event | category | flops | bytes accessed | tf_op | source)
XLA Modules:
  0.0 105.4 jit_solution(11004048069446786031)
XLA Ops:
  1.3 1.5 %shard_map.146 = (bf16[32,16,128]{2,1,0:T(8,128)(2,1)S(1)}, bf16[96,128]{1,0:T(8,128)(2,1)S(1)}, bf16[128,128]{1,0:T(8,128)(2,1)S(1)}, bf16[256,3456]{1,0:T(8,128)(2,1)S(1)}, bf16[2592,96]{1,0:T(8,128)(2,1)S(1)}) custom-call(s32[1]{0:T(128)S(6)} %copy.30.refs_0_, bf16[96,128]{1,0:T(8,128)(2,1)} %refs_1_.1, s32[8,16]{1,0:T(8,128)} %refs_2_.1, ...), custom_call_target="tpu_custom_call" | custom-call | tf_op jit(solution)/shard_map/pallas_call | solution.py:531
  2.8 15.3 %all_to_all.35.refs_1_ = bf16[32,16,128]{2,1,0:T(8,128)(2,1)S(1)} all-to-all(bf16[32,16,128]{2,1,0:T(8,128)(2,1)S(1)} %get-tuple-element.51), channel_id=1, replica_groups=mesh['gx'=8,'gy'=4] {'gx','gy'}, dimensions={0} | all-to-all | bytes 262144 | tf_op jit(solution)/shard_map/all_to_all | solution.py:543
  18.1 1.1 %shard_map.147 = (bf16[32,16,128]{2,1,0:T(8,128)(2,1)S(1)}, f32[96,128]{1,0:T(8,128)S(1)}, bf16[2592,128]{1,0:T(8,128)(2,1)S(1)}, f32[128,128]{1,0:T(8,128)S(1)}) custom-call(s32[1]{0:T(128)S(6)} %copy.30.refs_0_, bf16[32,16,128]{2,1,0:T(8,128)(2,1)S(1)} %all_to_all.35.refs_1_, bf16[96,128]{1,0:T(8,128)(2,1)S(1)} %get-tuple-element.52.refs_2_.refs_3_, ...), custom_call_target="tpu_custom_call" | custom-call | tf_op jit(solution)/shard_map/pallas_call | solution.py:531
  19.2 10.0 %all_to_all.36.refs_1_ = bf16[32,16,128]{2,1,0:T(8,128)(2,1)S(1)} all-to-all(bf16[32,16,128]{2,1,0:T(8,128)(2,1)S(1)} %get-tuple-element.56), channel_id=1, replica_groups=mesh['gx'=8,'gy'=4] {'gx','gy'}, dimensions={0} | all-to-all | bytes 262144 | tf_op jit(solution)/shard_map/all_to_all | solution.py:543
  29.2 0.0 copy-start.2
  29.3 0.0 copy-start.3
  29.3 0.0 copy-start.4
  29.3 1.3 %shard_map.148 = (f32[32,2,128]{2,1,0:T(2,128)S(1)}, f32[96,128]{1,0:T(8,128)S(1)}, bf16[2592,128]{1,0:T(8,128)(2,1)S(1)}, f32[96,128]{1,0:T(8,128)S(1)}, f32[96...) custom-call(s32[1]{0:T(128)S(6)} %copy.30.refs_0_, ...), custom_call_target="tpu_custom_call", output_to_operand_aliasing={{8}: (8, {})} | custom-call | tf_op jit(solution)/shard_map/pallas_call | solution.py:531
  30.6 9.0 %all_to_all.37.refs_1_ = f32[32,2,128]{2,1,0:T(2,128)S(1)} all-to-all(f32[32,2,128]{2,1,0:T(2,128)S(1)} %get-tuple-element.60), channel_id=1, replica_groups=mesh['gx'=8,'gy'=4] {'gx','gy'}, dimensions={0} | all-to-all | bytes 65536 | tf_op jit(solution)/shard_map/all_to_all | solution.py:543
  39.6 0.5 shard_map.149
  40.1 8.9 %all_to_all.38.refs_1_ = f32[32,2,128]{2,1,0:T(2,128)S(1)} all-to-all(f32[32,2,128]{2,1,0:T(2,128)S(1)} %get-tuple-element.64), channel_id=1, replica_groups=mesh['gx'=8,'gy'=4] {'gx','gy'}, dimensions={0} | all-to-all | bytes 65536 | tf_op jit(solution)/shard_map/all_to_all | solution.py:543
  49.0 1.5 %shard_map.150 = (bf16[32,16,128]{2,1,0:T(8,128)(2,1)S(1)}, bf16[96,128]{1,0:T(8,128)(2,1)S(1)}, f32[96,128]{1,0:T(8,128)S(1)}, f32[2,128]{1,0:T(2,128)S(1)}, bf...) custom-call(s32[1]{0:T(128)S(6)} %copy.30.refs_0_, ...), custom_call_target="tpu_custom_call", output_to_operand_aliasing={{4}: (11, {}), {5}: (12, {})} | custom-call | tf_op jit(solution)/shard_map/pallas_call | solution.py:531
  50.5 10.1 %all_to_all.39.refs_1_ = bf16[32,16,128]{2,1,0:T(8,128)(2,1)S(1)} all-to-all(bf16[32,16,128]{2,1,0:T(8,128)(2,1)S(1)} %get-tuple-element.74), channel_id=1, replica_groups=mesh['gx'=8,'gy'=4] {'gx','gy'}, dimensions={0} | all-to-all | bytes 262144 | tf_op jit(solution)/shard_map/all_to_all | solution.py:543
  60.6 0.7 shard_map.151
  61.3 0.3 collective-permute-start
  61.6 1.4 %shard_map.152 = (f32[96,128]{1,0:T(8,128)S(1)}, bf16[128,128]{1,0:T(8,128)(2,1)S(1)}, f32[2048,128]{1,0:T(8,128)S(1)}) custom-call(bf16[96,128]{1,0:T(8,128)(2,1)S(1)} %get-tuple-element.81.refs_0_, bf16[2592,96]{1,0:T(8,128)(2,1)S(1)} %bitcast.10, bf16[256,3456]{1,0:T(8,128)(2,1)S(1)} %get-tuple-element.53.refs_3_.refs_6_.refs_2_, ...), custom_call_target="tpu_custom_call" | custom-call | tf_op jit(solution)/shard_map/pallas_call | solution.py:531
  63.1 0.3 collective-permute-done.refs_2_
  63.3 0.1 shard_map.153
  63.5 19.6 %all_to_all.40.refs_1_ = bf16[32,80,128]{2,1,0:T(8,128)(2,1)S(1)} all-to-all(bf16[32,80,128]{2,1,0:T(8,128)(2,1)S(1)} %shard_map.153), channel_id=1, replica_groups=mesh['gx'=8,'gy'=4] {'gx','gy'}, dimensions={0} | all-to-all | bytes 1310720 | tf_op jit(solution)/shard_map/all_to_all | solution.py:543
  83.1 0.4 shard_map.154
  83.5 18.8 %all_to_all.41 = bf16[32,64,128]{2,1,0:T(8,128)(2,1)S(1)} all-to-all(bf16[32,64,128]{2,1,0:T(8,128)(2,1)S(1)} %get-tuple-element.86), channel_id=1, replica_groups=mesh['gx'=8,'gy'=4] {'gx','gy'}, dimensions={0} | all-to-all | bytes 1048576 | tf_op jit(solution)/shard_map/all_to_all | solution.py:543
  102.3 1.8 %shard_map.155 = (f32[27,96,96]{2,1,0:T(8,128)}, f32[27,96,96]{2,1,0:T(8,128)}, bf16[96,128]{1,0:T(8,128)(2,1)}, bf16[96,128]{1,0:T(8,128)(2,1)}, f32[4,96]{1,0:T(4,128)}) custom-call(bf16[2048,128]{1,0:T(8,128)(2,1)S(1)} %bitcast.12, bf16[96,128]{1,0:T(8,128)(2,1)S(1)} %get-tuple-element.87.refs_1_, bf16[96,128]{1,0:T(8,128)(2,1)S(1)} %get-tuple-element.88.refs_2_, ...), custom_call_target="tpu_custom_call" | custom-call | tf_op jit(solution)/shard_map/pallas_call | solution.py:531
  104.1 0.1 collective-permute-done.1.refs_0_
  104.2 1.2 %shard_map.156 = (f32[27,96,96]{2,1,0:T(8,128)}, f32[27,96,96]{2,1,0:T(8,128)}) custom-call(bf16[2048,128]{1,0:T(8,128)(2,1)S(1)} %collective-permute-done.1.refs_0_, f32[27,96,96]{2,1,0:T(8,128)} %get-tuple-element.92.refs_1_, f32[27,96,96]{2,1,0:T(8,128)} %get-tuple-element.93.refs_2_), custom_call_target="tpu_custom_call", output_to_operand_aliasing={{0}: (1, {}), {1}: (2, {})} | custom-call | tf_op jit(solution)/shard_map/pallas_call | solution.py:531
  (12 shorter events, 0.0 us)
Async XLA Ops:
  18.1 11.1 %copy-start = (bf16[27,96,96]{2,1,0:T(8,128)(2,1)S(1)}, bf16[27,96,96]{2,1,0:T(8,128)(2,1)}, u32[]{:S(2)}) copy-start(bf16[27,96,96]{2,1,0:T(8,128)(2,1)} %param.16) | copy-start | bytes 1492996
  18.1 11.1 %copy-start.5 = (f32[96]{0:T(128)S(1)}, f32[96]{0:T(128)}, u32[]{:S(2)}) copy-start(f32[96]{0:T(128)} %param.17) | copy-start | bytes 1156
  18.1 11.1 %copy-start.6 = (f32[96]{0:T(128)S(1)}, f32[96]{0:T(128)}, u32[]{:S(2)}) copy-start(f32[96]{0:T(128)} %param.18) | copy-start | bytes 1156
  29.2 10.4 %copy-start.2 = (bf16[96,128]{1,0:T(8,128)(2,1)S(1)}, bf16[96,128]{1,0:T(8,128)(2,1)}, u32[]{:S(2)}) copy-start(bf16[96,128]{1,0:T(8,128)(2,1)} %refs_4_.1) | copy-start | bytes 73732
  29.3 10.3 %copy-start.3 = (f32[96]{0:T(128)S(1)}, f32[96]{0:T(128)}, u32[]{:S(2)}) copy-start(f32[96]{0:T(128)} %param.19) | copy-start | bytes 1156
  29.3 10.3 %copy-start.4 = (f32[96]{0:T(128)S(1)}, f32[96]{0:T(128)}, u32[]{:S(2)}) copy-start(f32[96]{0:T(128)} %param.20) | copy-start | bytes 1156
  50.5 11.1 %copy-start.1 = (bf16[27,96,96]{2,1,0:T(8,128)(2,1)S(1)}, bf16[27,96,96]{2,1,0:T(8,128)(2,1)}, u32[]{:S(2)}) copy-start(bf16[27,96,96]{2,1,0:T(8,128)(2,1)} %param.15) | copy-start | bytes 1492996
  61.3 2.0 %collective-permute-start = (bf16[2048,128]{1,0:T(8,128)(2,1)S(1)}, bf16[2048,128]{1,0:T(8,128)(2,1)S(1)}, u32[]{:S(2)}, u32[]{:S(2)}) collective-permute-start(bf16[2048,128]{1,0:T(8,128)(2,1)S(1)} %get-tuple-element.84), channel_id=1, source_target_pairs={{0,1},{1,0},{2,3},{3,2},{4,5},{5,4},{6,7},{7,6},{8,9},{9,8},{10,11... | collective-permute-start | bytes 1572872 | tf_op jit(solution)/shard_map/ppermute | solution.py:548
  102.3 1.9 %collective-permute-start.1 = (bf16[2048,128]{1,0:T(8,128)(2,1)S(1)}, bf16[2048,128]{1,0:T(8,128)(2,1)S(1)}, u32[]{:S(2)}, u32[]{:S(2)}) collective-permute-start(bf16[2048,128]{1,0:T(8,128)(2,1)S(1)} %bitcast.11), channel_id=1, source_target_pairs={{0,1},{1,0},{2,3},{3,2},{4,5},{5,4},{6,7},{7,6},{8,9},{9,8},{10,11... | collective-permute-start | bytes 1572872 | tf_op jit(solution)/shard_map/ppermute | solution.py:548

commit v6 on v5

--- a/solution.py
+++ b/solution.py
@@ -23,12 +23,12 @@
     return lax.dot_general(a, b, (((1,), (1,)), ((), ())), preferred_element_type=F32)
 
 
+def tn(a, b):
+    return lax.dot_general(a, b, (((0,), (0,)), ((), ())), preferred_element_type=F32)
+
+
 def iota(shape, dim):
     return lax.broadcasted_iota(jnp.int32, shape, dim)
-
-
-def eye(size):
-    return jnp.where(iota((size, size), 0) == iota((size, size), 1), 1.0, 0.0).astype(BF16)
 
 
 def sigmoid(v):
@@ -158,11 +158,11 @@
     rows = nt(place, jnp.concatenate([start, extra], axis=0).astype(BF16))
     put_blocks(buf_ref, rows, grid, 1, width)
     copies[2].wait()
-    sub = iota((hot_ref.shape[0], LANES), 0)
+    sub = iota((hot_ref.shape[0], LANES), 0).astype(jnp.int16)
+    columns = map_ref[...].astype(jnp.int16)
+    one, zero = jnp.ones(sub.shape, BF16), jnp.zeros(sub.shape, BF16)
     for k in range(map_ref.shape[0]):
-        hot_ref[:, k * LANES : (k + 1) * LANES] = jnp.where(
-            sub == map_ref[k : k + 1, :], 1.0, 0.0
-        ).astype(BF16)
+        hot_ref[:, k * LANES : (k + 1) * LANES] = jnp.where(sub == columns[k : k + 1, :], one, zero)
     copies[3].wait()
 
 
@@ -178,9 +178,7 @@
 
 def gather_convolve(table, hot_ref, weight_ref, taken_ref):
     gather([table], hot_ref, [taken_ref])
-    return lax.dot_general(
-        weight_ref[...], taken_ref[...], (((0,), (0,)), ((), ())), preferred_element_type=F32
-    )
+    return tn(weight_ref[...], taken_ref[...])
 
 
 def first_kernel(
@@ -189,9 +187,9 @@
 ):
     width = buf_ref.shape[1]
     channels = start_ref.shape[0]
-    halo_rows = take_blocks(buf_ref, grid, -1, width).astype(BF16)
-    flag_ref[...] = jnp.broadcast_to(halo_rows[:, 96:97].astype(F32), (LANES, LANES))
-    halo = nt(eye(LANES), halo_rows)[:channels].astype(BF16)
+    halo_rows = take_blocks(buf_ref, grid, -1, width)
+    flag_ref[...] = jnp.broadcast_to(halo_rows[:, 96:97], (LANES, LANES))
+    halo = halo_rows.T[:channels].astype(BF16)
     table = jnp.concatenate([start_ref[...], halo], axis=1)
     hidden = gather_convolve(table, hot_ref, weight_ref, taken_ref)
     hidden_ref[...] = hidden
@@ -254,7 +252,7 @@
     halo_slope = halo_sig * (1.0 + halo_linear * (1.0 - halo_sig)) * flag
     halo_slope_ref[...] = halo_slope
     halo_cross_ref[...] = halo_slope * halo_normal
-    halo_act = nt(eye(LANES), (halo_linear * halo_sig * flag).astype(BF16))[:channels].astype(BF16)
+    halo_act = (halo_linear * halo_sig * flag).T[:channels].astype(BF16)
 
     table = jnp.concatenate([act, halo_act], axis=1)
     hidden = gather_convolve(table, hot_ref, weight_ref, taken_ref)
@@ -394,8 +392,8 @@
     )
     two = sums_two_ref[...]
     sums_ref[...] = jnp.concatenate([dgain, dbias, two], axis=0)[:, :channels]
-    arrived = nt(eye(LANES), take_blocks(buf_ref, grid, 1, width).astype(BF16))[:channels].astype(BF16)
-    back = table_ref[...] + nn(arrived, place_ref[...])
+    arrived = take_blocks(buf_ref, grid, 1, width).astype(BF16)
+    back = table_ref[...] + tn(arrived, place_ref[...])[:channels]
     grad = row_gradient(back * slope_ref[...], norm_ref[...], const_ref[...], dgain, dbias, valid)
     grad_one_ref[...] = grad
     core = lax.axis_index("gy") % 2
@@ -434,13 +432,9 @@
     out_buf_ref[:, width:, :] = total.reshape(devices, rows, LANES)
 
 
-def seventh_kernel(grid, width, counts_ref, buf_ref, table_ref, place_ref, grad_ref, out_buf_ref, out_ref):
-    channels = table_ref.shape[0]
+def seventh_kernel(grid, width, buf_ref, out_buf_ref, halo_ref):
+    halo_ref[...] = take_blocks(buf_ref, grid, 1, width).astype(BF16)
     devices, rows = buf_ref.shape[0], buf_ref.shape[1] - width
-    valid = valid_lanes(counts_ref)
-    arrived = nt(eye(LANES), take_blocks(buf_ref, grid, 1, width).astype(BF16))[:channels].astype(BF16)
-    back = table_ref[...] + nn(arrived, place_ref[...])
-    out_ref[...] = ((back + grad_ref[...]) * valid).astype(BF16)
     pieces = []
     for core in range(2):
         total = jnp.zeros((rows, LANES), F32)
@@ -478,11 +472,18 @@
         copy.wait()
 
 
-def own_kernel(own_ref, small_in, more_in, sums_in, one_hbm, two_hbm, small_out, more_out, sums_out, block_ref, sems):
+def own_kernel(
+    counts_ref, own_ref, small_in, sums_in, halo_ref, table_ref, place_ref, grad_ref,
+    one_hbm, two_hbm, small_hbm, sums_hbm, more_hbm, more_ref, block_ref, sems, small_sems,
+):
     core = lax.axis_index("gy") % 2
-    small_out[...] = small_in[...]
-    more_out[...] = more_in[...]
-    sums_out[...] = sums_in[...]
+    channels = table_ref.shape[0]
+    back = table_ref[...] + tn(halo_ref[...], place_ref[...])[:channels]
+    more_ref[...] = ((back + grad_ref[...]) * valid_lanes(counts_ref)).astype(BF16)
+    pairs = ((small_in, small_hbm), (sums_in, sums_hbm), (more_ref, more_hbm))
+    copies = [pltpu.make_async_copy(src, dst, small_sems.at[at]) for at, (src, dst) in enumerate(pairs)]
+    for copy in copies:
+        copy.start()
 
     @pl.when(core == 0)
     def _():
@@ -491,6 +492,9 @@
     @pl.when(core != 0)
     def _():
         unpack(own_ref, two_hbm, block_ref, sems)
+
+    for copy in copies:
+        copy.wait()
 
 
 def other_kernel(other_ref, one_in, two_in, one_hbm, two_hbm, block_ref, sems):
@@ -631,19 +635,20 @@
         halo_one, keep, got,
     )
     buf = to_all(buf)
-    buf, grad_features = call(
+    buf, halo = call(
         functools.partial(seventh_kernel, grid, width),
-        [((devices, piece, LANES), BF16), (full, BF16)],
-        counts, buf, table_one, place, grad_sum, smem=1,
+        [((devices, piece, LANES), BF16), (square, BF16)],
+        buf,
     )
     own = to_all(buf).reshape(packed, LANES)
     other = swap_core(own)
     weights = [(weight_one.shape, F32), (weight_two.shape, F32)]
     blocks = [pltpu.VMEM(weight_one.shape, F32), pltpu.SemaphoreType.DMA((13,))]
-    grad_weight_one, grad_weight_two, output, grad_features, grad_norms = call(
+    grad_weight_one, grad_weight_two, output, grad_norms, grad_features = call(
         own_kernel,
-        weights + [(full, BF16), (full, BF16), ((4, channels), F32)],
-        own, output, grad_features, grad_norms, hbm_outs=(0, 1), scratch=blocks,
+        weights + [(full, BF16), ((4, channels), F32), (full, BF16)],
+        counts, own, output, grad_norms, halo, table_one, place, grad_sum, smem=1, hbm_outs=(0, 1, 2, 3, 4),
+        scratch=[pltpu.VMEM(full, BF16)] + blocks + [pltpu.SemaphoreType.DMA((3,))],
     )
     grad_weight_one, grad_weight_two = call(
         other_kernel, weights, other, grad_weight_one, grad_weight_two,

time: 106 us -> 105 us (level)
  no operation moved by 1% of the time
where the time goes in v6:
time: 105 us
  blocking collectives  91.8 us (87%)
  Pallas kernels  10.7 us (10%)
  between operations  1.39 us (1%)
    all_to_all x7, blocking collectives, to_all(): return lax.all_to_all(x, AXES, 0, 0)  91.8 us
    pallas_call x11, Pallas kernels, call(): pl.pallas_call(body, out_shape=tuple((jax.ShapeDtypeStruct(shape, dtype)...  10.7 us
  transfers between devices with their start and end apart: 2, of which 2 were waited for; matrix products, arithmetic and copies ran while one was open for 0% of the time, Pallas kernels for 3%

profile of v6, /device:TPU:0, one launch (start us, length us, event | category | flops | bytes accessed | tf_op | source)
XLA Modules:
  0.0 104.9 jit_solution(15650501673472543352)
XLA Ops:
  1.3 1.4 %shard_map.146 = (bf16[32,16,128]{2,1,0:T(8,128)(2,1)S(1)}, bf16[96,128]{1,0:T(8,128)(2,1)S(1)}, bf16[128,128]{1,0:T(8,128)(2,1)S(1)}, bf16[256,3456]{1,0:T(8,128)(2,1)S(1)}, bf16[2592,96]{1,0:T(8,128)(2,1)S(1)}) custom-call(s32[1]{0:T(128)S(6)} %copy.30.refs_0_, bf16[96,128]{1,0:T(8,128)(2,1)} %refs_1_.1, s32[8,16]{1,0:T(8,128)} %refs_2_.1, ...), custom_call_target="tpu_custom_call" | custom-call | tf_op jit(solution)/shard_map/pallas_call | solution.py:535
  2.7 15.3 %all_to_all.35.refs_1_ = bf16[32,16,128]{2,1,0:T(8,128)(2,1)S(1)} all-to-all(bf16[32,16,128]{2,1,0:T(8,128)(2,1)S(1)} %get-tuple-element.51), channel_id=1, replica_groups=mesh['gx'=8,'gy'=4] {'gx','gy'}, dimensions={0} | all-to-all | bytes 262144 | tf_op jit(solution)/shard_map/all_to_all | solution.py:547
  18.0 1.0 shard_map.147
  19.0 10.0 %all_to_all.36.refs_1_ = bf16[32,16,128]{2,1,0:T(8,128)(2,1)S(1)} all-to-all(bf16[32,16,128]{2,1,0:T(8,128)(2,1)S(1)} %get-tuple-element.56), channel_id=1, replica_groups=mesh['gx'=8,'gy'=4] {'gx','gy'}, dimensions={0} | all-to-all | bytes 262144 | tf_op jit(solution)/shard_map/all_to_all | solution.py:547
  29.0 0.0 copy-start.2
  29.1 0.0 copy-start.4
  29.1 1.3 %shard_map.148 = (f32[32,2,128]{2,1,0:T(2,128)S(1)}, f32[96,128]{1,0:T(8,128)S(1)}, bf16[2592,128]{1,0:T(8,128)(2,1)S(1)}, f32[96,128]{1,0:T(8,128)S(1)}, f32[96...) custom-call(s32[1]{0:T(128)S(6)} %copy.30.refs_0_, ...), custom_call_target="tpu_custom_call", output_to_operand_aliasing={{8}: (8, {})} | custom-call | tf_op jit(solution)/shard_map/pallas_call | solution.py:535
  30.4 9.0 %all_to_all.37.refs_1_ = f32[32,2,128]{2,1,0:T(2,128)S(1)} all-to-all(f32[32,2,128]{2,1,0:T(2,128)S(1)} %get-tuple-element.60), channel_id=1, replica_groups=mesh['gx'=8,'gy'=4] {'gx','gy'}, dimensions={0} | all-to-all | bytes 65536 | tf_op jit(solution)/shard_map/all_to_all | solution.py:547
  39.4 0.5 shard_map.149
  39.9 8.9 %all_to_all.38.refs_1_ = f32[32,2,128]{2,1,0:T(2,128)S(1)} all-to-all(f32[32,2,128]{2,1,0:T(2,128)S(1)} %get-tuple-element.64), channel_id=1, replica_groups=mesh['gx'=8,'gy'=4] {'gx','gy'}, dimensions={0} | all-to-all | bytes 65536 | tf_op jit(solution)/shard_map/all_to_all | solution.py:547
  48.9 1.5 %shard_map.150 = (bf16[32,16,128]{2,1,0:T(8,128)(2,1)S(1)}, bf16[96,128]{1,0:T(8,128)(2,1)S(1)}, f32[96,128]{1,0:T(8,128)S(1)}, f32[2,128]{1,0:T(2,128)S(1)}, bf...) custom-call(s32[1]{0:T(128)S(6)} %copy.30.refs_0_, ...), custom_call_target="tpu_custom_call", output_to_operand_aliasing={{4}: (11, {}), {5}: (12, {})} | custom-call | tf_op jit(solution)/shard_map/pallas_call | solution.py:535
  50.3 0.0 copy-start.1
  50.4 10.1 %all_to_all.39.refs_1_ = bf16[32,16,128]{2,1,0:T(8,128)(2,1)S(1)} all-to-all(bf16[32,16,128]{2,1,0:T(8,128)(2,1)S(1)} %get-tuple-element.74), channel_id=1, replica_groups=mesh['gx'=8,'gy'=4] {'gx','gy'}, dimensions={0} | all-to-all | bytes 262144 | tf_op jit(solution)/shard_map/all_to_all | solution.py:547
  60.4 0.7 shard_map.151
  61.2 0.3 collective-permute-start
  61.5 1.4 %shard_map.152 = (f32[96,128]{1,0:T(8,128)S(1)}, bf16[128,128]{1,0:T(8,128)(2,1)S(1)}, f32[2048,128]{1,0:T(8,128)S(1)}) custom-call(bf16[96,128]{1,0:T(8,128)(2,1)S(1)} %get-tuple-element.81.refs_0_, bf16[2592,96]{1,0:T(8,128)(2,1)S(1)} %bitcast.10, bf16[256,3456]{1,0:T(8,128)(2,1)S(1)} %get-tuple-element.53.refs_3_.refs_6_.refs_2_, ...), custom_call_target="tpu_custom_call" | custom-call | tf_op jit(solution)/shard_map/pallas_call | solution.py:535
  62.9 0.3 collective-permute-done.refs_2_
  63.1 0.1 shard_map.153
  63.3 19.6 %all_to_all.40.refs_0_ = bf16[32,80,128]{2,1,0:T(8,128)(2,1)S(1)} all-to-all(bf16[32,80,128]{2,1,0:T(8,128)(2,1)S(1)} %shard_map.153), channel_id=1, replica_groups=mesh['gx'=8,'gy'=4] {'gx','gy'}, dimensions={0} | all-to-all | bytes 1310720 | tf_op jit(solution)/shard_map/all_to_all | solution.py:547
  82.9 0.1 shard_map.154
  83.0 18.8 %all_to_all.41 = bf16[32,64,128]{2,1,0:T(8,128)(2,1)S(1)} all-to-all(bf16[32,64,128]{2,1,0:T(8,128)(2,1)S(1)} %get-tuple-element.85), channel_id=1, replica_groups=mesh['gx'=8,'gy'=4] {'gx','gy'}, dimensions={0} | all-to-all | bytes 1048576 | tf_op jit(solution)/shard_map/all_to_all | solution.py:547
  101.8 1.4 %shard_map.155 = (f32[27,96,96]{2,1,0:T(8,128)}, f32[27,96,96]{2,1,0:T(8,128)}, bf16[96,128]{1,0:T(8,128)(2,1)}, f32[4,96]{1,0:T(4,128)}, bf16[96,128]{1,0:T(8,128)(2,1)}) custom-call(s32[1]{0:T(128)S(6)} %copy.30.refs_0_, bf16[2048,128]{1,0:T(8,128)(2,1)S(1)} %bitcast.12, bf16[96,128]{1,0:T(8,128)(2,1)S(1)} %get-tuple-element.86.refs_2_, ...), custom_call_target="tpu_custom_call" | custom-call | tf_op jit(solution)/shard_map/pallas_call | solution.py:535
  103.3 0.5 collective-permute-done.1.refs_0_
  103.7 1.2 %shard_map.156 = (f32[27,96,96]{2,1,0:T(8,128)}, f32[27,96,96]{2,1,0:T(8,128)}) custom-call(bf16[2048,128]{1,0:T(8,128)(2,1)S(1)} %collective-permute-done.1.refs_0_, f32[27,96,96]{2,1,0:T(8,128)} %get-tuple-element.92.refs_1_, f32[27,96,96]{2,1,0:T(8,128)} %get-tuple-element.93.refs_2_), custom_call_target="tpu_custom_call", output_to_operand_aliasing={{0}: (1, {}), {1}: (2, {})} | custom-call | tf_op jit(solution)/shard_map/pallas_call | solution.py:535
  (12 shorter events, 0.0 us)
Async XLA Ops:
  18.0 11.0 %copy-start = (bf16[27,96,96]{2,1,0:T(8,128)(2,1)S(1)}, bf16[27,96,96]{2,1,0:T(8,128)(2,1)}, u32[]{:S(2)}) copy-start(bf16[27,96,96]{2,1,0:T(8,128)(2,1)} %param.16) | copy-start | bytes 1492996
  18.0 11.0 %copy-start.5 = (f32[96]{0:T(128)S(1)}, f32[96]{0:T(128)}, u32[]{:S(2)}) copy-start(f32[96]{0:T(128)} %param.17) | copy-start | bytes 1156
  18.0 11.0 %copy-start.6 = (f32[96]{0:T(128)S(1)}, f32[96]{0:T(128)}, u32[]{:S(2)}) copy-start(f32[96]{0:T(128)} %param.18) | copy-start | bytes 1156
  29.0 10.4 %copy-start.2 = (bf16[96,128]{1,0:T(8,128)(2,1)S(1)}, bf16[96,128]{1,0:T(8,128)(2,1)}, u32[]{:S(2)}) copy-start(bf16[96,128]{1,0:T(8,128)(2,1)} %refs_4_.1) | copy-start | bytes 73732
  29.1 10.4 %copy-start.3 = (f32[96]{0:T(128)S(1)}, f32[96]{0:T(128)}, u32[]{:S(2)}) copy-start(f32[96]{0:T(128)} %param.19) | copy-start | bytes 1156
  29.1 10.4 %copy-start.4 = (f32[96]{0:T(128)S(1)}, f32[96]{0:T(128)}, u32[]{:S(2)}) copy-start(f32[96]{0:T(128)} %param.20) | copy-start | bytes 1156
  50.3 11.1 %copy-start.1 = (bf16[27,96,96]{2,1,0:T(8,128)(2,1)S(1)}, bf16[27,96,96]{2,1,0:T(8,128)(2,1)}, u32[]{:S(2)}) copy-start(bf16[27,96,96]{2,1,0:T(8,128)(2,1)} %param.15) | copy-start | bytes 1492996
  61.2 2.0 %collective-permute-start = (bf16[2048,128]{1,0:T(8,128)(2,1)S(1)}, bf16[2048,128]{1,0:T(8,128)(2,1)S(1)}, u32[]{:S(2)}, u32[]{:S(2)}) collective-permute-start(bf16[2048,128]{1,0:T(8,128)(2,1)S(1)} %get-tuple-element.84), channel_id=1, source_target_pairs={{0,1},{1,0},{2,3},{3,2},{4,5},{5,4},{6,7},{7,6},{8,9},{9,8},{10,11... | collective-permute-start | bytes 1572872 | tf_op jit(solution)/shard_map/ppermute | solution.py:552
  101.8 1.9 %collective-permute-start.1 = (bf16[2048,128]{1,0:T(8,128)(2,1)S(1)}, bf16[2048,128]{1,0:T(8,128)(2,1)S(1)}, u32[]{:S(2)}, u32[]{:S(2)}) collective-permute-start(bf16[2048,128]{1,0:T(8,128)(2,1)S(1)} %bitcast.11), channel_id=1, source_target_pairs={{0,1},{1,0},{2,3},{3,2},{4,5},{5,4},{6,7},{7,6},{8,9},{9,8},{10,11... | collective-permute-start | bytes 1572872 | tf_op jit(solution)/shard_map/ppermute | solution.py:552

commit v7 on v6

--- a/solution.py
+++ b/solution.py
@@ -73,21 +73,25 @@
     return x
 
 
-def cols_to_rows(cols):
-    lane = iota((cols[0].shape[0], LANES), 1)
-    total = jnp.zeros((cols[0].shape[0], LANES), F32)
-    for at, col in enumerate(cols):
-        total = jnp.where(lane == at, col, total)
-    return pad_to(total, LANES, LANES).T
-
-
-def rows_to_cols(rows):
-    sub = iota((LANES, LANES), 0)
-    total = jnp.zeros((LANES, LANES), F32)
-    for at, row in enumerate(rows):
-        total = jnp.where(sub == at, row, total)
-    total = total.T
-    return [total[:, at : at + 1] for at in range(len(rows))]
+def turn(x):
+    return pad_to(x, LANES, LANES).T
+
+
+def lane_sums(x):
+    return jnp.sum(turn(x), axis=0, keepdims=True)
+
+
+def rows_to_cols(rows, channels):
+    return [jnp.broadcast_to(row, (LANES, LANES)).T[:channels] for row in rows]
+
+
+def centre(hidden, counts_ref):
+    count = counts_ref[0].astype(F32)
+    mask = (iota((LANES, LANES), 0) < counts_ref[0]).astype(F32)
+    turned = turn(hidden)
+    sums = jnp.sum(turned * mask, axis=0, keepdims=True)
+    centred = (turned - sums / count) * mask
+    return sums, centred, jnp.sum(centred * centred, axis=0, keepdims=True)
 
 
 def split3(x):
@@ -193,15 +197,10 @@
     table = jnp.concatenate([start_ref[...], halo], axis=1)
     hidden = gather_convolve(table, hot_ref, weight_ref, taken_ref)
     hidden_ref[...] = hidden
-    valid = valid_lanes(counts_ref)
-    count = counts_ref[0].astype(F32)
-    sums = jnp.sum(hidden * valid, axis=1, keepdims=True)
-    centred = (hidden - sums / count) * valid
-    spread = jnp.sum(centred * centred, axis=1, keepdims=True)
-    stat = cols_to_rows([sums, spread])
-    base = pack_rows(split3(stat[0:1]) + split3(stat[1:2])[:2], count)
+    sums, centred, spread = centre(hidden, counts_ref)
+    base = pack_rows(split3(sums) + split3(spread)[:2], counts_ref[0].astype(F32))
     out_buf_ref[...] = jnp.broadcast_to(base.astype(BF16)[None], out_buf_ref.shape)
-    rows = pad_to(nt(place_ref[...], centred.astype(BF16)), LANES, LANES)
+    rows = nn(place_ref[...], centred.astype(BF16))
     put_blocks(out_buf_ref, rows, grid, 1, width, base)
 
 
@@ -225,7 +224,7 @@
     scale = pad_to(scale_ref[...], 1, LANES)
     bias = pad_to(bias_ref[...], 1, LANES)
     total_row = jnp.broadcast_to(total, (1, LANES))
-    mean_c, rstd_c, scale_c, bias_c = [c[:channels] for c in rows_to_cols([mean, rstd, scale, bias])]
+    mean_c, rstd_c, scale_c, bias_c = rows_to_cols([mean, rstd, scale, bias], channels)
     sub = iota((8, LANES), 0)
     const_ref[...] = jnp.where(sub == 0, scale * rstd, jnp.where(sub == 1, total_row, 0.0))
 
@@ -257,12 +256,9 @@
     table = jnp.concatenate([act, halo_act], axis=1)
     hidden = gather_convolve(table, hot_ref, weight_ref, taken_ref)
     hidden_two_ref[...] = hidden
-    count = counts_ref[0].astype(F32)
-    sums_two = jnp.sum(hidden * valid, axis=1, keepdims=True)
-    centred = (hidden - sums_two / count) * valid
-    spread_two = jnp.sum(centred * centred, axis=1, keepdims=True)
-    stat = cols_to_rows([sums_two, spread_two])[0:2]
-    stat = jnp.where(iota((2, LANES), 1) < 96, stat, count)
+    sums_two, _, spread_two = centre(hidden, counts_ref)
+    stat = jnp.concatenate([sums_two, spread_two], axis=0)
+    stat = jnp.where(iota((2, LANES), 1) < 96, stat, counts_ref[0].astype(F32))
     out_buf_ref[...] = jnp.broadcast_to(stat[None], out_buf_ref.shape)
 
 
@@ -282,7 +278,7 @@
     scale = pad_to(scale_ref[...], 1, LANES)
     bias = pad_to(bias_ref[...], 1, LANES)
     total_row = jnp.broadcast_to(total, (1, LANES))
-    mean_c, rstd_c, scale_c, bias_c = [c[:channels] for c in rows_to_cols([mean, rstd, scale, bias])]
+    mean_c, rstd_c, scale_c, bias_c = rows_to_cols([mean, rstd, scale, bias], channels)
     sub = iota((8, LANES), 0)
     const_ref[...] = jnp.where(sub == 0, scale * rstd, jnp.where(sub == 1, total_row, 0.0))
     valid = valid_lanes(counts_ref)
@@ -293,9 +289,7 @@
     output_ref[...] = (summed * sig * valid).astype(BF16)
     grad = cotangent_ref[...].astype(F32) * valid * (sig * (1.0 + summed * (1.0 - sig)))
     grad_ref[...] = grad
-    dbias = jnp.sum(grad, axis=1, keepdims=True)
-    dgain = jnp.sum(grad * normal * valid, axis=1, keepdims=True)
-    rows = cols_to_rows([dgain, dbias])[0:2]
+    rows = jnp.concatenate([lane_sums(grad * normal * valid), lane_sums(grad)], axis=0)
     out_buf_ref[...] = jnp.broadcast_to(rows[None], out_buf_ref.shape)
 
 
@@ -310,10 +304,10 @@
 
 def row_gradient(grad, normal, const, dgain, dbias, valid):
     channels = grad.shape[0]
-    factor, part_bias, part_gain = rows_to_cols([const[0:1], dbias / const[1:2], dgain / const[1:2]])
-    return (
-        factor[:channels] * (grad - (part_bias[:channels] + normal * part_gain[:channels])) * valid
-    ).astype(BF16)
+    factor, part_bias, part_gain = rows_to_cols(
+        [const[0:1], dbias / const[1:2], dgain / const[1:2]], channels
+    )
+    return (factor * (grad - (part_bias + normal * part_gain)) * valid).astype(BF16)
 
 
 def fourth_kernel(
@@ -331,11 +325,8 @@
     local, halo = scatter(grad, weight_ref, hot_ref)
     table_ref[...] = local
     pulled = local * slope_ref[...]
-    dbias = jnp.sum(pulled, axis=1, keepdims=True)
-    dgain = jnp.sum(pulled * norm_one_ref[...], axis=1, keepdims=True)
-    rows = cols_to_rows([dgain, dbias])
-    dgain = rows[0:1] + jnp.sum(halo * halo_cross_ref[...], axis=0, keepdims=True)
-    dbias = rows[1:2] + jnp.sum(halo * halo_slope_ref[...], axis=0, keepdims=True)
+    dgain = lane_sums(pulled * norm_one_ref[...]) + jnp.sum(halo * halo_cross_ref[...], axis=0, keepdims=True)
+    dbias = lane_sums(pulled) + jnp.sum(halo * halo_slope_ref[...], axis=0, keepdims=True)
     base = pack_rows(split3(dgain)[:2] + split3(dbias)[:2], 0.0)
     out_buf_ref[...] = jnp.broadcast_to(base.astype(BF16)[None], out_buf_ref.shape)
     put_blocks(out_buf_ref, halo, grid, -1, width, base)

time: 105 us -> 105 us (level)
  no operation moved by 1% of the time
where the time goes in v7:
time: 105 us; the launch traced here: 104 us
  blocking collectives  91.8 us (87%)
  Pallas kernels  10 us (10%)
  between operations  1.39 us (1%)
    all_to_all x7, blocking collectives, to_all(): return lax.all_to_all(x, AXES, 0, 0)  91.8 us
    pallas_call x11, Pallas kernels, call(): pl.pallas_call(body, out_shape=tuple((jax.ShapeDtypeStruct(shape, dtype)...  10 us
  transfers between devices with their start and end apart: 2, of which 2 were waited for; matrix products, arithmetic and copies ran while one was open for 0% of the time, Pallas kernels for 3%

profile of v7, /device:TPU:0, one launch (start us, length us, event | category | flops | bytes accessed | tf_op | source)
XLA Modules:
  0.0 104.3 jit_solution(13419591236558550981)
XLA Ops:
  1.3 1.4 %shard_map.146 = (bf16[32,16,128]{2,1,0:T(8,128)(2,1)S(1)}, bf16[96,128]{1,0:T(8,128)(2,1)S(1)}, bf16[128,128]{1,0:T(8,128)(2,1)S(1)}, bf16[256,3456]{1,0:T(8,128)(2,1)S(1)}, bf16[2592,96]{1,0:T(8,128)(2,1)S(1)}) custom-call(s32[1]{0:T(128)S(6)} %copy.30.refs_0_, bf16[96,128]{1,0:T(8,128)(2,1)} %refs_1_.1, s32[8,16]{1,0:T(8,128)} %refs_2_.1, ...), custom_call_target="tpu_custom_call" | custom-call | tf_op jit(solution)/shard_map/pallas_call | solution.py:526
  2.7 15.3 %all_to_all.35.refs_1_ = bf16[32,16,128]{2,1,0:T(8,128)(2,1)S(1)} all-to-all(bf16[32,16,128]{2,1,0:T(8,128)(2,1)S(1)} %get-tuple-element.51), channel_id=1, replica_groups=mesh['gx'=8,'gy'=4] {'gx','gy'}, dimensions={0} | all-to-all | bytes 262144 | tf_op jit(solution)/shard_map/all_to_all | solution.py:538
  18.0 0.9 shard_map.147
  18.9 10.0 %all_to_all.36.refs_1_ = bf16[32,16,128]{2,1,0:T(8,128)(2,1)S(1)} all-to-all(bf16[32,16,128]{2,1,0:T(8,128)(2,1)S(1)} %get-tuple-element.56), channel_id=1, replica_groups=mesh['gx'=8,'gy'=4] {'gx','gy'}, dimensions={0} | all-to-all | bytes 262144 | tf_op jit(solution)/shard_map/all_to_all | solution.py:538
  28.9 0.0 copy-start.2
  29.0 0.0 copy-start.4
  29.0 1.1 %shard_map.148 = (f32[32,2,128]{2,1,0:T(2,128)S(1)}, f32[96,128]{1,0:T(8,128)S(1)}, bf16[2592,128]{1,0:T(8,128)(2,1)S(1)}, f32[96,128]{1,0:T(8,128)S(1)}, f32[96...) custom-call(s32[1]{0:T(128)S(6)} %copy.30.refs_0_, ...), custom_call_target="tpu_custom_call", output_to_operand_aliasing={{8}: (8, {})} | custom-call | tf_op jit(solution)/shard_map/pallas_call | solution.py:526
  30.1 9.0 %all_to_all.37.refs_1_ = f32[32,2,128]{2,1,0:T(2,128)S(1)} all-to-all(f32[32,2,128]{2,1,0:T(2,128)S(1)} %get-tuple-element.60), channel_id=1, replica_groups=mesh['gx'=8,'gy'=4] {'gx','gy'}, dimensions={0} | all-to-all | bytes 65536 | tf_op jit(solution)/shard_map/all_to_all | solution.py:538
  39.1 0.4 shard_map.149
  39.5 8.9 %all_to_all.38.refs_1_ = f32[32,2,128]{2,1,0:T(2,128)S(1)} all-to-all(f32[32,2,128]{2,1,0:T(2,128)S(1)} %get-tuple-element.64), channel_id=1, replica_groups=mesh['gx'=8,'gy'=4] {'gx','gy'}, dimensions={0} | all-to-all | bytes 65536 | tf_op jit(solution)/shard_map/all_to_all | solution.py:538
  48.5 1.3 %shard_map.150 = (bf16[32,16,128]{2,1,0:T(8,128)(2,1)S(1)}, bf16[96,128]{1,0:T(8,128)(2,1)S(1)}, f32[96,128]{1,0:T(8,128)S(1)}, f32[2,128]{1,0:T(2,128)S(1)}, bf...) custom-call(s32[1]{0:T(128)S(6)} %copy.30.refs_0_, ...), custom_call_target="tpu_custom_call", output_to_operand_aliasing={{4}: (11, {}), {5}: (12, {})} | custom-call | tf_op jit(solution)/shard_map/pallas_call | solution.py:526
  49.8 0.0 copy-start.1
  49.8 10.1 %all_to_all.39.refs_1_ = bf16[32,16,128]{2,1,0:T(8,128)(2,1)S(1)} all-to-all(bf16[32,16,128]{2,1,0:T(8,128)(2,1)S(1)} %get-tuple-element.74), channel_id=1, replica_groups=mesh['gx'=8,'gy'=4] {'gx','gy'}, dimensions={0} | all-to-all | bytes 262144 | tf_op jit(solution)/shard_map/all_to_all | solution.py:538
  59.9 0.7 shard_map.151
  60.5 0.3 collective-permute-start
  60.8 1.4 %shard_map.152 = (f32[96,128]{1,0:T(8,128)S(1)}, bf16[128,128]{1,0:T(8,128)(2,1)S(1)}, f32[2048,128]{1,0:T(8,128)S(1)}) custom-call(bf16[96,128]{1,0:T(8,128)(2,1)S(1)} %get-tuple-element.81.refs_0_, bf16[2592,96]{1,0:T(8,128)(2,1)S(1)} %bitcast.10, bf16[256,3456]{1,0:T(8,128)(2,1)S(1)} %get-tuple-element.53.refs_3_.refs_6_.refs_2_, ...), custom_call_target="tpu_custom_call" | custom-call | tf_op jit(solution)/shard_map/pallas_call | solution.py:526
  62.2 0.3 collective-permute-done.refs_2_
  62.5 0.1 shard_map.153
  62.7 19.6 %all_to_all.40.refs_0_ = bf16[32,80,128]{2,1,0:T(8,128)(2,1)S(1)} all-to-all(bf16[32,80,128]{2,1,0:T(8,128)(2,1)S(1)} %shard_map.153), channel_id=1, replica_groups=mesh['gx'=8,'gy'=4] {'gx','gy'}, dimensions={0} | all-to-all | bytes 1310720 | tf_op jit(solution)/shard_map/all_to_all | solution.py:538
  82.3 0.1 shard_map.154
  82.4 18.8 %all_to_all.41 = bf16[32,64,128]{2,1,0:T(8,128)(2,1)S(1)} all-to-all(bf16[32,64,128]{2,1,0:T(8,128)(2,1)S(1)} %get-tuple-element.85), channel_id=1, replica_groups=mesh['gx'=8,'gy'=4] {'gx','gy'}, dimensions={0} | all-to-all | bytes 1048576 | tf_op jit(solution)/shard_map/all_to_all | solution.py:538
  101.2 1.4 %shard_map.155 = (f32[27,96,96]{2,1,0:T(8,128)}, f32[27,96,96]{2,1,0:T(8,128)}, bf16[96,128]{1,0:T(8,128)(2,1)}, f32[4,96]{1,0:T(4,128)}, bf16[96,128]{1,0:T(8,128)(2,1)}) custom-call(s32[1]{0:T(128)S(6)} %copy.30.refs_0_, bf16[2048,128]{1,0:T(8,128)(2,1)S(1)} %bitcast.12, bf16[96,128]{1,0:T(8,128)(2,1)S(1)} %get-tuple-element.86.refs_2_, ...), custom_call_target="tpu_custom_call" | custom-call | tf_op jit(solution)/shard_map/pallas_call | solution.py:526
  102.7 0.5 collective-permute-done.1.refs_0_
  103.1 1.2 %shard_map.156 = (f32[27,96,96]{2,1,0:T(8,128)}, f32[27,96,96]{2,1,0:T(8,128)}) custom-call(bf16[2048,128]{1,0:T(8,128)(2,1)S(1)} %collective-permute-done.1.refs_0_, f32[27,96,96]{2,1,0:T(8,128)} %get-tuple-element.92.refs_1_, f32[27,96,96]{2,1,0:T(8,128)} %get-tuple-element.93.refs_2_), custom_call_target="tpu_custom_call", output_to_operand_aliasing={{0}: (1, {}), {1}: (2, {})} | custom-call | tf_op jit(solution)/shard_map/pallas_call | solution.py:526
  (12 shorter events, 0.0 us)
Async XLA Ops:
  18.0 10.9 %copy-start = (bf16[27,96,96]{2,1,0:T(8,128)(2,1)S(1)}, bf16[27,96,96]{2,1,0:T(8,128)(2,1)}, u32[]{:S(2)}) copy-start(bf16[27,96,96]{2,1,0:T(8,128)(2,1)} %param.16) | copy-start | bytes 1492996
  18.0 10.9 %copy-start.5 = (f32[96]{0:T(128)S(1)}, f32[96]{0:T(128)}, u32[]{:S(2)}) copy-start(f32[96]{0:T(128)} %param.17) | copy-start | bytes 1156
  18.0 10.9 %copy-start.6 = (f32[96]{0:T(128)S(1)}, f32[96]{0:T(128)}, u32[]{:S(2)}) copy-start(f32[96]{0:T(128)} %param.18) | copy-start | bytes 1156
  28.9 10.2 %copy-start.2 = (bf16[96,128]{1,0:T(8,128)(2,1)S(1)}, bf16[96,128]{1,0:T(8,128)(2,1)}, u32[]{:S(2)}) copy-start(bf16[96,128]{1,0:T(8,128)(2,1)} %refs_4_.1) | copy-start | bytes 73732
  29.0 10.2 %copy-start.3 = (f32[96]{0:T(128)S(1)}, f32[96]{0:T(128)}, u32[]{:S(2)}) copy-start(f32[96]{0:T(128)} %param.19) | copy-start | bytes 1156
  29.0 10.2 %copy-start.4 = (f32[96]{0:T(128)S(1)}, f32[96]{0:T(128)}, u32[]{:S(2)}) copy-start(f32[96]{0:T(128)} %param.20) | copy-start | bytes 1156
  49.8 11.0 %copy-start.1 = (bf16[27,96,96]{2,1,0:T(8,128)(2,1)S(1)}, bf16[27,96,96]{2,1,0:T(8,128)(2,1)}, u32[]{:S(2)}) copy-start(bf16[27,96,96]{2,1,0:T(8,128)(2,1)} %param.15) | copy-start | bytes 1492996
  60.5 2.0 %collective-permute-start = (bf16[2048,128]{1,0:T(8,128)(2,1)S(1)}, bf16[2048,128]{1,0:T(8,128)(2,1)S(1)}, u32[]{:S(2)}, u32[]{:S(2)}) collective-permute-start(bf16[2048,128]{1,0:T(8,128)(2,1)S(1)} %get-tuple-element.84), channel_id=1, source_target_pairs={{0,1},{1,0},{2,3},{3,2},{4,5},{5,4},{6,7},{7,6},{8,9},{9,8},{10,11... | collective-permute-start | bytes 1572872 | tf_op jit(solution)/shard_map/ppermute | solution.py:543
  101.2 1.9 %collective-permute-start.1 = (bf16[2048,128]{1,0:T(8,128)(2,1)S(1)}, bf16[2048,128]{1,0:T(8,128)(2,1)S(1)}, u32[]{:S(2)}, u32[]{:S(2)}) collective-permute-start(bf16[2048,128]{1,0:T(8,128)(2,1)S(1)} %bitcast.11), channel_id=1, source_target_pairs={{0,1},{1,0},{2,3},{3,2},{4,5},{5,4},{6,7},{7,6},{8,9},{9,8},{10,11... | collective-permute-start | bytes 1572872 | tf_op jit(solution)/shard_map/ppermute | solution.py:543

commit v8 on v7

--- a/solution.py
+++ b/solution.py
@@ -145,15 +145,14 @@
     copies = [pltpu.make_async_copy(src, dst, sems.at[at]) for at, (src, dst) in enumerate(pairs)]
     for copy in copies:
         copy.start()
-    for copy in copies[:2]:
+    for copy in copies[:3]:
         copy.wait()
     width = send_ref.shape[1]
-    send = send_ref[...].astype(F32).astype(BF16)
-    spread = jnp.where(iota((width, LANES), 1) % width == iota((width, LANES), 0), 1.0, 0.0).astype(BF16)
-    wide = nn(send, spread)
-    wide = jnp.where(iota(wide.shape, 1) // width == iota(wide.shape, 0), wide, 0.0)
-    row = jnp.sum(wide, axis=0, keepdims=True)
-    place = jnp.where(row == iota((LANES, LANES), 0).astype(F32), 1.0, 0.0).T.astype(BF16)
+    send = pad_to(send_ref[...].astype(F32), LANES, LANES).T
+    lane = iota((width, LANES), 1).astype(F32)
+    place = jnp.concatenate(
+        [jnp.where(lane == send[:width, n : n + 1], 1.0, 0.0) for n in range(send_ref.shape[0])], axis=0
+    ).astype(BF16)
     place_ref[...] = place
     valid = valid_lanes(counts_ref)
     start = features_ref[...].astype(F32) * valid
@@ -161,7 +160,6 @@
     extra = jnp.where(iota((LANES - 96, LANES), 0) == 0, valid, 0.0)
     rows = nt(place, jnp.concatenate([start, extra], axis=0).astype(BF16))
     put_blocks(buf_ref, rows, grid, 1, width)
-    copies[2].wait()
     sub = iota((hot_ref.shape[0], LANES), 0).astype(jnp.int16)
     columns = map_ref[...].astype(jnp.int16)
     one, zero = jnp.ones(sub.shape, BF16), jnp.zeros(sub.shape, BF16)
@@ -299,7 +297,7 @@
     offsets = hot_ref.shape[1] // LANES
     wide = jnp.concatenate([terms[k * channels : (k + 1) * channels] for k in range(offsets)], axis=1)
     table = pad_to(nt(hot_ref[...], wide), hot_ref.shape[0], LANES)
-    return table[:LANES].T[:channels], table[LANES : 2 * LANES]
+    return table[:LANES], table[LANES : 2 * LANES]
 
 
 def row_gradient(grad, normal, const, dgain, dbias, valid):
@@ -322,11 +320,11 @@
     sums_ref[...] = both
     grad = row_gradient(grad_ref[...], norm_ref[...], const_ref[...], both[0:1], both[1:2], valid)
     grad_two_ref[...] = grad
+    local_slope, local_cross = turn(slope_ref[...]), turn(slope_ref[...] * norm_one_ref[...])
     local, halo = scatter(grad, weight_ref, hot_ref)
-    table_ref[...] = local
-    pulled = local * slope_ref[...]
-    dgain = lane_sums(pulled * norm_one_ref[...]) + jnp.sum(halo * halo_cross_ref[...], axis=0, keepdims=True)
-    dbias = lane_sums(pulled) + jnp.sum(halo * halo_slope_ref[...], axis=0, keepdims=True)
+    dgain = jnp.sum(local * local_cross + halo * halo_cross_ref[...], axis=0, keepdims=True)
+    dbias = jnp.sum(local * local_slope + halo * halo_slope_ref[...], axis=0, keepdims=True)
+    table_ref[...] = local.T[: norm_ref.shape[0]]
     base = pack_rows(split3(dgain)[:2] + split3(dbias)[:2], 0.0)
     out_buf_ref[...] = jnp.broadcast_to(base.astype(BF16)[None], out_buf_ref.shape)
     put_blocks(out_buf_ref, halo, grid, -1, width, base)
@@ -412,7 +410,7 @@
         store_packed(taken_act_ref, grad_two_ref[...], keep_ref)
 
     local, halo = scatter(grad_ref[...], weight_ref, hot_ref)
-    table_ref[...] = local
+    table_ref[...] = local.T[: grad_ref.shape[0]]
     halo_ref[...] = halo.astype(BF16)
 
 

time: 105 us -> 104 us (level)
  no operation moved by 1% of the time
where the time goes in v8:
time: 104 us
  blocking collectives  91.8 us (88%)
  Pallas kernels  9.78 us (9%)
  between operations  1.39 us (1%)
    all_to_all x7, blocking collectives, to_all(): return lax.all_to_all(x, AXES, 0, 0)  91.8 us
    pallas_call x11, Pallas kernels, call(): pl.pallas_call(body, out_shape=tuple((jax.ShapeDtypeStruct(shape, dtype)...  9.78 us
  transfers between devices with their start and end apart: 2, of which 2 were waited for; matrix products, arithmetic and copies ran while one was open for 0% of the time, Pallas kernels for 3%

profile of v8, /device:TPU:0, one launch (start us, length us, event | category | flops | bytes accessed | tf_op | source)
XLA Modules:
  0.0 104.1 jit_solution(12313532800341333607)
XLA Ops:
  1.3 1.2 %shard_map.146 = (bf16[32,16,128]{2,1,0:T(8,128)(2,1)S(1)}, bf16[96,128]{1,0:T(8,128)(2,1)S(1)}, bf16[128,128]{1,0:T(8,128)(2,1)S(1)}, bf16[256,3456]{1,0:T(8,128)(2,1)S(1)}, bf16[2592,96]{1,0:T(8,128)(2,1)S(1)}) custom-call(s32[1]{0:T(128)S(6)} %copy.30.refs_0_, bf16[96,128]{1,0:T(8,128)(2,1)} %refs_1_.1, s32[8,16]{1,0:T(8,128)} %refs_2_.1, ...), custom_call_target="tpu_custom_call" | custom-call | tf_op jit(solution)/shard_map/pallas_call | solution.py:524
  2.5 15.3 %all_to_all.35.refs_1_ = bf16[32,16,128]{2,1,0:T(8,128)(2,1)S(1)} all-to-all(bf16[32,16,128]{2,1,0:T(8,128)(2,1)S(1)} %get-tuple-element.51), channel_id=1, replica_groups=mesh['gx'=8,'gy'=4] {'gx','gy'}, dimensions={0} | all-to-all | bytes 262144 | tf_op jit(solution)/shard_map/all_to_all | solution.py:536
  17.8 0.9 shard_map.147
  18.8 10.0 %all_to_all.36.refs_1_ = bf16[32,16,128]{2,1,0:T(8,128)(2,1)S(1)} all-to-all(bf16[32,16,128]{2,1,0:T(8,128)(2,1)S(1)} %get-tuple-element.56), channel_id=1, replica_groups=mesh['gx'=8,'gy'=4] {'gx','gy'}, dimensions={0} | all-to-all | bytes 262144 | tf_op jit(solution)/shard_map/all_to_all | solution.py:536
  28.8 0.0 copy-start.2
  28.8 0.0 copy-start.3
  28.8 0.0 copy-start.4
  28.8 1.1 %shard_map.148 = (f32[32,2,128]{2,1,0:T(2,128)S(1)}, f32[96,128]{1,0:T(8,128)S(1)}, bf16[2592,128]{1,0:T(8,128)(2,1)S(1)}, f32[96,128]{1,0:T(8,128)S(1)}, f32[96...) custom-call(s32[1]{0:T(128)S(6)} %copy.30.refs_0_, ...), custom_call_target="tpu_custom_call", output_to_operand_aliasing={{8}: (8, {})} | custom-call | tf_op jit(solution)/shard_map/pallas_call | solution.py:524
  29.9 9.0 %all_to_all.37.refs_1_ = f32[32,2,128]{2,1,0:T(2,128)S(1)} all-to-all(f32[32,2,128]{2,1,0:T(2,128)S(1)} %get-tuple-element.60), channel_id=1, replica_groups=mesh['gx'=8,'gy'=4] {'gx','gy'}, dimensions={0} | all-to-all | bytes 65536 | tf_op jit(solution)/shard_map/all_to_all | solution.py:536
  39.0 0.4 shard_map.149
  39.4 8.9 %all_to_all.38.refs_1_ = f32[32,2,128]{2,1,0:T(2,128)S(1)} all-to-all(f32[32,2,128]{2,1,0:T(2,128)S(1)} %get-tuple-element.64), channel_id=1, replica_groups=mesh['gx'=8,'gy'=4] {'gx','gy'}, dimensions={0} | all-to-all | bytes 65536 | tf_op jit(solution)/shard_map/all_to_all | solution.py:536
  48.3 1.2 %shard_map.150 = (bf16[32,16,128]{2,1,0:T(8,128)(2,1)S(1)}, bf16[96,128]{1,0:T(8,128)(2,1)S(1)}, f32[96,128]{1,0:T(8,128)S(1)}, f32[2,128]{1,0:T(2,128)S(1)}, bf...) custom-call(s32[1]{0:T(128)S(6)} %copy.30.refs_0_, ...), custom_call_target="tpu_custom_call", output_to_operand_aliasing={{4}: (11, {}), {5}: (12, {})} | custom-call | tf_op jit(solution)/shard_map/pallas_call | solution.py:524
  49.6 10.1 %all_to_all.39.refs_1_ = bf16[32,16,128]{2,1,0:T(8,128)(2,1)S(1)} all-to-all(bf16[32,16,128]{2,1,0:T(8,128)(2,1)S(1)} %get-tuple-element.74), channel_id=1, replica_groups=mesh['gx'=8,'gy'=4] {'gx','gy'}, dimensions={0} | all-to-all | bytes 262144 | tf_op jit(solution)/shard_map/all_to_all | solution.py:536
  59.6 0.7 shard_map.151
  60.3 0.3 collective-permute-start
  60.6 1.4 %shard_map.152 = (f32[96,128]{1,0:T(8,128)S(1)}, bf16[128,128]{1,0:T(8,128)(2,1)S(1)}, f32[2048,128]{1,0:T(8,128)S(1)}) custom-call(bf16[96,128]{1,0:T(8,128)(2,1)S(1)} %get-tuple-element.81.refs_0_, bf16[2592,96]{1,0:T(8,128)(2,1)S(1)} %bitcast.10, bf16[256,3456]{1,0:T(8,128)(2,1)S(1)} %get-tuple-element.53.refs_3_.refs_6_.refs_2_, ...), custom_call_target="tpu_custom_call" | custom-call | tf_op jit(solution)/shard_map/pallas_call | solution.py:524
  62.0 0.3 collective-permute-done.refs_2_
  62.3 0.1 shard_map.153
  62.4 19.6 %all_to_all.40.refs_0_ = bf16[32,80,128]{2,1,0:T(8,128)(2,1)S(1)} all-to-all(bf16[32,80,128]{2,1,0:T(8,128)(2,1)S(1)} %shard_map.153), channel_id=1, replica_groups=mesh['gx'=8,'gy'=4] {'gx','gy'}, dimensions={0} | all-to-all | bytes 1310720 | tf_op jit(solution)/shard_map/all_to_all | solution.py:536
  82.0 0.1 shard_map.154
  82.1 18.8 %all_to_all.41 = bf16[32,64,128]{2,1,0:T(8,128)(2,1)S(1)} all-to-all(bf16[32,64,128]{2,1,0:T(8,128)(2,1)S(1)} %get-tuple-element.85), channel_id=1, replica_groups=mesh['gx'=8,'gy'=4] {'gx','gy'}, dimensions={0} | all-to-all | bytes 1048576 | tf_op jit(solution)/shard_map/all_to_all | solution.py:536
  101.0 1.4 %shard_map.155 = (f32[27,96,96]{2,1,0:T(8,128)}, f32[27,96,96]{2,1,0:T(8,128)}, bf16[96,128]{1,0:T(8,128)(2,1)}, f32[4,96]{1,0:T(4,128)}, bf16[96,128]{1,0:T(8,128)(2,1)}) custom-call(s32[1]{0:T(128)S(6)} %copy.30.refs_0_, bf16[2048,128]{1,0:T(8,128)(2,1)S(1)} %bitcast.12, bf16[96,128]{1,0:T(8,128)(2,1)S(1)} %get-tuple-element.86.refs_2_, ...), custom_call_target="tpu_custom_call" | custom-call | tf_op jit(solution)/shard_map/pallas_call | solution.py:524
  102.4 0.5 collective-permute-done.1.refs_0_
  102.9 1.2 %shard_map.156 = (f32[27,96,96]{2,1,0:T(8,128)}, f32[27,96,96]{2,1,0:T(8,128)}) custom-call(bf16[2048,128]{1,0:T(8,128)(2,1)S(1)} %collective-permute-done.1.refs_0_, f32[27,96,96]{2,1,0:T(8,128)} %get-tuple-element.92.refs_1_, f32[27,96,96]{2,1,0:T(8,128)} %get-tuple-element.93.refs_2_), custom_call_target="tpu_custom_call", output_to_operand_aliasing={{0}: (1, {}), {1}: (2, {})} | custom-call | tf_op jit(solution)/shard_map/pallas_call | solution.py:524
  (12 shorter events, 0.0 us)
Async XLA Ops:
  17.8 10.9 %copy-start = (bf16[27,96,96]{2,1,0:T(8,128)(2,1)S(1)}, bf16[27,96,96]{2,1,0:T(8,128)(2,1)}, u32[]{:S(2)}) copy-start(bf16[27,96,96]{2,1,0:T(8,128)(2,1)} %param.16) | copy-start | bytes 1492996
  17.8 10.9 %copy-start.5 = (f32[96]{0:T(128)S(1)}, f32[96]{0:T(128)}, u32[]{:S(2)}) copy-start(f32[96]{0:T(128)} %param.17) | copy-start | bytes 1156
  17.8 10.9 %copy-start.6 = (f32[96]{0:T(128)S(1)}, f32[96]{0:T(128)}, u32[]{:S(2)}) copy-start(f32[96]{0:T(128)} %param.18) | copy-start | bytes 1156
  28.8 10.2 %copy-start.2 = (bf16[96,128]{1,0:T(8,128)(2,1)S(1)}, bf16[96,128]{1,0:T(8,128)(2,1)}, u32[]{:S(2)}) copy-start(bf16[96,128]{1,0:T(8,128)(2,1)} %refs_4_.1) | copy-start | bytes 73732
  28.8 10.2 %copy-start.3 = (f32[96]{0:T(128)S(1)}, f32[96]{0:T(128)}, u32[]{:S(2)}) copy-start(f32[96]{0:T(128)} %param.19) | copy-start | bytes 1156
  28.8 10.2 %copy-start.4 = (f32[96]{0:T(128)S(1)}, f32[96]{0:T(128)}, u32[]{:S(2)}) copy-start(f32[96]{0:T(128)} %param.20) | copy-start | bytes 1156
  49.5 11.0 %copy-start.1 = (bf16[27,96,96]{2,1,0:T(8,128)(2,1)S(1)}, bf16[27,96,96]{2,1,0:T(8,128)(2,1)}, u32[]{:S(2)}) copy-start(bf16[27,96,96]{2,1,0:T(8,128)(2,1)} %param.15) | copy-start | bytes 1492996
  60.3 2.0 %collective-permute-start = (bf16[2048,128]{1,0:T(8,128)(2,1)S(1)}, bf16[2048,128]{1,0:T(8,128)(2,1)S(1)}, u32[]{:S(2)}, u32[]{:S(2)}) collective-permute-start(bf16[2048,128]{1,0:T(8,128)(2,1)S(1)} %get-tuple-element.84), channel_id=1, source_target_pairs={{0,1},{1,0},{2,3},{3,2},{4,5},{5,4},{6,7},{7,6},{8,9},{9,8},{10,11... | collective-permute-start | bytes 1572872 | tf_op jit(solution)/shard_map/ppermute | solution.py:541
  101.0 1.9 %collective-permute-start.1 = (bf16[2048,128]{1,0:T(8,128)(2,1)S(1)}, bf16[2048,128]{1,0:T(8,128)(2,1)S(1)}, u32[]{:S(2)}, u32[]{:S(2)}) collective-permute-start(bf16[2048,128]{1,0:T(8,128)(2,1)S(1)} %bitcast.11), channel_id=1, source_target_pairs={{0,1},{1,0},{2,3},{3,2},{4,5},{5,4},{6,7},{7,6},{8,9},{9,8},{10,11... | collective-permute-start | bytes 1572872 | tf_op jit(solution)/shard_map/ppermute | solution.py:541

commit v9 on v8

--- a/solution.py
+++ b/solution.py
@@ -73,12 +73,23 @@
     return x
 
 
+def halve(x, least):
+    while x.shape[0] > least and x.shape[0] % 2 == 0:
+        rows = x.shape[0] // 2
+        x = x[:rows] + x[rows:]
+    return x
+
+
+def row_sum(x):
+    return jnp.sum(halve(x, 8), axis=0, keepdims=True)
+
+
 def turn(x):
     return pad_to(x, LANES, LANES).T
 
 
 def lane_sums(x):
-    return jnp.sum(turn(x), axis=0, keepdims=True)
+    return row_sum(turn(x))
 
 
 def rows_to_cols(rows, channels):
@@ -89,9 +100,9 @@
     count = counts_ref[0].astype(F32)
     mask = (iota((LANES, LANES), 0) < counts_ref[0]).astype(F32)
     turned = turn(hidden)
-    sums = jnp.sum(turned * mask, axis=0, keepdims=True)
+    sums = row_sum(turned * mask)
     centred = (turned - sums / count) * mask
-    return sums, centred, jnp.sum(centred * centred, axis=0, keepdims=True)
+    return sums, centred, row_sum(centred * centred)
 
 
 def split3(x):
@@ -296,8 +307,8 @@
     terms = nn(weight_ref[...], grad).astype(BF16)
     offsets = hot_ref.shape[1] // LANES
     wide = jnp.concatenate([terms[k * channels : (k + 1) * channels] for k in range(offsets)], axis=1)
-    table = pad_to(nt(hot_ref[...], wide), hot_ref.shape[0], LANES)
-    return table[:LANES], table[LANES : 2 * LANES]
+    halo = pad_to(nt(hot_ref[LANES : 2 * LANES, :], wide), LANES, LANES)
+    return pad_to(nt(hot_ref[:LANES, :], wide), LANES, LANES), halo
 
 
 def row_gradient(grad, normal, const, dgain, dbias, valid):
@@ -316,14 +327,14 @@
     channels = norm_ref.shape[0]
     width = out_buf_ref.shape[1]
     valid = valid_lanes(counts_ref)
-    both = jnp.sum(buf_ref[...], axis=0)
+    both = halve(buf_ref[...], 1)[0]
     sums_ref[...] = both
     grad = row_gradient(grad_ref[...], norm_ref[...], const_ref[...], both[0:1], both[1:2], valid)
     grad_two_ref[...] = grad
     local_slope, local_cross = turn(slope_ref[...]), turn(slope_ref[...] * norm_one_ref[...])
     local, halo = scatter(grad, weight_ref, hot_ref)
-    dgain = jnp.sum(local * local_cross + halo * halo_cross_ref[...], axis=0, keepdims=True)
-    dbias = jnp.sum(local * local_slope + halo * halo_slope_ref[...], axis=0, keepdims=True)
+    dgain = row_sum(local * local_cross + halo * halo_cross_ref[...])
+    dbias = row_sum(local * local_slope + halo * halo_slope_ref[...])
     table_ref[...] = local.T[: norm_ref.shape[0]]
     base = pack_rows(split3(dgain)[:2] + split3(dbias)[:2], 0.0)
     out_buf_ref[...] = jnp.broadcast_to(base.astype(BF16)[None], out_buf_ref.shape)
@@ -377,7 +388,7 @@
     channels = norm_ref.shape[0]
     valid = valid_lanes(counts_ref)
     dgain, dbias = unpack_rows(
-        jnp.sum(buf_ref[...].astype(F32), axis=0, keepdims=True), ((0, 2), (2, 4))
+        halve(buf_ref[...].astype(F32), 1), ((0, 2), (2, 4))
     )
     two = sums_two_ref[...]
     sums_ref[...] = jnp.concatenate([dgain, dbias, two], axis=0)[:, :channels]

time: 104 us -> 104 us (level)
  no operation moved by 1% of the time
where the time goes in v9:
time: 104 us
  blocking collectives  91.8 us (88%)
  Pallas kernels  9.64 us (9%)
  between operations  1.39 us (1%)
    all_to_all x7, blocking collectives, to_all(): return lax.all_to_all(x, AXES, 0, 0)  91.8 us
    pallas_call x11, Pallas kernels, call(): pl.pallas_call(body, out_shape=tuple((jax.ShapeDtypeStruct(shape, dtype)...  9.64 us
  transfers between devices with their start and end apart: 2, of which 2 were waited for; matrix products, arithmetic and copies ran while one was open for 0% of the time, Pallas kernels for 3%

profile of v9, /device:TPU:0, one launch (start us, length us, event | category | flops | bytes accessed | tf_op | source)
XLA Modules:
  0.0 104.0 jit_solution(12002651880489198189)
XLA Ops:
  1.3 1.2 %shard_map.146 = (bf16[32,16,128]{2,1,0:T(8,128)(2,1)S(1)}, bf16[96,128]{1,0:T(8,128)(2,1)S(1)}, bf16[128,128]{1,0:T(8,128)(2,1)S(1)}, bf16[256,3456]{1,0:T(8,128)(2,1)S(1)}, bf16[2592,96]{1,0:T(8,128)(2,1)S(1)}) custom-call(s32[1]{0:T(128)S(6)} %copy.30.refs_0_, bf16[96,128]{1,0:T(8,128)(2,1)} %refs_1_.1, s32[8,16]{1,0:T(8,128)} %refs_2_.1, ...), custom_call_target="tpu_custom_call" | custom-call | tf_op jit(solution)/shard_map/pallas_call | solution.py:535
  2.5 15.3 %all_to_all.35.refs_1_ = bf16[32,16,128]{2,1,0:T(8,128)(2,1)S(1)} all-to-all(bf16[32,16,128]{2,1,0:T(8,128)(2,1)S(1)} %get-tuple-element.51), channel_id=1, replica_groups=mesh['gx'=8,'gy'=4] {'gx','gy'}, dimensions={0} | all-to-all | bytes 262144 | tf_op jit(solution)/shard_map/all_to_all | solution.py:547
  17.8 0.9 shard_map.147
  18.8 10.0 %all_to_all.36.refs_1_ = bf16[32,16,128]{2,1,0:T(8,128)(2,1)S(1)} all-to-all(bf16[32,16,128]{2,1,0:T(8,128)(2,1)S(1)} %get-tuple-element.56), channel_id=1, replica_groups=mesh['gx'=8,'gy'=4] {'gx','gy'}, dimensions={0} | all-to-all | bytes 262144 | tf_op jit(solution)/shard_map/all_to_all | solution.py:547
  28.8 0.0 copy-start.2
  28.8 0.0 copy-start.3
  28.8 0.0 copy-start.4
  28.8 1.1 %shard_map.148 = (f32[32,2,128]{2,1,0:T(2,128)S(1)}, f32[96,128]{1,0:T(8,128)S(1)}, bf16[2592,128]{1,0:T(8,128)(2,1)S(1)}, f32[96,128]{1,0:T(8,128)S(1)}, f32[96...) custom-call(s32[1]{0:T(128)S(6)} %copy.30.refs_0_, ...), custom_call_target="tpu_custom_call", output_to_operand_aliasing={{8}: (8, {})} | custom-call | tf_op jit(solution)/shard_map/pallas_call | solution.py:535
  29.9 9.0 %all_to_all.37.refs_1_ = f32[32,2,128]{2,1,0:T(2,128)S(1)} all-to-all(f32[32,2,128]{2,1,0:T(2,128)S(1)} %get-tuple-element.60), channel_id=1, replica_groups=mesh['gx'=8,'gy'=4] {'gx','gy'}, dimensions={0} | all-to-all | bytes 65536 | tf_op jit(solution)/shard_map/all_to_all | solution.py:547
  39.0 0.4 shard_map.149
  39.3 8.9 %all_to_all.38.refs_1_ = f32[32,2,128]{2,1,0:T(2,128)S(1)} all-to-all(f32[32,2,128]{2,1,0:T(2,128)S(1)} %get-tuple-element.64), channel_id=1, replica_groups=mesh['gx'=8,'gy'=4] {'gx','gy'}, dimensions={0} | all-to-all | bytes 65536 | tf_op jit(solution)/shard_map/all_to_all | solution.py:547
  48.3 1.2 %shard_map.150 = (bf16[32,16,128]{2,1,0:T(8,128)(2,1)S(1)}, bf16[96,128]{1,0:T(8,128)(2,1)S(1)}, f32[96,128]{1,0:T(8,128)S(1)}, f32[2,128]{1,0:T(2,128)S(1)}, bf...) custom-call(s32[1]{0:T(128)S(6)} %copy.30.refs_0_, ...), custom_call_target="tpu_custom_call", output_to_operand_aliasing={{4}: (11, {}), {5}: (12, {})} | custom-call | tf_op jit(solution)/shard_map/pallas_call | solution.py:535
  49.5 10.1 %all_to_all.39.refs_1_ = bf16[32,16,128]{2,1,0:T(8,128)(2,1)S(1)} all-to-all(bf16[32,16,128]{2,1,0:T(8,128)(2,1)S(1)} %get-tuple-element.74), channel_id=1, replica_groups=mesh['gx'=8,'gy'=4] {'gx','gy'}, dimensions={0} | all-to-all | bytes 262144 | tf_op jit(solution)/shard_map/all_to_all | solution.py:547
  59.5 0.6 shard_map.151
  60.2 0.3 collective-permute-start
  60.5 1.4 %shard_map.152 = (f32[96,128]{1,0:T(8,128)S(1)}, bf16[128,128]{1,0:T(8,128)(2,1)S(1)}, f32[2048,128]{1,0:T(8,128)S(1)}) custom-call(bf16[96,128]{1,0:T(8,128)(2,1)S(1)} %get-tuple-element.81.refs_0_, bf16[2592,96]{1,0:T(8,128)(2,1)S(1)} %bitcast.10, bf16[256,3456]{1,0:T(8,128)(2,1)S(1)} %get-tuple-element.53.refs_3_.refs_6_.refs_2_, ...), custom_call_target="tpu_custom_call" | custom-call | tf_op jit(solution)/shard_map/pallas_call | solution.py:535
  61.9 0.3 collective-permute-done.refs_2_
  62.2 0.1 shard_map.153
  62.3 19.6 %all_to_all.40.refs_0_ = bf16[32,80,128]{2,1,0:T(8,128)(2,1)S(1)} all-to-all(bf16[32,80,128]{2,1,0:T(8,128)(2,1)S(1)} %shard_map.153), channel_id=1, replica_groups=mesh['gx'=8,'gy'=4] {'gx','gy'}, dimensions={0} | all-to-all | bytes 1310720 | tf_op jit(solution)/shard_map/all_to_all | solution.py:547
  81.9 0.1 shard_map.154
  82.0 18.8 %all_to_all.41 = bf16[32,64,128]{2,1,0:T(8,128)(2,1)S(1)} all-to-all(bf16[32,64,128]{2,1,0:T(8,128)(2,1)S(1)} %get-tuple-element.85), channel_id=1, replica_groups=mesh['gx'=8,'gy'=4] {'gx','gy'}, dimensions={0} | all-to-all | bytes 1048576 | tf_op jit(solution)/shard_map/all_to_all | solution.py:547
  100.9 1.4 %shard_map.155 = (f32[27,96,96]{2,1,0:T(8,128)}, f32[27,96,96]{2,1,0:T(8,128)}, bf16[96,128]{1,0:T(8,128)(2,1)}, f32[4,96]{1,0:T(4,128)}, bf16[96,128]{1,0:T(8,128)(2,1)}) custom-call(s32[1]{0:T(128)S(6)} %copy.30.refs_0_, bf16[2048,128]{1,0:T(8,128)(2,1)S(1)} %bitcast.12, bf16[96,128]{1,0:T(8,128)(2,1)S(1)} %get-tuple-element.86.refs_2_, ...), custom_call_target="tpu_custom_call" | custom-call | tf_op jit(solution)/shard_map/pallas_call | solution.py:535
  102.3 0.5 collective-permute-done.1.refs_0_
  102.8 1.2 %shard_map.156 = (f32[27,96,96]{2,1,0:T(8,128)}, f32[27,96,96]{2,1,0:T(8,128)}) custom-call(bf16[2048,128]{1,0:T(8,128)(2,1)S(1)} %collective-permute-done.1.refs_0_, f32[27,96,96]{2,1,0:T(8,128)} %get-tuple-element.92.refs_1_, f32[27,96,96]{2,1,0:T(8,128)} %get-tuple-element.93.refs_2_), custom_call_target="tpu_custom_call", output_to_operand_aliasing={{0}: (1, {}), {1}: (2, {})} | custom-call | tf_op jit(solution)/shard_map/pallas_call | solution.py:535
  (12 shorter events, 0.0 us)
Async XLA Ops:
  17.8 10.9 %copy-start = (bf16[27,96,96]{2,1,0:T(8,128)(2,1)S(1)}, bf16[27,96,96]{2,1,0:T(8,128)(2,1)}, u32[]{:S(2)}) copy-start(bf16[27,96,96]{2,1,0:T(8,128)(2,1)} %param.16) | copy-start | bytes 1492996
  17.8 10.9 %copy-start.5 = (f32[96]{0:T(128)S(1)}, f32[96]{0:T(128)}, u32[]{:S(2)}) copy-start(f32[96]{0:T(128)} %param.17) | copy-start | bytes 1156
  17.8 10.9 %copy-start.6 = (f32[96]{0:T(128)S(1)}, f32[96]{0:T(128)}, u32[]{:S(2)}) copy-start(f32[96]{0:T(128)} %param.18) | copy-start | bytes 1156
  28.8 10.2 %copy-start.2 = (bf16[96,128]{1,0:T(8,128)(2,1)S(1)}, bf16[96,128]{1,0:T(8,128)(2,1)}, u32[]{:S(2)}) copy-start(bf16[96,128]{1,0:T(8,128)(2,1)} %refs_4_.1) | copy-start | bytes 73732
  28.8 10.2 %copy-start.3 = (f32[96]{0:T(128)S(1)}, f32[96]{0:T(128)}, u32[]{:S(2)}) copy-start(f32[96]{0:T(128)} %param.19) | copy-start | bytes 1156
  28.8 10.2 %copy-start.4 = (f32[96]{0:T(128)S(1)}, f32[96]{0:T(128)}, u32[]{:S(2)}) copy-start(f32[96]{0:T(128)} %param.20) | copy-start | bytes 1156
  49.5 11.0 %copy-start.1 = (bf16[27,96,96]{2,1,0:T(8,128)(2,1)S(1)}, bf16[27,96,96]{2,1,0:T(8,128)(2,1)}, u32[]{:S(2)}) copy-start(bf16[27,96,96]{2,1,0:T(8,128)(2,1)} %param.15) | copy-start | bytes 1492996
  60.2 2.0 %collective-permute-start = (bf16[2048,128]{1,0:T(8,128)(2,1)S(1)}, bf16[2048,128]{1,0:T(8,128)(2,1)S(1)}, u32[]{:S(2)}, u32[]{:S(2)}) collective-permute-start(bf16[2048,128]{1,0:T(8,128)(2,1)S(1)} %get-tuple-element.84), channel_id=1, source_target_pairs={{0,1},{1,0},{2,3},{3,2},{4,5},{5,4},{6,7},{7,6},{8,9},{9,8},{10,11... | collective-permute-start | bytes 1572872 | tf_op jit(solution)/shard_map/ppermute | solution.py:552
  100.9 1.9 %collective-permute-start.1 = (bf16[2048,128]{1,0:T(8,128)(2,1)S(1)}, bf16[2048,128]{1,0:T(8,128)(2,1)S(1)}, u32[]{:S(2)}, u32[]{:S(2)}) collective-permute-start(bf16[2048,128]{1,0:T(8,128)(2,1)S(1)} %bitcast.11), channel_id=1, source_target_pairs={{0,1},{1,0},{2,3},{3,2},{4,5},{5,4},{6,7},{7,6},{8,9},{9,8},{10,11... | collective-permute-start | bytes 1572872 | tf_op jit(solution)/shard_map/ppermute | solution.py:552

commit v10 on v9

--- a/solution.py
+++ b/solution.py
@@ -181,12 +181,15 @@
 
 def gather(tables, hot_ref, taken_refs):
     channels = tables[0].shape[0]
-    taken = nn(jnp.concatenate(tables, axis=0), hot_ref[...]).astype(BF16)
-    for at, ref in enumerate(taken_refs):
-        for k in range(hot_ref.shape[1] // LANES):
-            ref[k * channels : (k + 1) * channels, :] = taken[
-                at * channels : (at + 1) * channels, k * LANES : (k + 1) * LANES
-            ]
+    table = jnp.concatenate(tables, axis=0)
+    offsets = hot_ref.shape[1] // LANES
+    for first, last in ((0, offsets // 2), (offsets // 2, offsets)):
+        taken = nn(table, hot_ref[:, first * LANES : last * LANES]).astype(BF16)
+        for at, ref in enumerate(taken_refs):
+            for k in range(first, last):
+                ref[k * channels : (k + 1) * channels, :] = taken[
+                    at * channels : (at + 1) * channels, (k - first) * LANES : (k - first + 1) * LANES
+                ]
 
 
 def gather_convolve(table, hot_ref, weight_ref, taken_ref):

time: 104 us -> 104 us (level)
  no operation moved by 1% of the time
where the time goes in v10:
time: 104 us
  blocking collectives  91.8 us (88%)
  Pallas kernels  9.63 us (9%)
  between operations  1.39 us (1%)
    all_to_all x7, blocking collectives, to_all(): return lax.all_to_all(x, AXES, 0, 0)  91.8 us
    pallas_call x11, Pallas kernels, call(): pl.pallas_call(body, out_shape=tuple((jax.ShapeDtypeStruct(shape, dtype)...  9.63 us
  transfers between devices with their start and end apart: 2, of which 2 were waited for; matrix products, arithmetic and copies ran while one was open for 0% of the time, Pallas kernels for 3%

profile of v10, /device:TPU:0, one launch (start us, length us, event | category | flops | bytes accessed | tf_op | source)
XLA Modules:
  0.0 104.0 jit_solution(6569093848377633128)
XLA Ops:
  1.3 1.2 %shard_map.146 = (bf16[32,16,128]{2,1,0:T(8,128)(2,1)S(1)}, bf16[96,128]{1,0:T(8,128)(2,1)S(1)}, bf16[128,128]{1,0:T(8,128)(2,1)S(1)}, bf16[256,3456]{1,0:T(8,128)(2,1)S(1)}, bf16[2592,96]{1,0:T(8,128)(2,1)S(1)}) custom-call(s32[1]{0:T(128)S(6)} %copy.30.refs_0_, bf16[96,128]{1,0:T(8,128)(2,1)} %refs_1_.1, s32[8,16]{1,0:T(8,128)} %refs_2_.1, ...), custom_call_target="tpu_custom_call" | custom-call | tf_op jit(solution)/shard_map/pallas_call | solution.py:538
  2.5 15.3 %all_to_all.35.refs_1_ = bf16[32,16,128]{2,1,0:T(8,128)(2,1)S(1)} all-to-all(bf16[32,16,128]{2,1,0:T(8,128)(2,1)S(1)} %get-tuple-element.51), channel_id=1, replica_groups=mesh['gx'=8,'gy'=4] {'gx','gy'}, dimensions={0} | all-to-all | bytes 262144 | tf_op jit(solution)/shard_map/all_to_all | solution.py:550
  17.8 0.9 shard_map.147
  18.8 10.0 %all_to_all.36.refs_1_ = bf16[32,16,128]{2,1,0:T(8,128)(2,1)S(1)} all-to-all(bf16[32,16,128]{2,1,0:T(8,128)(2,1)S(1)} %get-tuple-element.56), channel_id=1, replica_groups=mesh['gx'=8,'gy'=4] {'gx','gy'}, dimensions={0} | all-to-all | bytes 262144 | tf_op jit(solution)/shard_map/all_to_all | solution.py:550
  28.8 0.0 copy-start.3
  28.8 0.0 copy-start.4
  28.8 1.1 %shard_map.148 = (f32[32,2,128]{2,1,0:T(2,128)S(1)}, f32[96,128]{1,0:T(8,128)S(1)}, bf16[2592,128]{1,0:T(8,128)(2,1)S(1)}, f32[96,128]{1,0:T(8,128)S(1)}, f32[96...) custom-call(s32[1]{0:T(128)S(6)} %copy.30.refs_0_, ...), custom_call_target="tpu_custom_call", output_to_operand_aliasing={{8}: (8, {})} | custom-call | tf_op jit(solution)/shard_map/pallas_call | solution.py:538
  29.9 9.0 %all_to_all.37.refs_1_ = f32[32,2,128]{2,1,0:T(2,128)S(1)} all-to-all(f32[32,2,128]{2,1,0:T(2,128)S(1)} %get-tuple-element.60), channel_id=1, replica_groups=mesh['gx'=8,'gy'=4] {'gx','gy'}, dimensions={0} | all-to-all | bytes 65536 | tf_op jit(solution)/shard_map/all_to_all | solution.py:550
  39.0 0.4 shard_map.149
  39.4 8.9 %all_to_all.38.refs_1_ = f32[32,2,128]{2,1,0:T(2,128)S(1)} all-to-all(f32[32,2,128]{2,1,0:T(2,128)S(1)} %get-tuple-element.64), channel_id=1, replica_groups=mesh['gx'=8,'gy'=4] {'gx','gy'}, dimensions={0} | all-to-all | bytes 65536 | tf_op jit(solution)/shard_map/all_to_all | solution.py:550
  48.3 1.1 %shard_map.150 = (bf16[32,16,128]{2,1,0:T(8,128)(2,1)S(1)}, bf16[96,128]{1,0:T(8,128)(2,1)S(1)}, f32[96,128]{1,0:T(8,128)S(1)}, f32[2,128]{1,0:T(2,128)S(1)}, bf...) custom-call(s32[1]{0:T(128)S(6)} %copy.30.refs_0_, ...), custom_call_target="tpu_custom_call", output_to_operand_aliasing={{4}: (11, {}), {5}: (12, {})} | custom-call | tf_op jit(solution)/shard_map/pallas_call | solution.py:538
  49.5 0.0 copy-start.1
  49.5 10.1 %all_to_all.39.refs_1_ = bf16[32,16,128]{2,1,0:T(8,128)(2,1)S(1)} all-to-all(bf16[32,16,128]{2,1,0:T(8,128)(2,1)S(1)} %get-tuple-element.74), channel_id=1, replica_groups=mesh['gx'=8,'gy'=4] {'gx','gy'}, dimensions={0} | all-to-all | bytes 262144 | tf_op jit(solution)/shard_map/all_to_all | solution.py:550
  59.5 0.6 shard_map.151
  60.2 0.3 collective-permute-start
  60.5 1.4 %shard_map.152 = (f32[96,128]{1,0:T(8,128)S(1)}, bf16[128,128]{1,0:T(8,128)(2,1)S(1)}, f32[2048,128]{1,0:T(8,128)S(1)}) custom-call(bf16[96,128]{1,0:T(8,128)(2,1)S(1)} %get-tuple-element.81.refs_0_, bf16[2592,96]{1,0:T(8,128)(2,1)S(1)} %bitcast.10, bf16[256,3456]{1,0:T(8,128)(2,1)S(1)} %get-tuple-element.53.refs_3_.refs_6_.refs_2_, ...), custom_call_target="tpu_custom_call" | custom-call | tf_op jit(solution)/shard_map/pallas_call | solution.py:538
  61.8 0.3 collective-permute-done.refs_2_
  62.2 0.1 shard_map.153
  62.3 19.6 %all_to_all.40.refs_0_ = bf16[32,80,128]{2,1,0:T(8,128)(2,1)S(1)} all-to-all(bf16[32,80,128]{2,1,0:T(8,128)(2,1)S(1)} %shard_map.153), channel_id=1, replica_groups=mesh['gx'=8,'gy'=4] {'gx','gy'}, dimensions={0} | all-to-all | bytes 1310720 | tf_op jit(solution)/shard_map/all_to_all | solution.py:550
  81.9 0.1 shard_map.154
  82.0 18.8 %all_to_all.41 = bf16[32,64,128]{2,1,0:T(8,128)(2,1)S(1)} all-to-all(bf16[32,64,128]{2,1,0:T(8,128)(2,1)S(1)} %get-tuple-element.85), channel_id=1, replica_groups=mesh['gx'=8,'gy'=4] {'gx','gy'}, dimensions={0} | all-to-all | bytes 1048576 | tf_op jit(solution)/shard_map/all_to_all | solution.py:550
  100.9 1.4 %shard_map.155 = (f32[27,96,96]{2,1,0:T(8,128)}, f32[27,96,96]{2,1,0:T(8,128)}, bf16[96,128]{1,0:T(8,128)(2,1)}, f32[4,96]{1,0:T(4,128)}, bf16[96,128]{1,0:T(8,128)(2,1)}) custom-call(s32[1]{0:T(128)S(6)} %copy.30.refs_0_, bf16[2048,128]{1,0:T(8,128)(2,1)S(1)} %bitcast.12, bf16[96,128]{1,0:T(8,128)(2,1)S(1)} %get-tuple-element.86.refs_2_, ...), custom_call_target="tpu_custom_call" | custom-call | tf_op jit(solution)/shard_map/pallas_call | solution.py:538
  102.3 0.5 collective-permute-done.1.refs_0_
  102.8 1.2 %shard_map.156 = (f32[27,96,96]{2,1,0:T(8,128)}, f32[27,96,96]{2,1,0:T(8,128)}) custom-call(bf16[2048,128]{1,0:T(8,128)(2,1)S(1)} %collective-permute-done.1.refs_0_, f32[27,96,96]{2,1,0:T(8,128)} %get-tuple-element.92.refs_1_, f32[27,96,96]{2,1,0:T(8,128)} %get-tuple-element.93.refs_2_), custom_call_target="tpu_custom_call", output_to_operand_aliasing={{0}: (1, {}), {1}: (2, {})} | custom-call | tf_op jit(solution)/shard_map/pallas_call | solution.py:538
  (12 shorter events, 0.0 us)
Async XLA Ops:
  17.8 10.9 %copy-start = (bf16[27,96,96]{2,1,0:T(8,128)(2,1)S(1)}, bf16[27,96,96]{2,1,0:T(8,128)(2,1)}, u32[]{:S(2)}) copy-start(bf16[27,96,96]{2,1,0:T(8,128)(2,1)} %param.16) | copy-start | bytes 1492996
  17.8 10.9 %copy-start.5 = (f32[96]{0:T(128)S(1)}, f32[96]{0:T(128)}, u32[]{:S(2)}) copy-start(f32[96]{0:T(128)} %param.17) | copy-start | bytes 1156
  17.8 10.9 %copy-start.6 = (f32[96]{0:T(128)S(1)}, f32[96]{0:T(128)}, u32[]{:S(2)}) copy-start(f32[96]{0:T(128)} %param.18) | copy-start | bytes 1156
  28.8 10.2 %copy-start.2 = (bf16[96,128]{1,0:T(8,128)(2,1)S(1)}, bf16[96,128]{1,0:T(8,128)(2,1)}, u32[]{:S(2)}) copy-start(bf16[96,128]{1,0:T(8,128)(2,1)} %refs_4_.1) | copy-start | bytes 73732
  28.8 10.2 %copy-start.3 = (f32[96]{0:T(128)S(1)}, f32[96]{0:T(128)}, u32[]{:S(2)}) copy-start(f32[96]{0:T(128)} %param.19) | copy-start | bytes 1156
  28.8 10.2 %copy-start.4 = (f32[96]{0:T(128)S(1)}, f32[96]{0:T(128)}, u32[]{:S(2)}) copy-start(f32[96]{0:T(128)} %param.20) | copy-start | bytes 1156
  49.5 11.0 %copy-start.1 = (bf16[27,96,96]{2,1,0:T(8,128)(2,1)S(1)}, bf16[27,96,96]{2,1,0:T(8,128)(2,1)}, u32[]{:S(2)}) copy-start(bf16[27,96,96]{2,1,0:T(8,128)(2,1)} %param.15) | copy-start | bytes 1492996
  60.2 2.0 %collective-permute-start = (bf16[2048,128]{1,0:T(8,128)(2,1)S(1)}, bf16[2048,128]{1,0:T(8,128)(2,1)S(1)}, u32[]{:S(2)}, u32[]{:S(2)}) collective-permute-start(bf16[2048,128]{1,0:T(8,128)(2,1)S(1)} %get-tuple-element.84), channel_id=1, source_target_pairs={{0,1},{1,0},{2,3},{3,2},{4,5},{5,4},{6,7},{7,6},{8,9},{9,8},{10,11... | collective-permute-start | bytes 1572872 | tf_op jit(solution)/shard_map/ppermute | solution.py:555
  100.9 1.9 %collective-permute-start.1 = (bf16[2048,128]{1,0:T(8,128)(2,1)S(1)}, bf16[2048,128]{1,0:T(8,128)(2,1)S(1)}, u32[]{:S(2)}, u32[]{:S(2)}) collective-permute-start(bf16[2048,128]{1,0:T(8,128)(2,1)S(1)} %bitcast.11), channel_id=1, source_target_pairs={{0,1},{1,0},{2,3},{3,2},{4,5},{5,4},{6,7},{7,6},{8,9},{9,8},{10,11... | collective-permute-start | bytes 1572872 | tf_op jit(solution)/shard_map/ppermute | solution.py:555

commit v11 on v8

--- a/solution.py
+++ b/solution.py
@@ -296,8 +296,8 @@
     terms = nn(weight_ref[...], grad).astype(BF16)
     offsets = hot_ref.shape[1] // LANES
     wide = jnp.concatenate([terms[k * channels : (k + 1) * channels] for k in range(offsets)], axis=1)
-    table = pad_to(nt(hot_ref[...], wide), hot_ref.shape[0], LANES)
-    return table[:LANES], table[LANES : 2 * LANES]
+    halo = pad_to(nt(hot_ref[LANES : 2 * LANES, :], wide), LANES, LANES)
+    return pad_to(nt(hot_ref[:LANES, :], wide), LANES, LANES), halo
 
 
 def row_gradient(grad, normal, const, dgain, dbias, valid):

time: 104 us -> 104 us (level)
  no operation moved by 1% of the time
where the time goes in v11:
time: 104 us
  blocking collectives  91.8 us (88%)
  Pallas kernels  9.67 us (9%)
  between operations  1.39 us (1%)
    all_to_all x7, blocking collectives, to_all(): return lax.all_to_all(x, AXES, 0, 0)  91.8 us
    pallas_call x11, Pallas kernels, call(): pl.pallas_call(body, out_shape=tuple((jax.ShapeDtypeStruct(shape, dtype)...  9.67 us
  transfers between devices with their start and end apart: 2, of which 2 were waited for; matrix products, arithmetic and copies ran while one was open for 0% of the time, Pallas kernels for 3%

profile of v11, /device:TPU:0, one launch (start us, length us, event | category | flops | bytes accessed | tf_op | source)
XLA Modules:
  0.0 104.0 jit_solution(9956928788784981388)
XLA Ops:
  1.3 1.2 %shard_map.146 = (bf16[32,16,128]{2,1,0:T(8,128)(2,1)S(1)}, bf16[96,128]{1,0:T(8,128)(2,1)S(1)}, bf16[128,128]{1,0:T(8,128)(2,1)S(1)}, bf16[256,3456]{1,0:T(8,128)(2,1)S(1)}, bf16[2592,96]{1,0:T(8,128)(2,1)S(1)}) custom-call(s32[1]{0:T(128)S(6)} %copy.30.refs_0_, bf16[96,128]{1,0:T(8,128)(2,1)} %refs_1_.1, s32[8,16]{1,0:T(8,128)} %refs_2_.1, ...), custom_call_target="tpu_custom_call" | custom-call | tf_op jit(solution)/shard_map/pallas_call | solution.py:524
  2.5 15.3 %all_to_all.35.refs_1_ = bf16[32,16,128]{2,1,0:T(8,128)(2,1)S(1)} all-to-all(bf16[32,16,128]{2,1,0:T(8,128)(2,1)S(1)} %get-tuple-element.51), channel_id=1, replica_groups=mesh['gx'=8,'gy'=4] {'gx','gy'}, dimensions={0} | all-to-all | bytes 262144 | tf_op jit(solution)/shard_map/all_to_all | solution.py:536
  17.8 0.9 shard_map.147
  18.8 10.0 %all_to_all.36.refs_1_ = bf16[32,16,128]{2,1,0:T(8,128)(2,1)S(1)} all-to-all(bf16[32,16,128]{2,1,0:T(8,128)(2,1)S(1)} %get-tuple-element.56), channel_id=1, replica_groups=mesh['gx'=8,'gy'=4] {'gx','gy'}, dimensions={0} | all-to-all | bytes 262144 | tf_op jit(solution)/shard_map/all_to_all | solution.py:536
  28.8 0.0 copy-start.2
  28.8 0.0 copy-start.4
  28.8 1.1 %shard_map.148 = (f32[32,2,128]{2,1,0:T(2,128)S(1)}, f32[96,128]{1,0:T(8,128)S(1)}, bf16[2592,128]{1,0:T(8,128)(2,1)S(1)}, f32[96,128]{1,0:T(8,128)S(1)}, f32[96...) custom-call(s32[1]{0:T(128)S(6)} %copy.30.refs_0_, ...), custom_call_target="tpu_custom_call", output_to_operand_aliasing={{8}: (8, {})} | custom-call | tf_op jit(solution)/shard_map/pallas_call | solution.py:524
  29.9 9.0 %all_to_all.37.refs_1_ = f32[32,2,128]{2,1,0:T(2,128)S(1)} all-to-all(f32[32,2,128]{2,1,0:T(2,128)S(1)} %get-tuple-element.60), channel_id=1, replica_groups=mesh['gx'=8,'gy'=4] {'gx','gy'}, dimensions={0} | all-to-all | bytes 65536 | tf_op jit(solution)/shard_map/all_to_all | solution.py:536
  39.0 0.4 shard_map.149
  39.4 8.9 %all_to_all.38.refs_1_ = f32[32,2,128]{2,1,0:T(2,128)S(1)} all-to-all(f32[32,2,128]{2,1,0:T(2,128)S(1)} %get-tuple-element.64), channel_id=1, replica_groups=mesh['gx'=8,'gy'=4] {'gx','gy'}, dimensions={0} | all-to-all | bytes 65536 | tf_op jit(solution)/shard_map/all_to_all | solution.py:536
  48.3 1.2 %shard_map.150 = (bf16[32,16,128]{2,1,0:T(8,128)(2,1)S(1)}, bf16[96,128]{1,0:T(8,128)(2,1)S(1)}, f32[96,128]{1,0:T(8,128)S(1)}, f32[2,128]{1,0:T(2,128)S(1)}, bf...) custom-call(s32[1]{0:T(128)S(6)} %copy.30.refs_0_, ...), custom_call_target="tpu_custom_call", output_to_operand_aliasing={{4}: (11, {}), {5}: (12, {})} | custom-call | tf_op jit(solution)/shard_map/pallas_call | solution.py:524
  49.5 0.0 copy-start.1
  49.5 10.1 %all_to_all.39.refs_1_ = bf16[32,16,128]{2,1,0:T(8,128)(2,1)S(1)} all-to-all(bf16[32,16,128]{2,1,0:T(8,128)(2,1)S(1)} %get-tuple-element.74), channel_id=1, replica_groups=mesh['gx'=8,'gy'=4] {'gx','gy'}, dimensions={0} | all-to-all | bytes 262144 | tf_op jit(solution)/shard_map/all_to_all | solution.py:536
  59.6 0.7 shard_map.151
  60.2 0.3 collective-permute-start
  60.5 1.4 %shard_map.152 = (f32[96,128]{1,0:T(8,128)S(1)}, bf16[128,128]{1,0:T(8,128)(2,1)S(1)}, f32[2048,128]{1,0:T(8,128)S(1)}) custom-call(bf16[96,128]{1,0:T(8,128)(2,1)S(1)} %get-tuple-element.81.refs_0_, bf16[2592,96]{1,0:T(8,128)(2,1)S(1)} %bitcast.10, bf16[256,3456]{1,0:T(8,128)(2,1)S(1)} %get-tuple-element.53.refs_3_.refs_6_.refs_2_, ...), custom_call_target="tpu_custom_call" | custom-call | tf_op jit(solution)/shard_map/pallas_call | solution.py:524
  61.9 0.3 collective-permute-done.refs_2_
  62.2 0.1 shard_map.153
  62.3 19.6 %all_to_all.40.refs_0_ = bf16[32,80,128]{2,1,0:T(8,128)(2,1)S(1)} all-to-all(bf16[32,80,128]{2,1,0:T(8,128)(2,1)S(1)} %shard_map.153), channel_id=1, replica_groups=mesh['gx'=8,'gy'=4] {'gx','gy'}, dimensions={0} | all-to-all | bytes 1310720 | tf_op jit(solution)/shard_map/all_to_all | solution.py:536
  82.0 0.1 shard_map.154
  82.1 18.8 %all_to_all.41 = bf16[32,64,128]{2,1,0:T(8,128)(2,1)S(1)} all-to-all(bf16[32,64,128]{2,1,0:T(8,128)(2,1)S(1)} %get-tuple-element.85), channel_id=1, replica_groups=mesh['gx'=8,'gy'=4] {'gx','gy'}, dimensions={0} | all-to-all | bytes 1048576 | tf_op jit(solution)/shard_map/all_to_all | solution.py:536
  100.9 1.4 %shard_map.155 = (f32[27,96,96]{2,1,0:T(8,128)}, f32[27,96,96]{2,1,0:T(8,128)}, bf16[96,128]{1,0:T(8,128)(2,1)}, f32[4,96]{1,0:T(4,128)}, bf16[96,128]{1,0:T(8,128)(2,1)}) custom-call(s32[1]{0:T(128)S(6)} %copy.30.refs_0_, bf16[2048,128]{1,0:T(8,128)(2,1)S(1)} %bitcast.12, bf16[96,128]{1,0:T(8,128)(2,1)S(1)} %get-tuple-element.86.refs_2_, ...), custom_call_target="tpu_custom_call" | custom-call | tf_op jit(solution)/shard_map/pallas_call | solution.py:524
  102.3 0.5 collective-permute-done.1.refs_0_
  102.8 1.2 %shard_map.156 = (f32[27,96,96]{2,1,0:T(8,128)}, f32[27,96,96]{2,1,0:T(8,128)}) custom-call(bf16[2048,128]{1,0:T(8,128)(2,1)S(1)} %collective-permute-done.1.refs_0_, f32[27,96,96]{2,1,0:T(8,128)} %get-tuple-element.92.refs_1_, f32[27,96,96]{2,1,0:T(8,128)} %get-tuple-element.93.refs_2_), custom_call_target="tpu_custom_call", output_to_operand_aliasing={{0}: (1, {}), {1}: (2, {})} | custom-call | tf_op jit(solution)/shard_map/pallas_call | solution.py:524
  (12 shorter events, 0.0 us)
Async XLA Ops:
  17.8 10.9 %copy-start = (bf16[27,96,96]{2,1,0:T(8,128)(2,1)S(1)}, bf16[27,96,96]{2,1,0:T(8,128)(2,1)}, u32[]{:S(2)}) copy-start(bf16[27,96,96]{2,1,0:T(8,128)(2,1)} %param.16) | copy-start | bytes 1492996
  17.8 10.9 %copy-start.5 = (f32[96]{0:T(128)S(1)}, f32[96]{0:T(128)}, u32[]{:S(2)}) copy-start(f32[96]{0:T(128)} %param.17) | copy-start | bytes 1156
  17.8 10.9 %copy-start.6 = (f32[96]{0:T(128)S(1)}, f32[96]{0:T(128)}, u32[]{:S(2)}) copy-start(f32[96]{0:T(128)} %param.18) | copy-start | bytes 1156
  28.8 10.2 %copy-start.2 = (bf16[96,128]{1,0:T(8,128)(2,1)S(1)}, bf16[96,128]{1,0:T(8,128)(2,1)}, u32[]{:S(2)}) copy-start(bf16[96,128]{1,0:T(8,128)(2,1)} %refs_4_.1) | copy-start | bytes 73732
  28.8 10.2 %copy-start.3 = (f32[96]{0:T(128)S(1)}, f32[96]{0:T(128)}, u32[]{:S(2)}) copy-start(f32[96]{0:T(128)} %param.19) | copy-start | bytes 1156
  28.8 10.2 %copy-start.4 = (f32[96]{0:T(128)S(1)}, f32[96]{0:T(128)}, u32[]{:S(2)}) copy-start(f32[96]{0:T(128)} %param.20) | copy-start | bytes 1156
  49.5 11.0 %copy-start.1 = (bf16[27,96,96]{2,1,0:T(8,128)(2,1)S(1)}, bf16[27,96,96]{2,1,0:T(8,128)(2,1)}, u32[]{:S(2)}) copy-start(bf16[27,96,96]{2,1,0:T(8,128)(2,1)} %param.15) | copy-start | bytes 1492996
  60.2 2.0 %collective-permute-start = (bf16[2048,128]{1,0:T(8,128)(2,1)S(1)}, bf16[2048,128]{1,0:T(8,128)(2,1)S(1)}, u32[]{:S(2)}, u32[]{:S(2)}) collective-permute-start(bf16[2048,128]{1,0:T(8,128)(2,1)S(1)} %get-tuple-element.84), channel_id=1, source_target_pairs={{0,1},{1,0},{2,3},{3,2},{4,5},{5,4},{6,7},{7,6},{8,9},{9,8},{10,11... | collective-permute-start | bytes 1572872 | tf_op jit(solution)/shard_map/ppermute | solution.py:541
  100.9 1.9 %collective-permute-start.1 = (bf16[2048,128]{1,0:T(8,128)(2,1)S(1)}, bf16[2048,128]{1,0:T(8,128)(2,1)S(1)}, u32[]{:S(2)}, u32[]{:S(2)}) collective-permute-start(bf16[2048,128]{1,0:T(8,128)(2,1)S(1)} %bitcast.11), channel_id=1, source_target_pairs={{0,1},{1,0},{2,3},{3,2},{4,5},{5,4},{6,7},{7,6},{8,9},{9,8},{10,11... | collective-permute-start | bytes 1572872 | tf_op jit(solution)/shard_map/ppermute | solution.py:541
